TPU v7x, 256 devices: a whole 4x4x8 slice. The times are simulated.
256 devices in a mesh: nodes: 128 (over y, z, x), rep: 2 (over core).
Axes of the slice: x: 4, y: 4, z: 8, core: 2. Of those that a mesh axis runs over, the one named last changes fastest.
Arguments:
- features: bfloat16 [131072, 128], P('nodes'), may hold values from -6 to 6
- weight: bfloat16 [128, 256], replicated, may hold values from -0.5 to 0.5
- out_bias: float32 [256], replicated, may hold values from -3 to 3
- edge_tiles: bfloat16 [16384, 128, 128], P(('nodes', 'rep')), may hold values from -0.125 to 0.125
- block_row: int32 [16384], P(('nodes', 'rep')), may hold values from 0 to 1023, as said below
- tile_slot: int32 [16384], P(('nodes', 'rep')), may hold values from 0 to 255, as said below
- send_list: int32 [32768, 2], P(('nodes', 'rep')), may hold values from 0 to 7, as said below
- out_grad: bfloat16 [131072, 256], P('nodes'), may hold values from -6 to 6
Outputs:
- activations: bfloat16 [131072, 256], P('nodes', 'rep')
- feature_grad: float32 [131072, 128], P(('nodes', 'rep'))
- weight_grad: float32 [128, 256], P(None, 'rep')
- bias_grad: float32 [256], P('rep')
Inputs may be any that keep to these rules, and one draw needn't show every extreme that they name: `block_row`: an adjacency block of the device at nodes index r lies in block rows r * 8 to r * 8 + 7. `tile_slot`: slot s * 2 + c names the c-th block that nodes index s sends to this device's nodes index, as send_list states. `send_list`: row (s * 2 + q) * 128 + r lists the local block numbers that nodes index s sends to nodes index r, both at rep index q; the 2 numbers of a row differ.
All inputs are finite; a program needn't handle non-finite values.
Results may differ from a plain program's by a relative error of at most 0.012.
Values may be sent and summed in bfloat16 or wider, within the bound.
No kernel may reach another device: no remote copies, remote signals or barrier semaphores. Data moves between devices by JAX's collectives and lax.ppermute only.
A program may use at most 128 MiB of HBM per device.

v0:
```python
import functools
import math

import jax
import jax.numpy as jnp
from jax import lax
from jax.experimental import pallas as pl
from jax.experimental.pallas import tpu as pltpu
from jax.sharding import PartitionSpec as P

ROOT_TWO_PI = 0.7978845608028654
CUBIC_TERM = 0.044715

NY, NZ, NX = 4, 8, 4
BLK = 128
HALF = 64
NB = 8
CAP = 56
ROWS = NB * HALF
MSG = ROWS + 16
PART = NZ * MSG
LOCAL = NY * PART
FAR = CAP * HALF
TILES = 128
LOC0, REM0, CNT0, OVER, ROW0 = 128, 256, 440, 444, 512
INFO = 640
SUMS = BLK + 16
SEND = 64 * HALF


def gelu_value(values):
    inner_term = ROOT_TWO_PI * (values + CUBIC_TERM * values * values * values)
    return 0.5 * values * (1.0 + jnp.tanh(inner_term))


def gelu_slope(values):
    tangent = jnp.tanh(ROOT_TWO_PI * (values + CUBIC_TERM * values * values * values))
    outer_part = 0.5 * values * (1.0 - tangent * tangent) * ROOT_TWO_PI
    return 0.5 * (1.0 + tangent) + outer_part * (1.0 + 3.0 * CUBIC_TERM * values * values)


def general_shards(features, weight, out_bias, edge_tiles, block_row, tile_slot, send_list, out_grad):
    node_count = lax.axis_size("nodes")
    rep_count = lax.axis_size("rep")
    rep_position = lax.axis_index("rep")
    block_size = edge_tiles.shape[1]
    local_blocks = features.shape[0] // block_size
    width_in = features.shape[1]
    capacity = send_list.shape[1]
    half_out = weight.shape[1] // rep_count
    feature_blocks = features.reshape(local_blocks, block_size, width_in)
    outgoing = feature_blocks[send_list]
    incoming = lax.all_to_all(outgoing, "nodes", split_axis=0, concat_axis=0, tiled=True)
    incoming = incoming.reshape(node_count * capacity, block_size, width_in)
    picked = incoming[tile_slot]
    products = jnp.einsum("tij,tjf->tif", edge_tiles, picked, preferred_element_type=jnp.float32)
    local_rows = block_row - lax.axis_index("nodes") * local_blocks
    partial_value = jax.ops.segment_sum(products, local_rows, num_segments=local_blocks)
    partial_value = partial_value.reshape(local_blocks * block_size, width_in)
    aggregate_bf = lax.psum(partial_value, "rep").astype(jnp.bfloat16)
    preact = jnp.dot(aggregate_bf, weight, preferred_element_type=jnp.float32) + out_bias
    own_preact = lax.dynamic_slice_in_dim(preact, rep_position * half_out, half_out, 1)
    activations = gelu_value(own_preact).astype(jnp.bfloat16)
    pre_grad = (out_grad.astype(jnp.float32) * gelu_slope(preact)).astype(jnp.bfloat16)
    agg_grad = lax.dot_general(
        pre_grad, weight, (((1,), (1,)), ((), ())), preferred_element_type=jnp.float32
    ).astype(jnp.bfloat16)
    grad_rows = agg_grad.reshape(local_blocks, block_size, width_in)[local_rows]
    back_products = jnp.einsum(
        "tji,tjf->tif", edge_tiles, grad_rows, preferred_element_type=jnp.float32
    )
    slot_sums = jax.ops.segment_sum(back_products, tile_slot, num_segments=node_count * capacity)
    slot_sums = slot_sums.astype(jnp.bfloat16)
    returned = lax.all_to_all(
        slot_sums.reshape(node_count, capacity, block_size, width_in),
        "nodes",
        split_axis=0,
        concat_axis=0,
        tiled=True,
    )
    returned = returned.astype(jnp.float32)
    owner_sums = jax.ops.segment_sum(
        returned.reshape(node_count * capacity, block_size, width_in),
        send_list.reshape(-1),
        num_segments=local_blocks,
    )
    feature_grad = lax.psum_scatter(
        owner_sums.reshape(local_blocks * block_size, width_in).astype(jnp.bfloat16),
        "rep",
        scatter_dimension=0,
        tiled=True,
    ).astype(jnp.float32)
    own_grad = lax.dynamic_slice_in_dim(pre_grad, rep_position * half_out, half_out, 1)
    norm_scale = 1.0 / math.sqrt(features.shape[0] * node_count)
    weight_part = (
        lax.dot_general(
            aggregate_bf, own_grad, (((0,), (0,)), ((), ())), preferred_element_type=jnp.float32
        )
        * norm_scale
    )
    bias_part = jnp.sum(own_grad.astype(jnp.float32), axis=0) * norm_scale
    weight_grad, bias_grad = lax.psum((weight_part, bias_part), "nodes")
    return (activations, feature_grad, weight_grad, bias_grad)


def device_of(y, z, x, c):
    return ((y % NY * NZ + z % NZ) * NX + x % NX) * 2 + c


def moved(value, target):
    pairs = [
        (device_of(y, z, x, c), device_of(*target(y, z, x, c)))
        for y in range(NY)
        for z in range(NZ)
        for x in range(NX)
        for c in range(2)
    ]
    return lax.ppermute(value, ("nodes", "rep"), pairs)


def along_z(value, step):
    return moved(value, lambda y, z, x, c: (y, z + step if c == 0 else z - step, x, c))


def along_dense(value, step):
    return moved(value, lambda y, z, x, c: (y + step, z, x, c) if c == 0 else (y, z, x + step, c))


def along_sparse(value, step):
    return moved(value, lambda y, z, x, c: (y, z, x + step, c) if c == 0 else (y + step, z, x, c))


def to_other_core(value):
    return moved(value, lambda y, z, x, c: (y, z, x, 1 - c))


SMEM = pl.BlockSpec(memory_space=pltpu.SMEM)
VMEM = pl.BlockSpec(memory_space=pltpu.VMEM)
ANY = pl.BlockSpec(memory_space=pl.ANY)


def call(kernel, out_shape, in_specs, out_specs, scratch=(), flops=0, moved_bytes=0, vmem=12):
    return pl.pallas_call(
        kernel,
        out_shape=out_shape,
        in_specs=in_specs,
        out_specs=out_specs,
        scratch_shapes=list(scratch),
        compiler_params=pltpu.CompilerParams(vmem_limit_bytes=vmem << 20),
        cost_estimate=pl.CostEstimate(flops=flops, bytes_accessed=moved_bytes, transcendentals=0),
    )


def struct(shape, dtype):
    return jax.ShapeDtypeStruct(shape, dtype)


def message_kernel(core_ref, features_ref, own_ref, other_ref, out_ref, half_ref):
    core = core_ref[0]
    for block in range(NB):
        turned = features_ref[block * BLK : (block + 1) * BLK, :].astype(jnp.float32).T
        mine = jnp.where(core == 0, turned[:HALF], turned[HALF:]).astype(jnp.bfloat16)
        rest = jnp.where(core == 0, turned[HALF:], turned[:HALF]).astype(jnp.bfloat16)
        out_ref[block * HALF : (block + 1) * HALF, :] = mine
        half_ref[block * HALF : (block + 1) * HALF, :] = mine
        out_ref[MSG + block * HALF : MSG + (block + 1) * HALF, :] = rest
    own, other = own_ref[1:3, :], other_ref[1:3, :]
    lists = jnp.concatenate(
        [
            jnp.where(core == 0, own, other),
            jnp.where(core == 0, other, own),
            jnp.zeros((12, BLK), jnp.int32),
        ],
        axis=0,
    )
    lists = lists.astype(jnp.float32).astype(jnp.bfloat16)
    out_ref[ROWS:MSG, :] = lists
    half_ref[ROWS:MSG, :] = lists


def plan_kernel(code_ref, rows_ref, info_ref, first_ref, second_ref, third_ref, count_ref):
    requests = (first_ref, second_ref, third_ref)
    for k in range(8):
        count_ref[k] = 0

    def clear(i, carry):
        for ref in requests:
            ref[i] = 0
        info_ref[i] = 0
        info_ref[LOC0 + i] = 0
        info_ref[REM0 + i] = 0
        info_ref[REM0 + 128 + i] = 0
        info_ref[ROW0 + i] = rows_ref[i]
        return carry

    lax.fori_loop(0, 128, clear, 0)

    def place(t, carry):
        code = code_ref[t]
        other_key = code // 512
        key = code // 128 % 4
        slot = code % 128
        count_ref[4 + other_key] = count_ref[4 + other_key] + 1
        rank = count_ref[key]
        count_ref[key] = rank + 1

        @pl.when(key == 0)
        def _():
            info_ref[rank] = slot
            info_ref[LOC0 + rank] = t

        @pl.when(jnp.logical_and(key > 0, rank < CAP))
        def _():
            info_ref[REM0 + (key - 1) * CAP + rank] = t
            for k in (1, 2, 3):

                @pl.when(key == k)
                def _():
                    requests[k - 1][rank] = slot

        return carry

    lax.fori_loop(0, TILES, place, 0)
    over = 0
    info_ref[CNT0] = count_ref[0]
    for k in (1, 2, 3):
        kept = jnp.minimum(count_ref[k], CAP)
        info_ref[CNT0 + k] = kept
        requests[k - 1][64] = kept
        over += count_ref[k] - kept
        over += jnp.maximum(count_ref[4 + k] - CAP, 0)
    info_ref[OVER] = over


def start_all(pairs, sem):
    copies = [pltpu.make_async_copy(src, dst, sem.at[n]) for n, (src, dst) in enumerate(pairs)]
    for copy in copies:
        copy.start()
    return copies


def wait_all(copies):
    for copy in copies:
        copy.wait()


def half_rows(index):
    return pl.ds(pl.multiple_of(index * HALF, HALF), HALF)


def local_block(parts, slot, table, k):
    at = pl.ds(pl.multiple_of(slot // 4 % NZ * MSG + table[slot * 4 + k] * HALF, 16), HALF)
    part = slot // (4 * NZ)
    low = jnp.where(part == 0, parts[0][at, :], parts[1][at, :])
    high = jnp.where(part == 2, parts[2][at, :], parts[3][at, :])
    return jnp.where(part < 2, low, high)


def pick_kernel(
    a_ref, b_ref, c_ref, d_ref, first_ref, second_ref, third_ref, table_ref, o1, o2, o3,
    q1, q2, q3, table, sem,
):
    parts = (a_ref, b_ref, c_ref, d_ref)
    wait_all(
        start_all([(first_ref, q1), (second_ref, q2), (third_ref, q3), (table_ref, table)], sem)
    )
    for k, (req, out) in enumerate(((q1, o1), (q2, o2), (q3, o3))):

        def body(i, carry, req=req, out=out, k=k):
            for u in range(8):
                p = i * 8 + u
                out[half_rows(p), :] = local_block(parts, req[p], table, k + 1)
            return carry

        lax.fori_loop(0, CAP // 8, body, 0)


def near_kernel(
    a_ref, b_ref, c_ref, d_ref, tiles, info_ref, table_ref, out_ref, acc, info, table, sem
):
    parts = (a_ref, b_ref, c_ref, d_ref)
    copies = start_all([(info_ref, info), (table_ref, table)], sem)
    acc[...] = jnp.zeros_like(acc)
    wait_all(copies)
    count = info[CNT0]

    def body(i, carry):
        done = []
        for u in range(8):
            p = i * 8 + u
            block = local_block(parts, info[p], table, 0)
            done.append(
                lax.dot_general(
                    block, tiles[info[LOC0 + p]], (((1,), (1,)), ((), ())),
                    preferred_element_type=jnp.float32,
                )
            )
        for u in range(8):
            p = i * 8 + u
            row = jnp.where(p < count, info[ROW0 + info[LOC0 + p]], NB)
            acc[half_rows(row), :] += done[u]
        return carry

    lax.fori_loop(0, (count + 7) // 8, body, 0)
    out_ref[...] = acc[:ROWS, :]


def far_kernel(near_ref, r1, r2, r3, tiles, info_ref, out_ref, acc, info, sem):
    copies = start_all([(info_ref, info)], sem)
    acc[:ROWS, :] = near_ref[...]
    acc[ROWS:, :] = jnp.zeros((HALF, BLK), jnp.float32)
    wait_all(copies)
    for k, got in enumerate((r1, r2, r3)):
        count = info[CNT0 + 1 + k]

        def body(i, carry, k=k, got=got, count=count):
            done = []
            for u in range(8):
                p = i * 8 + u
                done.append(
                    lax.dot_general(
                        got[half_rows(p), :], tiles[info[REM0 + k * CAP + p]],
                        (((1,), (1,)), ((), ())), preferred_element_type=jnp.float32,
                    )
                )
            for u in range(8):
                p = i * 8 + u
                row = jnp.where(p < count, info[ROW0 + info[REM0 + k * CAP + p]], NB)
                acc[half_rows(row), :] += done[u]
            return carry

        lax.fori_loop(0, (count + 7) // 8, body, 0)
    out_ref[...] = acc[:ROWS, :].astype(jnp.bfloat16)


def products(step, tiles, turned_ref, info, out):
    first = REM0 + (step - 1) * CAP

    def body(i, carry):
        for u in range(8):
            p = i * 8 + u
            t = info[first + p]
            left = turned_ref[half_rows(info[ROW0 + t]), :]
            out[half_rows(p), :] = jnp.dot(
                left, tiles[t], preferred_element_type=jnp.float32
            ).astype(jnp.bfloat16)
        return carry

    lax.fori_loop(0, (info[CNT0 + step] + 7) // 8, body, 0)


def middle_kernel(
    core_ref, own_agg, other_agg, weight_ref, bias_ref, grad_ref, tiles, info_ref,
    act_ref, sums_ref, turned_ref, out, info, sem,
):
    copies = start_all([(info_ref, info)], sem)
    core = core_ref[0]
    sums_ref[...] = jnp.zeros_like(sums_ref)
    weight_half = weight_ref[half_rows(core), :]

    def block_step(b, carry):
        own, other = own_agg[half_rows(b), :], other_agg[half_rows(b), :]
        low = jnp.where(core == 0, own, other)
        high = jnp.where(core == 0, other, own)
        agg = jnp.concatenate([low, high], axis=0)
        preact = lax.dot_general(
            agg, weight_ref[...], (((0,), (0,)), ((), ())), preferred_element_type=jnp.float32
        )
        preact = preact + bias_ref[...]
        tangent = jnp.tanh(ROOT_TWO_PI * (preact + CUBIC_TERM * preact * preact * preact))
        nodes = pl.ds(pl.multiple_of(b * BLK, BLK), BLK)
        value = 0.5 * preact * (1.0 + tangent)
        act_ref[nodes, :] = jnp.where(core == 0, value[:, :BLK], value[:, BLK:]).astype(jnp.bfloat16)
        outer = 0.5 * preact * (1.0 - tangent * tangent) * ROOT_TWO_PI
        slope = 0.5 * (1.0 + tangent) + outer * (1.0 + 3.0 * CUBIC_TERM * preact * preact)
        pre = (grad_ref[nodes, :].astype(jnp.float32) * slope).astype(jnp.bfloat16)
        turned_ref[half_rows(b), :] = lax.dot_general(
            weight_half, pre, (((1,), (1,)), ((), ())), preferred_element_type=jnp.float32
        ).astype(jnp.bfloat16)
        mine = jnp.where(core == 0, pre[:, :BLK], pre[:, BLK:])
        sums_ref[:BLK, :] += lax.dot_general(
            agg, mine, (((1,), (0,)), ((), ())), preferred_element_type=jnp.float32
        )
        sums_ref[BLK : BLK + 1, :] += jnp.sum(mine.astype(jnp.float32), axis=0, keepdims=True)
        return carry

    lax.fori_loop(0, NB, block_step, 0, unroll=2)
    wait_all(copies)
    over = info[OVER].astype(jnp.float32)
    sums_ref[BLK + 1 : BLK + 2, :] = jnp.full((1, BLK), over, jnp.float32)
    products(2, tiles, turned_ref, info, out)


def side_kernel(tiles, turned_ref, info_ref, o1, o3, info, sem):
    wait_all(start_all([(info_ref, info)], sem))
    products(1, tiles, turned_ref, info, o1)
    products(3, tiles, turned_ref, info, o3)


NORM = 1.0 / math.sqrt(NY * NZ * NX * NB * BLK)


def two_parts(value):
    upper = value.astype(jnp.bfloat16)
    return upper, (value - upper.astype(jnp.float32)).astype(jnp.bfloat16)


def owner_kernel(
    info_ref, table_ref, first_ref, second_ref, third_ref, turned_ref, tiles,
    r1, r2, r3, sums_ref, o0, o1, o2, o3, total, info, table, q1, q2, q3, sem,
):
    copies = start_all(
        [(info_ref, info), (table_ref, table), (first_ref, q1), (second_ref, q2), (third_ref, q3)],
        sem,
    )
    total[...] = jnp.zeros_like(total)
    wait_all(copies)

    def total_rows(slot, k, used):
        return half_rows(jnp.where(used, slot // 4 * NB + table[slot * 4 + k], 256))

    count = info[CNT0]

    def near(i, carry):
        done = []
        for u in range(8):
            t = info[LOC0 + i * 8 + u]
            left = turned_ref[half_rows(info[ROW0 + t]), :]
            done.append(jnp.dot(left, tiles[t], preferred_element_type=jnp.float32))
        for u in range(8):
            p = i * 8 + u
            total[total_rows(info[p], 0, p < count), :] += done[u]
        return carry

    lax.fori_loop(0, (count + 7) // 8, near, 0)
    for k, (req, got) in enumerate(((q1, r1), (q2, r2), (q3, r3))):
        kept = req[64]

        def far(i, carry, req=req, got=got, k=k, kept=kept):
            for u in range(8):
                p = i * 8 + u
                at = total_rows(req[p], k + 1, p < kept)
                total[at, :] += got[half_rows(p), :].astype(jnp.float32)
            return carry

        lax.fori_loop(0, (kept + 7) // 8, far, 0)
    upper, lower = two_parts(sums_ref[...])
    for j, out in enumerate((o0, o1, o2, o3)):
        out[:SEND, :] = total[j * SEND : (j + 1) * SEND, :].astype(jnp.bfloat16)
        if j > 0:
            out[SEND : SEND + SUMS, :] = upper
            out[SEND + SUMS :, :] = lower


def split_sum_kernel(
    odd_ref, a_ref, b_ref, c_ref, d_ref, sums_ref, keep_ref, far_ref, mine_ref, swap_ref, passed_ref
):
    def sent(ref):
        upper, lower = ref[SEND : SEND + SUMS, :], ref[SEND + SUMS :, :]
        return upper.astype(jnp.float32) + lower.astype(jnp.float32)

    upper, lower = two_parts(sums_ref[...])
    own = upper.astype(jnp.float32) + lower.astype(jnp.float32)
    one, two, three = sent(b_ref), sent(c_ref), sent(d_ref)
    odd = odd_ref[0] == 1
    passed_ref[...] = (own + jnp.where(odd, three, one)) + (two + jnp.where(odd, one, three))
    for m in range(NZ):
        at = slice(m * ROWS, (m + 1) * ROWS)
        value = a_ref[at, :].astype(jnp.float32) + b_ref[at, :].astype(jnp.float32)
        value = value + (c_ref[at, :].astype(jnp.float32) + d_ref[at, :].astype(jnp.float32))
        value = value.astype(jnp.bfloat16)
        if m == 0:
            keep_ref[...] = value
        elif m < 4:
            mine_ref[(m - 1) * ROWS : m * ROWS, :] = value
        elif m == 4:
            far_ref[...] = value
        else:
            swap_ref[(m - 5) * ROWS : (m - 4) * ROWS, :] = value


def last_sum_kernel(
    core_ref, sums_ref, keep_ref, far_ref, a_ref, b_ref, c_ref, hold_ref, send_ref, passed_ref
):
    passed_ref[...] = sums_ref[...]
    core = core_ref[0]
    half = ROWS // 2

    def total(first):
        at = slice(first, first + half)
        value = a_ref[at, :].astype(jnp.float32) + b_ref[at, :].astype(jnp.float32)
        value = value + c_ref[at, :].astype(jnp.float32)
        if first < ROWS:
            value = value + keep_ref[at, :].astype(jnp.float32) + far_ref[at, :].astype(jnp.float32)
        return value

    for n in range(2):
        low, high = total(n * ROWS), total(n * ROWS + half)
        at = slice(n * half, (n + 1) * half)
        hold_ref[at, :] = jnp.where(core == 0, low, high)
        send_ref[at, :] = jnp.where(core == 0, high, low)


def turn_kernel(core_ref, hold_ref, got_ref, sums_ref, out_ref, weight_ref, bias_ref):
    core = core_ref[0]
    half = ROWS // 2
    for b in range(NB // 2):
        first = slice(b * HALF, (b + 1) * HALF)
        second = slice(half + b * HALF, half + (b + 1) * HALF)
        own = hold_ref[first, :] + got_ref[second, :]
        other = hold_ref[second, :] + got_ref[first, :]
        both = jnp.concatenate(
            [jnp.where(core == 0, own, other), jnp.where(core == 0, other, own)], axis=0
        )
        out_ref[b * BLK : (b + 1) * BLK, :] = both.T
    weight_ref[...] = sums_ref[:BLK, :] * NORM
    bias_ref[...] = sums_ref[BLK : BLK + 1, :] * NORM


def butterfly(value, target, size):
    step = 1
    while step < size:
        value = value + moved(value, functools.partial(target, step))
        step *= 2
    return value


def shards(features, weight, out_bias, edge_tiles, block_row, tile_slot, send_list, out_grad):
    bf16, f32, i32 = jnp.bfloat16, jnp.float32, jnp.int32
    node = lax.axis_index("nodes")
    core = lax.axis_index("rep")
    y, z, x = node // (NZ * NX), node // NX % NZ, node % NX
    core_array = jnp.reshape(core, (1,)).astype(i32)
    dma = pltpu.SemaphoreType.DMA

    local_rows = block_row - node * NB
    packed = jnp.pad(tile_slot * NB + local_rows, (0, BLK - 64))
    own_meta = jnp.concatenate([packed[None, :], send_list.T], axis=0)
    other_meta = to_other_core(own_meta)
    tiles = jnp.concatenate([edge_tiles, to_other_core(edge_tiles)], axis=0)

    message, half_message = call(
        message_kernel,
        [struct((MSG + ROWS, BLK), bf16), struct((MSG, BLK), bf16)],
        [SMEM, VMEM, VMEM, VMEM],
        [VMEM] * 2,
        moved_bytes=500000,
    )(core_array, features, own_meta, other_meta)
    first, second = along_z(message, 1), along_z(message, 2)
    first, second = lax.optimization_barrier((first, second))
    across, third = along_z(second[:MSG], 2), along_z(second, 1)
    swapped = to_other_core(jnp.concatenate([first[ROWS:], second[ROWS:]], axis=0))
    swapped = [swapped[:MSG], swapped[MSG:], to_other_core(third[ROWS:])]
    column = [half_message, first[:MSG], second[:MSG], third[:MSG], across]
    for piece in swapped:
        column += [piece[MSG - ROWS :], piece[: MSG - ROWS]]
    column = jnp.concatenate(column, axis=0)

    both = jnp.concatenate([own_meta[0, :64], other_meta[0, :64]])
    rows = both % NB
    slot = both // NB
    source, which = slot // 2, slot % 2
    step_y = (source // (NZ * NX) - y) % NY
    step_z = (source // NX - z) % NZ
    step_x = (source - x) % NX
    dense = jnp.where(core == 0, step_y, step_x)
    sparse = jnp.where(core == 0, step_x, step_y)
    step_z = jnp.where(core == 0, (NZ - step_z) % NZ, step_z)
    step_z = jnp.where(step_z <= 4, step_z, 12 - step_z)
    holder = jnp.where(jnp.arange(TILES) < 64, core, 1 - core)
    code = (dense * 4 + sparse) * 128 + (dense * NZ + step_z) * 4 + holder * 2 + which
    info, *requests = call(
        plan_kernel,
        [struct((INFO,), i32)] + [struct((128,), i32)] * 3,
        [SMEM] * 2,
        [SMEM] * 4,
        [pltpu.SMEM((8,), i32)],
        moved_bytes=100000,
    )(code.astype(i32), rows)
    requests = [along_sparse(requests[k - 1], k) for k in (1, 2, 3)]

    column, *requests = lax.optimization_barrier((column, *requests))
    parts = [column] + [along_dense(column, -j) for j in range(1, 4)]

    away = jnp.arange(4)
    asker = jnp.where(
        core == 0,
        node - x + (x - away) % NX,
        node - y * (NZ * NX) + (y - away) % NY * (NZ * NX),
    )
    lists = jnp.stack([part.reshape(NZ, MSG, BLK)[:, ROWS : ROWS + 4] for part in parts])
    chosen = (jnp.arange(BLK)[:, None] == asker[None, :]).astype(bf16)
    table = jnp.dot(lists.reshape(4 * NZ * 4, BLK), chosen, preferred_element_type=f32)
    table = table.astype(i32).reshape(-1)

    picked = call(
        pick_kernel,
        [struct((FAR, BLK), bf16)] * 3,
        [VMEM] * 4 + [ANY] * 4,
        [VMEM] * 3,
        [pltpu.SMEM((128,), i32)] * 3 + [pltpu.SMEM((512,), i32), dma((4,))],
        moved_bytes=7000000,
    )(*parts, *requests, table)
    far = [along_sparse(picked[k - 1], -k) for k in (1, 2, 3)]

    near = call(
        near_kernel,
        struct((ROWS, BLK), f32),
        [VMEM] * 5 + [ANY] * 2,
        VMEM,
        [
            pltpu.VMEM((ROWS + HALF, BLK), f32),
            pltpu.SMEM((INFO,), i32),
            pltpu.SMEM((512,), i32),
            dma((2,)),
        ],
        flops=2 * 32 * HALF * BLK * BLK,
        moved_bytes=11000000,
    )(*parts, tiles, info, table)
    agg_half = call(
        far_kernel,
        struct((ROWS, BLK), bf16),
        [VMEM] * 5 + [ANY],
        VMEM,
        [pltpu.VMEM((ROWS + HALF, BLK), f32), pltpu.SMEM((INFO,), i32), dma((1,))],
        flops=2 * 96 * HALF * BLK * BLK,
        moved_bytes=7000000,
    )(near, *far, tiles, info)
    other_half = to_other_core(agg_half)

    activations, sums, turned, second_back = call(
        middle_kernel,
        [
            struct((NB * BLK, BLK), bf16),
            struct((SUMS, BLK), f32),
            struct((ROWS, BLK), bf16),
            struct((FAR, BLK), bf16),
        ],
        [SMEM] + [VMEM] * 6 + [ANY],
        [VMEM] * 4,
        [pltpu.SMEM((INFO,), i32), dma((1,))],
        flops=2 * TILES * HALF * BLK * BLK,
        moved_bytes=8000000,
    )(
        core_array, agg_half, other_half, weight, out_bias[None, :], out_grad, tiles, info
    )
    first_back, third_back = call(
        side_kernel,
        [struct((FAR, BLK), bf16)] * 2,
        [VMEM] * 2 + [ANY],
        [VMEM] * 2,
        [pltpu.SMEM((INFO,), i32), dma((1,))],
        flops=2 * 64 * HALF * BLK * BLK,
        moved_bytes=4000000,
    )(tiles, turned, info)
    second_back = along_sparse(second_back, 2)
    back = [along_sparse(first_back, 1), second_back, along_sparse(third_back, 3)]

    sums = butterfly(sums, lambda step, y, z, x, c: (y, z ^ step, x, c), NZ)
    owned = call(
        owner_kernel,
        [struct((SEND, BLK), bf16)] + [struct((SEND + 2 * SUMS, BLK), bf16)] * 3,
        [ANY] * 5 + [VMEM] * 6,
        [VMEM] * 4,
        [
            pltpu.VMEM((257 * HALF, BLK), f32),
            pltpu.SMEM((INFO,), i32),
            pltpu.SMEM((512,), i32),
        ]
        + [pltpu.SMEM((128,), i32)] * 3
        + [dma((5,))],
        flops=2 * 32 * HALF * BLK * BLK,
        moved_bytes=11000000,
        vmem=21,
    )(info, table, *requests, turned, tiles, *back, sums)
    owned = [owned[0]] + [along_dense(owned[j], j) for j in range(1, 4)]
    keep, opposite, mine, swap, sums = call(
        split_sum_kernel,
        [struct((ROWS, BLK), bf16)] * 2
        + [struct((3 * ROWS, BLK), bf16)] * 2
        + [struct((SUMS, BLK), f32)],
        [SMEM] + [VMEM] * 5,
        [VMEM] * 5,
        moved_bytes=5000000,
    )(jnp.reshape(jnp.where(core == 0, y, x) % 2, (1,)).astype(i32), *owned, sums)
    opposite = along_z(opposite, 4)
    swap = to_other_core(swap)
    pieces = [
        jnp.concatenate([mine[s * ROWS : (s + 1) * ROWS], swap[s * ROWS : (s + 1) * ROWS]], axis=0)
        for s in range(3)
    ]
    pieces = [along_z(pieces[s - 1], -s) for s in (3, 2, 1)][::-1]
    sums = butterfly(sums, lambda step, y, z, x, c: (y, z, x ^ step, c) if c == 0 else (y ^ step, z, x, c), NX)

    hold, send, sums = call(
        last_sum_kernel,
        [struct((ROWS, BLK), f32)] * 2 + [struct((SUMS, BLK), f32)],
        [SMEM] + [VMEM] * 6,
        [VMEM] * 3,
        moved_bytes=1500000,
    )(core_array, sums, keep, opposite, *pieces)
    feature_grad, weight_grad, bias_grad = call(
        turn_kernel,
        [struct((NB // 2 * BLK, BLK), f32), struct((BLK, BLK), f32), struct((1, BLK), f32)],
        [SMEM] + [VMEM] * 3,
        [VMEM] * 3,
        moved_bytes=1000000,
    )(core_array, hold, to_other_core(send), sums)

    def again(state):
        return (jnp.float32(0.0),) + general_shards(
            features, weight, out_bias, edge_tiles, block_row, tile_slot, send_list, out_grad
        )

    state = (sums[BLK + 1, 0], activations, feature_grad, weight_grad, bias_grad.reshape(-1))
    return lax.while_loop(lambda state: state[0] > 0.5, again, state)[1:]


def solution(mesh):
    placed = (
        P("nodes", None),
        P(),
        P(),
        P(("nodes", "rep"), None, None),
        P(("nodes", "rep")),
        P(("nodes", "rep")),
        P(("nodes", "rep"), None),
        P("nodes", None),
    )
    return jax.shard_map(
        shards,
        mesh=mesh,
        in_specs=placed,
        out_specs=(P("nodes", "rep"), P(("nodes", "rep"), None), P(None, "rep"), P("rep")),
        check_vma=False,
    )
```

profile of v0, /device:TPU:1, one launch (start us, length us, event | category | flops | bytes accessed | tf_op | source)
XLA Modules:
  0.0 234.2 jit_solution(9911487086717567877)
XLA Ops:
  8.5 3.2 %collective-permute-start = (s32[3,128]{1,0:T(4,128)S(1)}, s32[3,128]{1,0:T(4,128)S(1)}, u32[]{:S(2)}, u32[]{:S(2)}) collective-permute-start(s32[3,128]{1,0:T(4,128)S(1)} %pad_add_fusion.own_ref), channel_id=1, source_target_pairs={{0,1},{1,0},{2,3},{3,2},{4,5},{5,4},{6,7},{7,6},{8,9},{9,8},{10,11... | collective-permute-start | bytes 4616 | tf_op jit(solution)/shard_map/ppermute | solution.py:118
  13.7 4.4 %collective-permute-start.2 = (bf16[1040,128]{1,0:T(8,128)(2,1)S(1)}, bf16[1040,128]{1,0:T(8,128)(2,1)S(1)}, u32[]{:S(2)}, u32[]{:S(2)}) collective-permute-start(bf16[1040,128]{1,0:T(8,128)(2,1)S(1)} %get-tuple-element.107), channel_id=1, source_target_pairs={{0,16},{1,49},{2,18},{3,51},{4,20},{5,53},{6,22},{7,55},{8,24},{9,... | collective-permute-start | bytes 798728 | tf_op jit(solution)/shard_map/ppermute | solution.py:118
  18.9 6.3 %shard_map.111 = (s32[640]{0:T(1024)S(1)}, s32[128]{0:T(128)S(1)}, s32[128]{0:T(128)S(1)}, s32[128]{0:T(128)S(1)}) custom-call(s32[128]{0:T(128)S(1)} %get-tuple-element.202.code_ref, s32[128]{0:T(128)S(1)} %get-tuple-element.201.rows_ref), custom_call_target="tpu_custom_call" | custom-call | bytes 100000 | tf_op jit(solution)/shard_map/pallas_call | solution.py:572
  26.6 2.6 %collective-permute-start.8 = (s32[128]{0:T(128)S(1)}, s32[128]{0:T(128)S(1)}, u32[]{:S(2)}, u32[]{:S(2)}) collective-permute-start(s32[128]{0:T(128)S(1)} %get-tuple-element.111), channel_id=1, source_target_pairs={{0,4},{1,129},{2,6},{3,131},{4,0},{5,133},{6,2},{7,135},{8,12},{9,... | collective-permute-start | bytes 1544 | tf_op jit(solution)/shard_map/ppermute | solution.py:118
  31.4 4.6 %collective-permute-done.3 = bf16[1040,128]{1,0:T(8,128)(2,1)S(1)} collective-permute-done((bf16[1040,128]{1,0:T(8,128)(2,1)S(1)}, bf16[1040,128]{1,0:T(8,128)(2,1)S(1)}, u32[]{:S(2)}, u32[]{:S(2)}) %collective-permute-start.3) | collective-permute-done | bytes 266272 | tf_op jit(solution)/shard_map/ppermute | solution.py:118
  44.4 3.3 %collective-permute-start.13 = (bf16[64,128,128]{2,1,0:T(8,128)(2,1)}, bf16[64,128,128]{2,1,0:T(8,128)(2,1)}, u32[]{:S(2)}, u32[]{:S(2)}) collective-permute-start(bf16[64,128,128]{2,1,0:T(8,128)(2,1)} %param.13), channel_id=1, source_target_pairs={{0,1},{1,0},{2,3},{3,2},{4,5},{5,4},{6,7},{7,6},{8,9},{9,8},{10,11... | collective-permute-start | bytes 6291464 | tf_op jit(solution)/shard_map/ppermute | solution.py:118
  47.7 20.9 %collective-permute-done.12.d_ref = bf16[4224,128]{1,0:T(8,128)(2,1)S(1)} collective-permute-done((bf16[4224,128]{1,0:T(8,128)(2,1)S(1)}, bf16[4224,128]{1,0:T(8,128)(2,1)S(1)}, u32[]{:S(2)}, u32[]{:S(2)}) %collective-permute-start.12) | collective-permute-done | bytes 1081376 | tf_op jit(solution)/shard_map/ppermute | solution.py:118
  70.5 5.8 %shard_map.114 = (bf16[3584,128]{1,0:T(8,128)(2,1)S(1)}, bf16[3584,128]{1,0:T(8,128)(2,1)S(1)}, bf16[3584,128]{1,0:T(8,128)(2,1)S(1)}) custom-call(bf16[4224,128]{1,0:T(8,128)(2,1)S(1)} %constant_dynamic-update-slice_fusion.a_ref, bf16[4224,128]{1,0:T(8,128)(2,1)} %collective-permute-done.10.b_ref, bf16[4224,128]{1,0:T(8,128)(2,1)S(1)} %collective-permute-done.11.c_ref, ...), custom_call_target="tpu_custom_call" | custom-call | bytes 7000000 | tf_op jit(solution)/shard_map/pallas_call | solution.py:596
  76.2 2.8 %collective-permute-start.14 = (bf16[3584,128]{1,0:T(8,128)(2,1)S(1)}, bf16[3584,128]{1,0:T(8,128)(2,1)S(1)}, u32[]{:S(2)}, u32[]{:S(2)}) collective-permute-start(bf16[3584,128]{1,0:T(8,128)(2,1)S(1)} %get-tuple-element.117), channel_id=1, source_target_pairs={{0,6},{1,193},{2,0},{3,195},{4,2},{5,197},{6,4},{7,199},{8,14},{9,... | collective-permute-start | bytes 2752520 | tf_op jit(solution)/shard_map/ppermute | solution.py:118
  84.1 3.4 %shard_map.113.near_ref = f32[512,128]{1,0:T(8,128)S(1)} custom-call(bf16[4224,128]{1,0:T(8,128)(2,1)S(1)} %constant_dynamic-update-slice_fusion.a_ref, bf16[4224,128]{1,0:T(8,128)(2,1)} %collective-permute-done.10.b_ref, bf16[4224,128]{1,0:T(8,128)(2,1)S(1)} %collective-permute-done.11.c_ref, bf16[4224,128]{1,0:T(8,128)(2,1)S(1)} %collective-permute-done.12.d_ref, ...), custom_call_target="tpu_custom_call" | custom-call | flops 67108864 | bytes 11000000 | tf_op jit(solution)/shard_map/pallas_call | solution.py:606
  87.5 11.7 %collective-permute-done.14.r1 = bf16[3584,128]{1,0:T(8,128)(2,1)S(1)} collective-permute-done((bf16[3584,128]{1,0:T(8,128)(2,1)S(1)}, bf16[3584,128]{1,0:T(8,128)(2,1)S(1)}, u32[]{:S(2)}, u32[]{:S(2)}) %collective-permute-start.14) | collective-permute-done | bytes 917536 | tf_op jit(solution)/shard_map/ppermute | solution.py:118
  99.2 3.9 %collective-permute-done.16.r3 = bf16[3584,128]{1,0:T(8,128)(2,1)S(1)} collective-permute-done((bf16[3584,128]{1,0:T(8,128)(2,1)S(1)}, bf16[3584,128]{1,0:T(8,128)(2,1)S(1)}, u32[]{:S(2)}, u32[]{:S(2)}) %collective-permute-start.16) | collective-permute-done | bytes 917536 | tf_op jit(solution)/shard_map/ppermute | solution.py:118
  103.2 4.1 %shard_map.115.own_agg = bf16[512,128]{1,0:T(8,128)(2,1)S(1)} custom-call(f32[512,128]{1,0:T(8,128)S(1)} %shard_map.113.near_ref, bf16[3584,128]{1,0:T(8,128)(2,1)S(1)} %collective-permute-done.14.r1, bf16[3584,128]{1,0:T(8,128)(2,1)S(1)} %collective-permute-done.15.r2, bf16[3584,128]{1,0:T(8,128)(2,1)S(1)} %collective-permute-done.16.r3, ...), custom_call_target="tpu_custom_call" | custom-call | flops 201326592 | bytes 7000000 | tf_op jit(solution)/shard_map/pallas_call | solution.py:620
  109.1 4.3 %shard_map.116 = (bf16[1024,128]{1,0:T(8,128)(2,1)}, f32[144,128]{1,0:T(8,128)S(1)}, bf16[512,128]{1,0:T(8,128)(2,1)S(1)}, bf16[3584,128]{1,0:T(8,128)(2,1)S(1)}) custom-call(s32[1]{0:T(128)} %bitcast.15.core_ref, bf16[512,128]{1,0:T(8,128)(2,1)S(1)} %shard_map.115.own_agg, bf16[512,128]{1,0:T(8,128)(2,1)S(1)} %collective-permute-done.17.other_agg, ...), custom_call_target="tpu_custom_call" | custom-call | flops 268435456 | bytes 8000000 | tf_op jit(solution)/shard_map/pallas_call | solution.py:631
  113.5 3.0 %collective-permute-start.19 = (bf16[3584,128]{1,0:T(8,128)(2,1)S(1)}, bf16[3584,128]{1,0:T(8,128)(2,1)S(1)}, u32[]{:S(2)}, u32[]{:S(2)}) collective-permute-start(bf16[3584,128]{1,0:T(8,128)(2,1)S(1)} %get-tuple-element.122), channel_id=1, source_target_pairs={{0,4},{1,129},{2,6},{3,131},{4,0},{5,133},{6,2},{7,135},{8,12},{9,... | collective-permute-start | bytes 2752520 | tf_op jit(solution)/shard_map/ppermute | solution.py:118
  125.3 2.6 %collective-permute-start.22 = (f32[144,128]{1,0:T(8,128)S(1)}, f32[144,128]{1,0:T(8,128)S(1)}, u32[]{:S(2)}, u32[]{:S(2)}) collective-permute-start(f32[144,128]{1,0:T(8,128)S(1)} %add.210), channel_id=1, source_target_pairs={{0,16},{1,17},{2,18},{3,19},{4,20},{5,21},{6,22},{7,23},{8,24},{9,... | collective-permute-start | bytes 221192 | tf_op jit(solution)/shard_map/ppermute | solution.py:118
  129.9 7.6 %collective-permute-start.23 = (f32[144,128]{1,0:T(8,128)S(1)}, f32[144,128]{1,0:T(8,128)S(1)}, u32[]{:S(2)}, u32[]{:S(2)}) collective-permute-start(f32[144,128]{1,0:T(8,128)S(1)} %add.211), channel_id=1, source_target_pairs={{0,32},{1,33},{2,34},{3,35},{4,36},{5,37},{6,38},{7,39},{8,40},{9,... | collective-permute-start | bytes 221192 | tf_op jit(solution)/shard_map/ppermute | solution.py:118
  139.5 4.4 %shard_map.118 = (bf16[4096,128]{1,0:T(8,128)(2,1)S(1)}, bf16[4384,128]{1,0:T(8,128)(2,1)}, bf16[4384,128]{1,0:T(8,128)(2,1)}, bf16[4384,128]{1,0:T(8,128)(2,1)}) custom-call(s32[640]{0:T(1024)S(1)} %get-tuple-element.105.info_ref, s32[512]{0:T(512)S(1)} %reshape.153.table_ref, s32[128]{0:T(128)S(1)} %collective-permute-done.7.first_ref, ...), custom_call_target="tpu_custom_call" | custom-call | flops 67108864 | bytes 11000000 | tf_op jit(solution)/shard_map/pallas_call | solution.py:660
  150.0 11.0 %collective-permute-done.24.b_ref = bf16[4384,128]{1,0:T(8,128)(2,1)S(1)} collective-permute-done((bf16[4384,128]{1,0:T(8,128)(2,1)}, bf16[4384,128]{1,0:T(8,128)(2,1)S(1)}, u32[]{:S(2)}, u32[]{:S(2)}) %collective-permute-start.24) | collective-permute-done | bytes 1122336 | tf_op jit(solution)/shard_map/ppermute | solution.py:118
  161.0 12.4 %collective-permute-done.25.c_ref = bf16[4384,128]{1,0:T(8,128)(2,1)S(1)} collective-permute-done((bf16[4384,128]{1,0:T(8,128)(2,1)}, bf16[4384,128]{1,0:T(8,128)(2,1)S(1)}, u32[]{:S(2)}, u32[]{:S(2)}) %collective-permute-start.25) | collective-permute-done | bytes 1122336 | tf_op jit(solution)/shard_map/ppermute | solution.py:118
  175.5 2.8 %collective-permute-start.30 = (bf16[1536,128]{1,0:T(8,128)(2,1)S(1)}, bf16[1536,128]{1,0:T(8,128)(2,1)S(1)}, u32[]{:S(2)}, u32[]{:S(2)}) collective-permute-start(bf16[1536,128]{1,0:T(8,128)(2,1)S(1)} %get-tuple-element.133), channel_id=1, source_target_pairs={{0,1},{1,0},{2,3},{3,2},{4,5},{5,4},{6,7},{7,6},{8,9},{9,8},{10,11... | collective-permute-start | bytes 1179656 | tf_op jit(solution)/shard_map/ppermute | solution.py:118
  179.7 17.5 %collective-permute-start.31 = (bf16[1024,128]{1,0:T(8,128)(2,1)S(1)}, bf16[1024,128]{1,0:T(8,128)(2,1)S(1)}, u32[]{:S(2)}, u32[]{:S(2)}) collective-permute-start(bf16[1024,128]{1,0:T(8,128)(2,1)S(1)} %pad_maximum_fusion.1), channel_id=1, source_target_pairs={{0,56},{1,9},{2,58},{3,11},{4,60},{5,13},{6,62},{7,15},{8,0},{9,17... | collective-permute-start | bytes 786440 | tf_op jit(solution)/shard_map/ppermute | solution.py:118
  197.2 2.8 %collective-permute-start.32 = (bf16[1024,128]{1,0:T(8,128)(2,1)S(1)}, bf16[1024,128]{1,0:T(8,128)(2,1)S(1)}, u32[]{:S(2)}, u32[]{:S(2)}) collective-permute-start(bf16[1024,128]{1,0:T(8,128)(2,1)S(1)} %pad_maximum_fusion.2), channel_id=1, source_target_pairs={{0,48},{1,17},{2,50},{3,19},{4,52},{5,21},{6,54},{7,23},{8,56},{9,... | collective-permute-start | bytes 786440 | tf_op jit(solution)/shard_map/ppermute | solution.py:118
  210.2 11.6 %collective-permute-done.29.far_ref = bf16[512,128]{1,0:T(8,128)(2,1)S(1)} collective-permute-done((bf16[512,128]{1,0:T(8,128)(2,1)S(1)}, bf16[512,128]{1,0:T(8,128)(2,1)S(1)}, u32[]{:S(2)}, u32[]{:S(2)}) %collective-permute-start.29) | collective-permute-done | bytes 131104 | tf_op jit(solution)/shard_map/ppermute | solution.py:118
  (118 shorter events, 62.7 us)
Async XLA Ops:
  13.7 16.6 %collective-permute-start.2 = (bf16[1040,128]{1,0:T(8,128)(2,1)S(1)}, bf16[1040,128]{1,0:T(8,128)(2,1)S(1)}, u32[]{:S(2)}, u32[]{:S(2)}) collective-permute-start(bf16[1040,128]{1,0:T(8,128)(2,1)S(1)} %get-tuple-element.107), channel_id=1, source_target_pairs={{0,16},{1,49},{2,18},{3,51},{4,20},{5,53},{6,22},{7,55},{8,24},{9,... | collective-permute-start | bytes 798728 | tf_op jit(solution)/shard_map/ppermute | solution.py:118
  18.1 12.2 %collective-permute-start.1 = (bf16[1040,128]{1,0:T(8,128)(2,1)S(1)}, bf16[1040,128]{1,0:T(8,128)(2,1)S(1)}, u32[]{:S(2)}, u32[]{:S(2)}) collective-permute-start(bf16[1040,128]{1,0:T(8,128)(2,1)S(1)} %get-tuple-element.107), channel_id=1, source_target_pairs={{0,8},{1,57},{2,10},{3,59},{4,12},{5,61},{6,14},{7,63},{8,16},{9,1... | collective-permute-start | bytes 798728 | tf_op jit(solution)/shard_map/ppermute | solution.py:118
  25.2 16.2 %collective-permute-start.7 = (s32[128]{0:T(128)S(1)}, s32[128]{0:T(128)S(1)}, u32[]{:S(2)}, u32[]{:S(2)}) collective-permute-start(s32[128]{0:T(128)S(1)} %get-tuple-element.110), channel_id=1, source_target_pairs={{0,2},{1,65},{2,4},{3,67},{4,6},{5,69},{6,0},{7,71},{8,10},{9,73},... | collective-permute-start | bytes 1544 | tf_op jit(solution)/shard_map/ppermute | solution.py:118
  26.6 14.8 %collective-permute-start.8 = (s32[128]{0:T(128)S(1)}, s32[128]{0:T(128)S(1)}, u32[]{:S(2)}, u32[]{:S(2)}) collective-permute-start(s32[128]{0:T(128)S(1)} %get-tuple-element.111), channel_id=1, source_target_pairs={{0,4},{1,129},{2,6},{3,131},{4,0},{5,133},{6,2},{7,135},{8,12},{9,... | collective-permute-start | bytes 1544 | tf_op jit(solution)/shard_map/ppermute | solution.py:118
  29.2 12.2 %collective-permute-start.9 = (s32[128]{0:T(128)S(1)}, s32[128]{0:T(128)S(1)}, u32[]{:S(2)}, u32[]{:S(2)}) collective-permute-start(s32[128]{0:T(128)S(1)} %get-tuple-element.112), channel_id=1, source_target_pairs={{0,6},{1,193},{2,0},{3,195},{4,2},{5,197},{6,4},{7,199},{8,14},{9,... | collective-permute-start | bytes 1544 | tf_op jit(solution)/shard_map/ppermute | solution.py:118
  31.2 6.6 %collective-permute-start.4 = (bf16[528,128]{1,0:T(8,128)(2,1)S(1)}, bf16[528,128]{1,0:T(8,128)(2,1)S(1)}, u32[]{:S(2)}, u32[]{:S(2)}) collective-permute-start(bf16[528,128]{1,0:T(8,128)(2,1)S(1)} %get-tuple-element.200), channel_id=1, source_target_pairs={{0,16},{1,49},{2,18},{3,51},{4,20},{5,53},{6,22},{7,55},{8,24},{9,... | collective-permute-start | bytes 405512 | tf_op jit(solution)/shard_map/ppermute | solution.py:118
  41.4 27.2 %collective-permute-start.12 = (bf16[4224,128]{1,0:T(8,128)(2,1)S(1)}, bf16[4224,128]{1,0:T(8,128)(2,1)S(1)}, u32[]{:S(2)}, u32[]{:S(2)}) collective-permute-start(bf16[4224,128]{1,0:T(8,128)(2,1)S(1)} %constant_dynamic-update-slice_fusion.a_ref), channel_id=1, source_target_pairs={{0,64},{1,3},{2,66},{3,5},{4,68},{5,7},{6,70},{7,1},{8,72},{9,11},... | collective-permute-start | bytes 3244040 | tf_op jit(solution)/shard_map/ppermute | solution.py:118
  41.8 26.8 %collective-permute-start.11 = (bf16[4224,128]{1,0:T(8,128)(2,1)S(1)}, bf16[4224,128]{1,0:T(8,128)(2,1)S(1)}, u32[]{:S(2)}, u32[]{:S(2)}) collective-permute-start(bf16[4224,128]{1,0:T(8,128)(2,1)S(1)} %constant_dynamic-update-slice_fusion.a_ref), channel_id=1, source_target_pairs={{0,128},{1,5},{2,130},{3,7},{4,132},{5,1},{6,134},{7,3},{8,136},{9... | collective-permute-start | bytes 3244040 | tf_op jit(solution)/shard_map/ppermute | solution.py:118
  43.1 26.2 %collective-permute-start.10 = (bf16[4224,128]{1,0:T(8,128)(2,1)S(1)}, bf16[4224,128]{1,0:T(8,128)(2,1)}, u32[]{:S(2)}, u32[]{:S(2)}) collective-permute-start(bf16[4224,128]{1,0:T(8,128)(2,1)S(1)} %constant_dynamic-update-slice_fusion.a_ref), channel_id=1, source_target_pairs={{0,192},{1,7},{2,194},{3,1},{4,196},{5,3},{6,198},{7,5},{8,200},{9... | collective-permute-start | bytes 3244040 | tf_op jit(solution)/shard_map/ppermute | solution.py:118
  44.4 37.7 %collective-permute-start.13 = (bf16[64,128,128]{2,1,0:T(8,128)(2,1)}, bf16[64,128,128]{2,1,0:T(8,128)(2,1)}, u32[]{:S(2)}, u32[]{:S(2)}) collective-permute-start(bf16[64,128,128]{2,1,0:T(8,128)(2,1)} %param.13), channel_id=1, source_target_pairs={{0,1},{1,0},{2,3},{3,2},{4,5},{5,4},{6,7},{7,6},{8,9},{9,8},{10,11... | collective-permute-start | bytes 6291464 | tf_op jit(solution)/shard_map/ppermute | solution.py:118
  76.2 23.0 %collective-permute-start.14 = (bf16[3584,128]{1,0:T(8,128)(2,1)S(1)}, bf16[3584,128]{1,0:T(8,128)(2,1)S(1)}, u32[]{:S(2)}, u32[]{:S(2)}) collective-permute-start(bf16[3584,128]{1,0:T(8,128)(2,1)S(1)} %get-tuple-element.117), channel_id=1, source_target_pairs={{0,6},{1,193},{2,0},{3,195},{4,2},{5,197},{6,4},{7,199},{8,14},{9,... | collective-permute-start | bytes 2752520 | tf_op jit(solution)/shard_map/ppermute | solution.py:118
  79.1 20.2 %collective-permute-start.15 = (bf16[3584,128]{1,0:T(8,128)(2,1)S(1)}, bf16[3584,128]{1,0:T(8,128)(2,1)S(1)}, u32[]{:S(2)}, u32[]{:S(2)}) collective-permute-start(bf16[3584,128]{1,0:T(8,128)(2,1)S(1)} %get-tuple-element.118), channel_id=1, source_target_pairs={{0,4},{1,129},{2,6},{3,131},{4,0},{5,133},{6,2},{7,135},{8,12},{9,... | collective-permute-start | bytes 2752520 | tf_op jit(solution)/shard_map/ppermute | solution.py:118
  79.7 23.5 %collective-permute-start.16 = (bf16[3584,128]{1,0:T(8,128)(2,1)S(1)}, bf16[3584,128]{1,0:T(8,128)(2,1)S(1)}, u32[]{:S(2)}, u32[]{:S(2)}) collective-permute-start(bf16[3584,128]{1,0:T(8,128)(2,1)S(1)} %get-tuple-element.119), channel_id=1, source_target_pairs={{0,2},{1,65},{2,4},{3,67},{4,6},{5,69},{6,0},{7,71},{8,10},{9,73},... | collective-permute-start | bytes 2752520 | tf_op jit(solution)/shard_map/ppermute | solution.py:118
  113.5 26.0 %collective-permute-start.19 = (bf16[3584,128]{1,0:T(8,128)(2,1)S(1)}, bf16[3584,128]{1,0:T(8,128)(2,1)S(1)}, u32[]{:S(2)}, u32[]{:S(2)}) collective-permute-start(bf16[3584,128]{1,0:T(8,128)(2,1)S(1)} %get-tuple-element.122), channel_id=1, source_target_pairs={{0,4},{1,129},{2,6},{3,131},{4,0},{5,133},{6,2},{7,135},{8,12},{9,... | collective-permute-start | bytes 2752520 | tf_op jit(solution)/shard_map/ppermute | solution.py:118
  118.8 20.7 %collective-permute-start.18 = (bf16[3584,128]{1,0:T(8,128)(2,1)S(1)}, bf16[3584,128]{1,0:T(8,128)(2,1)S(1)}, u32[]{:S(2)}, u32[]{:S(2)}) collective-permute-start(bf16[3584,128]{1,0:T(8,128)(2,1)S(1)} %get-tuple-element.121), channel_id=1, source_target_pairs={{0,2},{1,65},{2,4},{3,67},{4,6},{5,69},{6,0},{7,71},{8,10},{9,73},... | collective-permute-start | bytes 2752520 | tf_op jit(solution)/shard_map/ppermute | solution.py:118
  119.1 20.4 %collective-permute-start.20 = (bf16[3584,128]{1,0:T(8,128)(2,1)S(1)}, bf16[3584,128]{1,0:T(8,128)(2,1)S(1)}, u32[]{:S(2)}, u32[]{:S(2)}) collective-permute-start(bf16[3584,128]{1,0:T(8,128)(2,1)S(1)} %get-tuple-element.123), channel_id=1, source_target_pairs={{0,6},{1,193},{2,0},{3,195},{4,2},{5,197},{6,4},{7,199},{8,14},{9,... | collective-permute-start | bytes 2752520 | tf_op jit(solution)/shard_map/ppermute | solution.py:118
  129.9 9.5 %collective-permute-start.23 = (f32[144,128]{1,0:T(8,128)S(1)}, f32[144,128]{1,0:T(8,128)S(1)}, u32[]{:S(2)}, u32[]{:S(2)}) collective-permute-start(f32[144,128]{1,0:T(8,128)S(1)} %add.211), channel_id=1, source_target_pairs={{0,32},{1,33},{2,34},{3,35},{4,36},{5,37},{6,38},{7,39},{8,40},{9,... | collective-permute-start | bytes 221192 | tf_op jit(solution)/shard_map/ppermute | solution.py:118
  144.8 16.2 %collective-permute-start.24 = (bf16[4384,128]{1,0:T(8,128)(2,1)}, bf16[4384,128]{1,0:T(8,128)(2,1)S(1)}, u32[]{:S(2)}, u32[]{:S(2)}) collective-permute-start(bf16[4384,128]{1,0:T(8,128)(2,1)} %get-tuple-element.126), channel_id=1, source_target_pairs={{0,64},{1,3},{2,66},{3,5},{4,68},{5,7},{6,70},{7,1},{8,72},{9,11},... | collective-permute-start | bytes 3366920 | tf_op jit(solution)/shard_map/ppermute | solution.py:118
  146.3 27.1 %collective-permute-start.25 = (bf16[4384,128]{1,0:T(8,128)(2,1)}, bf16[4384,128]{1,0:T(8,128)(2,1)S(1)}, u32[]{:S(2)}, u32[]{:S(2)}) collective-permute-start(bf16[4384,128]{1,0:T(8,128)(2,1)} %get-tuple-element.127), channel_id=1, source_target_pairs={{0,128},{1,5},{2,130},{3,7},{4,132},{5,1},{6,134},{7,3},{8,136},{9... | collective-permute-start | bytes 3366920 | tf_op jit(solution)/shard_map/ppermute | solution.py:118
  147.9 25.8 %collective-permute-start.26 = (bf16[4384,128]{1,0:T(8,128)(2,1)}, bf16[4384,128]{1,0:T(8,128)(2,1)S(1)}, u32[]{:S(2)}, u32[]{:S(2)}) collective-permute-start(bf16[4384,128]{1,0:T(8,128)(2,1)} %get-tuple-element.128), channel_id=1, source_target_pairs={{0,192},{1,7},{2,194},{3,1},{4,196},{5,3},{6,198},{7,5},{8,200},{9... | collective-permute-start | bytes 3366920 | tf_op jit(solution)/shard_map/ppermute | solution.py:118
  179.7 42.1 %collective-permute-start.31 = (bf16[1024,128]{1,0:T(8,128)(2,1)S(1)}, bf16[1024,128]{1,0:T(8,128)(2,1)S(1)}, u32[]{:S(2)}, u32[]{:S(2)}) collective-permute-start(bf16[1024,128]{1,0:T(8,128)(2,1)S(1)} %pad_maximum_fusion.1), channel_id=1, source_target_pairs={{0,56},{1,9},{2,58},{3,11},{4,60},{5,13},{6,62},{7,15},{8,0},{9,17... | collective-permute-start | bytes 786440 | tf_op jit(solution)/shard_map/ppermute | solution.py:118
  197.2 24.6 %collective-permute-start.32 = (bf16[1024,128]{1,0:T(8,128)(2,1)S(1)}, bf16[1024,128]{1,0:T(8,128)(2,1)S(1)}, u32[]{:S(2)}, u32[]{:S(2)}) collective-permute-start(bf16[1024,128]{1,0:T(8,128)(2,1)S(1)} %pad_maximum_fusion.2), channel_id=1, source_target_pairs={{0,48},{1,17},{2,50},{3,19},{4,52},{5,21},{6,54},{7,23},{8,56},{9,... | collective-permute-start | bytes 786440 | tf_op jit(solution)/shard_map/ppermute | solution.py:118
  200.0 21.8 %collective-permute-start.33 = (bf16[1024,128]{1,0:T(8,128)(2,1)S(1)}, bf16[1024,128]{1,0:T(8,128)(2,1)S(1)}, u32[]{:S(2)}, u32[]{:S(2)}) collective-permute-start(bf16[1024,128]{1,0:T(8,128)(2,1)S(1)} %pad_maximum_fusion.3), channel_id=1, source_target_pairs={{0,40},{1,25},{2,42},{3,27},{4,44},{5,29},{6,46},{7,31},{8,48},{9,... | collective-permute-start | bytes 786440 | tf_op jit(solution)/shard_map/ppermute | solution.py:118
  202.5 19.2 %collective-permute-start.29 = (bf16[512,128]{1,0:T(8,128)(2,1)S(1)}, bf16[512,128]{1,0:T(8,128)(2,1)S(1)}, u32[]{:S(2)}, u32[]{:S(2)}) collective-permute-start(bf16[512,128]{1,0:T(8,128)(2,1)S(1)} %get-tuple-element.131), channel_id=1, source_target_pairs={{0,32},{1,33},{2,34},{3,35},{4,36},{5,37},{6,38},{7,39},{8,40},{9,... | collective-permute-start | bytes 393224 | tf_op jit(solution)/shard_map/ppermute | solution.py:118
  (20 other events, 291.0 us)
where the time goes:
time: 238 us; the launch traced here: 234 us
  waiting for transfers between devices  90.6 us (38%)
  starting transfers between devices  84.1 us (35%)
  Pallas kernels  33.1 us (14%)
  between operations  14.6 us (6%)
  local copies, waits for them, and re-layouts  9.34 us (4%)
    ppermute x35, waiting for transfers between devices, moved(): return lax.ppermute(value, ('nodes', 'rep'), pairs)  90.6 us
    ppermute x35, starting transfers between devices, moved(): return lax.ppermute(value, ('nodes', 'rep'), pairs)  84.1 us
    pallas_call x1, Pallas kernels, shards(): call(plan_kernel, [struct((INFO,), i32)] + [struct((128,), i32)] * 3, [SM...  6.26 us
    pallas_call x1, Pallas kernels, shards(): call(pick_kernel, [struct((FAR, BLK), bf16)] * 3, [VMEM] * 4 + [ANY] * 4,...  5.76 us
    unnamed x27, local copies, waits for them, and re-layouts  5.53 us
  transfers between devices with their start and end apart: 35, of which 20 were waited for; matrix products, arithmetic and copies ran while one was open for 3% of the time, Pallas kernels for 8%

commit v1 on v0

--- a/solution.py
+++ b/solution.py
@@ -92,15 +92,12 @@
     ).astype(jnp.float32)
     own_grad = lax.dynamic_slice_in_dim(pre_grad, rep_position * half_out, half_out, 1)
     norm_scale = 1.0 / math.sqrt(features.shape[0] * node_count)
-    weight_part = (
-        lax.dot_general(
-            aggregate_bf, own_grad, (((0,), (0,)), ((), ())), preferred_element_type=jnp.float32
-        )
-        * norm_scale
-    )
-    bias_part = jnp.sum(own_grad.astype(jnp.float32), axis=0) * norm_scale
-    weight_grad, bias_grad = lax.psum((weight_part, bias_part), "nodes")
-    return (activations, feature_grad, weight_grad, bias_grad)
+    weight_part = lax.dot_general(
+        aggregate_bf, own_grad, (((0,), (0,)), ((), ())), preferred_element_type=jnp.float32
+    )
+    bias_part = jnp.sum(own_grad.astype(jnp.float32), axis=0)
+    weight_sum, bias_sum = lax.psum((weight_part, bias_part), "nodes")
+    return (activations, feature_grad, weight_sum * norm_scale, bias_sum * norm_scale)
 
 
 def device_of(y, z, x, c):
@@ -197,9 +194,9 @@
 
     def place(t, carry):
         code = code_ref[t]
-        other_key = code // 512
-        key = code // 128 % 4
-        slot = code % 128
+        other_key = code >> 9
+        key = (code >> 7) & 3
+        slot = code & 127
         count_ref[4 + other_key] = count_ref[4 + other_key] + 1
         rank = count_ref[key]
         count_ref[key] = rank + 1
@@ -249,8 +246,9 @@
 
 
 def local_block(parts, slot, table, k):
-    at = pl.ds(pl.multiple_of(slot // 4 % NZ * MSG + table[slot * 4 + k] * HALF, 16), HALF)
-    part = slot // (4 * NZ)
+    row = ((slot >> 2) & (NZ - 1)) * MSG + (table[(slot << 2) + k] << 6)
+    at = pl.ds(pl.multiple_of(row, 16), HALF)
+    part = slot >> 5
     low = jnp.where(part == 0, parts[0][at, :], parts[1][at, :])
     high = jnp.where(part == 2, parts[2][at, :], parts[3][at, :])
     return jnp.where(part < 2, low, high)
@@ -301,17 +299,18 @@
             acc[half_rows(row), :] += done[u]
         return carry
 
-    lax.fori_loop(0, (count + 7) // 8, body, 0)
+    lax.fori_loop(0, (count + 7) >> 3, body, 0)
     out_ref[...] = acc[:ROWS, :]
 
 
-def far_kernel(near_ref, r1, r2, r3, tiles, info_ref, out_ref, acc, info, sem):
+def far_kernel(steps, near_ref, *refs):
+    *moved_refs, tiles, info_ref, out_ref, acc, info, sem = refs
     copies = start_all([(info_ref, info)], sem)
     acc[:ROWS, :] = near_ref[...]
     acc[ROWS:, :] = jnp.zeros((HALF, BLK), jnp.float32)
     wait_all(copies)
-    for k, got in enumerate((r1, r2, r3)):
-        count = info[CNT0 + 1 + k]
+    for k, got in zip(steps, moved_refs):
+        count = info[CNT0 + k]
 
         def body(i, carry, k=k, got=got, count=count):
             done = []
@@ -319,18 +318,18 @@
                 p = i * 8 + u
                 done.append(
                     lax.dot_general(
-                        got[half_rows(p), :], tiles[info[REM0 + k * CAP + p]],
+                        got[half_rows(p), :], tiles[info[REM0 + (k - 1) * CAP + p]],
                         (((1,), (1,)), ((), ())), preferred_element_type=jnp.float32,
                     )
                 )
             for u in range(8):
                 p = i * 8 + u
-                row = jnp.where(p < count, info[ROW0 + info[REM0 + k * CAP + p]], NB)
+                row = jnp.where(p < count, info[ROW0 + info[REM0 + (k - 1) * CAP + p]], NB)
                 acc[half_rows(row), :] += done[u]
             return carry
 
-        lax.fori_loop(0, (count + 7) // 8, body, 0)
-    out_ref[...] = acc[:ROWS, :].astype(jnp.bfloat16)
+        lax.fori_loop(0, (count + 7) >> 3, body, 0)
+    out_ref[...] = acc[:ROWS, :].astype(out_ref.dtype)
 
 
 def products(step, tiles, turned_ref, info, out):
@@ -346,7 +345,7 @@
             ).astype(jnp.bfloat16)
         return carry
 
-    lax.fori_loop(0, (info[CNT0 + step] + 7) // 8, body, 0)
+    lax.fori_loop(0, (info[CNT0 + step] + 7) >> 3, body, 0)
 
 
 def middle_kernel(
@@ -417,7 +416,7 @@
     wait_all(copies)
 
     def total_rows(slot, k, used):
-        return half_rows(jnp.where(used, slot // 4 * NB + table[slot * 4 + k], 256))
+        return half_rows(jnp.where(used, ((slot >> 2) << 3) + table[(slot << 2) + k], 256))
 
     count = info[CNT0]
 
@@ -432,7 +431,7 @@
             total[total_rows(info[p], 0, p < count), :] += done[u]
         return carry
 
-    lax.fori_loop(0, (count + 7) // 8, near, 0)
+    lax.fori_loop(0, (count + 7) >> 3, near, 0)
     for k, (req, got) in enumerate(((q1, r1), (q2, r2), (q3, r3))):
         kept = req[64]
 
@@ -443,27 +442,15 @@
                 total[at, :] += got[half_rows(p), :].astype(jnp.float32)
             return carry
 
-        lax.fori_loop(0, (kept + 7) // 8, far, 0)
-    upper, lower = two_parts(sums_ref[...])
+        lax.fori_loop(0, (kept + 7) >> 3, far, 0)
     for j, out in enumerate((o0, o1, o2, o3)):
-        out[:SEND, :] = total[j * SEND : (j + 1) * SEND, :].astype(jnp.bfloat16)
-        if j > 0:
-            out[SEND : SEND + SUMS, :] = upper
-            out[SEND + SUMS :, :] = lower
+        out[...] = total[j * SEND : (j + 1) * SEND, :].astype(jnp.bfloat16)
 
 
 def split_sum_kernel(
-    odd_ref, a_ref, b_ref, c_ref, d_ref, sums_ref, keep_ref, far_ref, mine_ref, swap_ref, passed_ref
+    a_ref, b_ref, c_ref, d_ref, sums_ref, keep_ref, far_ref, mine_ref, swap_ref, passed_ref
 ):
-    def sent(ref):
-        upper, lower = ref[SEND : SEND + SUMS, :], ref[SEND + SUMS :, :]
-        return upper.astype(jnp.float32) + lower.astype(jnp.float32)
-
-    upper, lower = two_parts(sums_ref[...])
-    own = upper.astype(jnp.float32) + lower.astype(jnp.float32)
-    one, two, three = sent(b_ref), sent(c_ref), sent(d_ref)
-    odd = odd_ref[0] == 1
-    passed_ref[...] = (own + jnp.where(odd, three, one)) + (two + jnp.where(odd, one, three))
+    passed_ref[...] = sums_ref[...]
     for m in range(NZ):
         at = slice(m * ROWS, (m + 1) * ROWS)
         value = a_ref[at, :].astype(jnp.float32) + b_ref[at, :].astype(jnp.float32)
@@ -617,15 +604,17 @@
         flops=2 * 32 * HALF * BLK * BLK,
         moved_bytes=11000000,
     )(*parts, tiles, info, table)
-    agg_half = call(
-        far_kernel,
-        struct((ROWS, BLK), bf16),
-        [VMEM] * 5 + [ANY],
-        VMEM,
-        [pltpu.VMEM((ROWS + HALF, BLK), f32), pltpu.SMEM((INFO,), i32), dma((1,))],
-        flops=2 * 96 * HALF * BLK * BLK,
-        moved_bytes=7000000,
-    )(near, *far, tiles, info)
+    agg_half = near
+    for steps, kind in (((1, 3), f32), ((2,), bf16)):
+        agg_half = call(
+            functools.partial(far_kernel, steps),
+            struct((ROWS, BLK), kind),
+            [VMEM] * (2 + len(steps)) + [ANY],
+            VMEM,
+            [pltpu.VMEM((ROWS + HALF, BLK), f32), pltpu.SMEM((INFO,), i32), dma((1,))],
+            flops=2 * 32 * len(steps) * HALF * BLK * BLK,
+            moved_bytes=7000000,
+        )(agg_half, *[far[k - 1] for k in steps], tiles, info)
     other_half = to_other_core(agg_half)
 
     activations, sums, turned, second_back = call(
@@ -659,7 +648,7 @@
     sums = butterfly(sums, lambda step, y, z, x, c: (y, z ^ step, x, c), NZ)
     owned = call(
         owner_kernel,
-        [struct((SEND, BLK), bf16)] + [struct((SEND + 2 * SUMS, BLK), bf16)] * 3,
+        [struct((SEND, BLK), bf16)] + [struct((SEND, BLK), bf16)] * 3,
         [ANY] * 5 + [VMEM] * 6,
         [VMEM] * 4,
         [
@@ -679,10 +668,10 @@
         [struct((ROWS, BLK), bf16)] * 2
         + [struct((3 * ROWS, BLK), bf16)] * 2
         + [struct((SUMS, BLK), f32)],
-        [SMEM] + [VMEM] * 5,
+        [VMEM] * 5,
         [VMEM] * 5,
         moved_bytes=5000000,
-    )(jnp.reshape(jnp.where(core == 0, y, x) % 2, (1,)).astype(i32), *owned, sums)
+    )(*owned, sums)
     opposite = along_z(opposite, 4)
     swap = to_other_core(swap)
     pieces = [
@@ -690,7 +679,8 @@
         for s in range(3)
     ]
     pieces = [along_z(pieces[s - 1], -s) for s in (3, 2, 1)][::-1]
-    sums = butterfly(sums, lambda step, y, z, x, c: (y, z, x ^ step, c) if c == 0 else (y ^ step, z, x, c), NX)
+    sums = butterfly(sums, lambda step, y, z, x, c: (y ^ step, z, x, c), NY)
+    sums = butterfly(sums, lambda step, y, z, x, c: (y, z, x ^ step, c), NX)
 
     hold, send, sums = call(
         last_sum_kernel,

time: 238 us -> 228 us (0.958)
  starting transfers between devices: 84.1 us -> 76.3 us
  waiting for transfers between devices: 90.6 us -> 97.6 us
  local copies, waits for them, and re-layouts: 9.34 us -> 5.69 us
  Pallas kernels: 33.1 us -> 29.7 us
    ppermute x35 -> x37, starting transfers between devices: 84.1 us -> 76.3 us  [moved(): return lax.ppermute(value, ('nodes', 'rep'), pairs)]
    ppermute x35 -> x37, waiting for transfers between devices: 90.6 us -> 97.6 us  [moved(): return lax.ppermute(value, ('nodes', 'rep'), pairs)]
    unnamed x27 -> x22, local copies, waits for them, and re-layouts: 5.53 us -> 1.87 us
    pallas_call x2 -> x3, Pallas kernels: 8.45 us -> 7.71 us  [the longest x2 4.96 us: shards(): call(functools.partial(far_kernel, steps), struct((ROWS, BLK), kind), [VM...]
  transfers between devices with their start and end apart: 35 -> 37, of which waited for: 20 -> 20; matrix products, arithmetic and copies ran while one was open for 3% -> 3% of each run, Pallas kernels for 8% -> 8%
where the time goes in v1:
time: 228 us; the launch traced here: 226 us
  waiting for transfers between devices  97.6 us (43%)
  starting transfers between devices  76.3 us (33%)
  Pallas kernels  29.7 us (13%)
  between operations  14.7 us (6%)
  local copies, waits for them, and re-layouts  5.69 us (2%)
    ppermute x37, waiting for transfers between devices, moved(): return lax.ppermute(value, ('nodes', 'rep'), pairs)  97.6 us
    ppermute x37, starting transfers between devices, moved(): return lax.ppermute(value, ('nodes', 'rep'), pairs)  76.3 us
    pallas_call x1, Pallas kernels, shards(): call(plan_kernel, [struct((INFO,), i32)] + [struct((128,), i32)] * 3, [SM...  5.31 us
    pallas_call x2, Pallas kernels, shards(): call(functools.partial(far_kernel, steps), struct((ROWS, BLK), kind), [VM...  4.96 us
  transfers between devices with their start and end apart: 37, of which 20 were waited for; matrix products, arithmetic and copies ran while one was open for 3% of the time, Pallas kernels for 8%

profile of v1, /device:TPU:1, one launch (start us, length us, event | category | flops | bytes accessed | tf_op | source)
XLA Modules:
  0.0 226.5 jit_solution(2944215090682726762)
XLA Ops:
  8.5 3.2 %collective-permute-start = (s32[3,128]{1,0:T(4,128)S(1)}, s32[3,128]{1,0:T(4,128)S(1)}, u32[]{:S(2)}, u32[]{:S(2)}) collective-permute-start(s32[3,128]{1,0:T(4,128)S(1)} %pad_add_fusion.own_ref), channel_id=1, source_target_pairs={{0,1},{1,0},{2,3},{3,2},{4,5},{5,4},{6,7},{7,6},{8,9},{9,8},{10,11... | collective-permute-start | bytes 4616 | tf_op jit(solution)/shard_map/ppermute | solution.py:115
  13.7 4.4 %collective-permute-start.2 = (bf16[1040,128]{1,0:T(8,128)(2,1)S(1)}, bf16[1040,128]{1,0:T(8,128)(2,1)S(1)}, u32[]{:S(2)}, u32[]{:S(2)}) collective-permute-start(bf16[1040,128]{1,0:T(8,128)(2,1)S(1)} %get-tuple-element.107), channel_id=1, source_target_pairs={{0,16},{1,49},{2,18},{3,51},{4,20},{5,53},{6,22},{7,55},{8,24},{9,... | collective-permute-start | bytes 798728 | tf_op jit(solution)/shard_map/ppermute | solution.py:115
  18.9 5.3 %shard_map.111 = (s32[640]{0:T(1024)S(1)}, s32[128]{0:T(128)S(1)}, s32[128]{0:T(128)S(1)}, s32[128]{0:T(128)S(1)}) custom-call(s32[128]{0:T(128)S(1)} %get-tuple-element.202.code_ref, s32[128]{0:T(128)S(1)} %get-tuple-element.201.rows_ref), custom_call_target="tpu_custom_call" | custom-call | bytes 100000 | tf_op jit(solution)/shard_map/pallas_call | solution.py:559
  30.7 4.3 %collective-permute-done.3 = bf16[1040,128]{1,0:T(8,128)(2,1)S(1)} collective-permute-done((bf16[1040,128]{1,0:T(8,128)(2,1)S(1)}, bf16[1040,128]{1,0:T(8,128)(2,1)S(1)}, u32[]{:S(2)}, u32[]{:S(2)}) %collective-permute-start.3) | collective-permute-done | bytes 266272 | tf_op jit(solution)/shard_map/ppermute | solution.py:115
  44.0 2.8 %collective-permute-start.13 = (bf16[64,128,128]{2,1,0:T(8,128)(2,1)}, bf16[64,128,128]{2,1,0:T(8,128)(2,1)}, u32[]{:S(2)}, u32[]{:S(2)}) collective-permute-start(bf16[64,128,128]{2,1,0:T(8,128)(2,1)} %param.13), channel_id=1, source_target_pairs={{0,1},{1,0},{2,3},{3,2},{4,5},{5,4},{6,7},{7,6},{8,9},{9,8},{10,11... | collective-permute-start | bytes 6291464 | tf_op jit(solution)/shard_map/ppermute | solution.py:115
  46.8 20.9 %collective-permute-done.12.d_ref = bf16[4224,128]{1,0:T(8,128)(2,1)S(1)} collective-permute-done((bf16[4224,128]{1,0:T(8,128)(2,1)S(1)}, bf16[4224,128]{1,0:T(8,128)(2,1)S(1)}, u32[]{:S(2)}, u32[]{:S(2)}) %collective-permute-start.12) | collective-permute-done | bytes 1081376 | tf_op jit(solution)/shard_map/ppermute | solution.py:115
  69.5 4.3 %shard_map.114 = (bf16[3584,128]{1,0:T(8,128)(2,1)S(1)}, bf16[3584,128]{1,0:T(8,128)(2,1)S(1)}, bf16[3584,128]{1,0:T(8,128)(2,1)S(1)}) custom-call(bf16[4224,128]{1,0:T(8,128)(2,1)S(1)} %constant_dynamic-update-slice_fusion.a_ref, bf16[4224,128]{1,0:T(8,128)(2,1)} %collective-permute-done.10.b_ref, bf16[4224,128]{1,0:T(8,128)(2,1)S(1)} %collective-permute-done.11.c_ref, ...), custom_call_target="tpu_custom_call" | custom-call | bytes 7000000 | tf_op jit(solution)/shard_map/pallas_call | solution.py:583
  73.8 2.8 %collective-permute-start.14 = (bf16[3584,128]{1,0:T(8,128)(2,1)S(1)}, bf16[3584,128]{1,0:T(8,128)(2,1)S(1)}, u32[]{:S(2)}, u32[]{:S(2)}) collective-permute-start(bf16[3584,128]{1,0:T(8,128)(2,1)S(1)} %get-tuple-element.117), channel_id=1, source_target_pairs={{0,6},{1,193},{2,0},{3,195},{4,2},{5,197},{6,4},{7,199},{8,14},{9,... | collective-permute-start | bytes 2752520 | tf_op jit(solution)/shard_map/ppermute | solution.py:115
  82.2 3.1 %shard_map.113.near_ref = f32[512,128]{1,0:T(8,128)S(1)} custom-call(bf16[4224,128]{1,0:T(8,128)(2,1)S(1)} %constant_dynamic-update-slice_fusion.a_ref, bf16[4224,128]{1,0:T(8,128)(2,1)} %collective-permute-done.10.b_ref, bf16[4224,128]{1,0:T(8,128)(2,1)S(1)} %collective-permute-done.11.c_ref, bf16[4224,128]{1,0:T(8,128)(2,1)S(1)} %collective-permute-done.12.d_ref, ...), custom_call_target="tpu_custom_call" | custom-call | flops 67108864 | bytes 11000000 | tf_op jit(solution)/shard_map/pallas_call | solution.py:593
  85.3 11.5 %collective-permute-done.14.refs_0_ = bf16[3584,128]{1,0:T(8,128)(2,1)S(1)} collective-permute-done((bf16[3584,128]{1,0:T(8,128)(2,1)S(1)}, bf16[3584,128]{1,0:T(8,128)(2,1)S(1)}, u32[]{:S(2)}, u32[]{:S(2)}) %collective-permute-start.14) | collective-permute-done | bytes 917536 | tf_op jit(solution)/shard_map/ppermute | solution.py:115
  96.8 3.6 %collective-permute-done.15.refs_1_ = bf16[3584,128]{1,0:T(8,128)(2,1)S(1)} collective-permute-done((bf16[3584,128]{1,0:T(8,128)(2,1)S(1)}, bf16[3584,128]{1,0:T(8,128)(2,1)S(1)}, u32[]{:S(2)}, u32[]{:S(2)}) %collective-permute-start.15) | collective-permute-done | bytes 917536 | tf_op jit(solution)/shard_map/ppermute | solution.py:115
  100.4 3.2 %shard_map.115.near_ref = f32[512,128]{1,0:T(8,128)S(1)} custom-call(f32[512,128]{1,0:T(8,128)S(1)} %shard_map.113.near_ref, bf16[3584,128]{1,0:T(8,128)(2,1)S(1)} %collective-permute-done.14.refs_0_, bf16[3584,128]{1,0:T(8,128)(2,1)S(1)} %collective-permute-done.15.refs_1_, ...), custom_call_target="tpu_custom_call" | custom-call | flops 134217728 | bytes 7000000 | tf_op jit(solution)/shard_map/pallas_call | solution.py:609
  107.8 4.3 %shard_map.117 = (bf16[1024,128]{1,0:T(8,128)(2,1)}, f32[144,128]{1,0:T(8,128)S(1)}, bf16[512,128]{1,0:T(8,128)(2,1)S(1)}, bf16[3584,128]{1,0:T(8,128)(2,1)S(1)}) custom-call(s32[1]{0:T(128)} %bitcast.15.core_ref, bf16[512,128]{1,0:T(8,128)(2,1)S(1)} %shard_map.116.own_agg, bf16[512,128]{1,0:T(8,128)(2,1)S(1)} %collective-permute-done.17.other_agg, ...), custom_call_target="tpu_custom_call" | custom-call | flops 268435456 | bytes 8000000 | tf_op jit(solution)/shard_map/pallas_call | solution.py:620
  112.2 2.7 %collective-permute-start.19 = (bf16[3584,128]{1,0:T(8,128)(2,1)S(1)}, bf16[3584,128]{1,0:T(8,128)(2,1)S(1)}, u32[]{:S(2)}, u32[]{:S(2)}) collective-permute-start(bf16[3584,128]{1,0:T(8,128)(2,1)S(1)} %get-tuple-element.122), channel_id=1, source_target_pairs={{0,4},{1,129},{2,6},{3,131},{4,0},{5,133},{6,2},{7,135},{8,12},{9,... | collective-permute-start | bytes 2752520 | tf_op jit(solution)/shard_map/ppermute | solution.py:115
  125.5 5.4 %collective-permute-done.22 = f32[144,128]{1,0:T(8,128)S(1)} collective-permute-done((f32[144,128]{1,0:T(8,128)S(1)}, f32[144,128]{1,0:T(8,128)S(1)}, u32[]{:S(2)}, u32[]{:S(2)}) %collective-permute-start.22) | collective-permute-done | bytes 73760 | tf_op jit(solution)/shard_map/ppermute | solution.py:115
  130.9 4.9 %collective-permute-start.23 = (f32[144,128]{1,0:T(8,128)S(1)}, f32[144,128]{1,0:T(8,128)S(1)}, u32[]{:S(2)}, u32[]{:S(2)}) collective-permute-start(f32[144,128]{1,0:T(8,128)S(1)} %add.213), channel_id=1, source_target_pairs={{0,32},{1,33},{2,34},{3,35},{4,36},{5,37},{6,38},{7,39},{8,40},{9,... | collective-permute-start | bytes 221192 | tf_op jit(solution)/shard_map/ppermute | solution.py:115
  135.8 4.3 %collective-permute-done.23 = f32[144,128]{1,0:T(8,128)S(1)} collective-permute-done((f32[144,128]{1,0:T(8,128)S(1)}, f32[144,128]{1,0:T(8,128)S(1)}, u32[]{:S(2)}, u32[]{:S(2)}) %collective-permute-start.23) | collective-permute-done | bytes 73760 | tf_op jit(solution)/shard_map/ppermute | solution.py:115
  140.2 2.8 %shard_map.119 = (bf16[4096,128]{1,0:T(8,128)(2,1)S(1)}, bf16[4096,128]{1,0:T(8,128)(2,1)S(1)}, bf16[4096,128]{1,0:T(8,128)(2,1)S(1)}, bf16[4096,128]{1,0:T(8,128)(2,1)S(1)}) custom-call(s32[640]{0:T(1024)S(1)} %get-tuple-element.105.info_ref.refs_3_.refs_2_, s32[512]{0:T(512)S(1)} %reshape.149.table_ref, s32[128]{0:T(128)S(1)} %collective-permute-done.7.first_ref, ...), custom_call_target="tpu_custom_call" | custom-call | flops 67108864 | bytes 11000000 | tf_op jit(solution)/shard_map/pallas_call | solution.py:649
  145.7 23.7 %collective-permute-done.24.b_ref = bf16[4096,128]{1,0:T(8,128)(2,1)S(1)} collective-permute-done((bf16[4096,128]{1,0:T(8,128)(2,1)S(1)}, bf16[4096,128]{1,0:T(8,128)(2,1)S(1)}, u32[]{:S(2)}, u32[]{:S(2)}) %collective-permute-start.24) | collective-permute-done | bytes 1048608 | tf_op jit(solution)/shard_map/ppermute | solution.py:115
  174.2 15.9 %collective-permute-start.33 = (bf16[1024,128]{1,0:T(8,128)(2,1)S(1)}, bf16[1024,128]{1,0:T(8,128)(2,1)S(1)}, u32[]{:S(2)}, u32[]{:S(2)}) collective-permute-start(bf16[1024,128]{1,0:T(8,128)(2,1)S(1)} %pad_maximum_fusion.1), channel_id=1, source_target_pairs={{0,56},{1,9},{2,58},{3,11},{4,60},{5,13},{6,62},{7,15},{8,0},{9,17... | collective-permute-start | bytes 786440 | tf_op jit(solution)/shard_map/ppermute | solution.py:115
  191.2 3.3 %collective-permute-start.35 = (bf16[1024,128]{1,0:T(8,128)(2,1)S(1)}, bf16[1024,128]{1,0:T(8,128)(2,1)S(1)}, u32[]{:S(2)}, u32[]{:S(2)}) collective-permute-start(bf16[1024,128]{1,0:T(8,128)(2,1)S(1)} %pad_maximum_fusion.3), channel_id=1, source_target_pairs={{0,40},{1,25},{2,42},{3,27},{4,44},{5,29},{6,46},{7,31},{8,48},{9,... | collective-permute-start | bytes 786440 | tf_op jit(solution)/shard_map/ppermute | solution.py:115
  197.0 3.0 %collective-permute-done.28 = f32[144,128]{1,0:T(8,128)S(1)} collective-permute-done((f32[144,128]{1,0:T(8,128)S(1)}, f32[144,128]{1,0:T(8,128)S(1)}, u32[]{:S(2)}, u32[]{:S(2)}) %collective-permute-start.28) | collective-permute-done | bytes 73760 | tf_op jit(solution)/shard_map/ppermute | solution.py:115
  203.9 4.6 %collective-permute-done.30 = f32[144,128]{1,0:T(8,128)S(1)} collective-permute-done((f32[144,128]{1,0:T(8,128)S(1)}, f32[144,128]{1,0:T(8,128)S(1)}, u32[]{:S(2)}, u32[]{:S(2)}) %collective-permute-start.30) | collective-permute-done | bytes 73760 | tf_op jit(solution)/shard_map/ppermute | solution.py:115
  208.5 5.6 %collective-permute-done.31.far_ref = bf16[512,128]{1,0:T(8,128)(2,1)S(1)} collective-permute-done((bf16[512,128]{1,0:T(8,128)(2,1)S(1)}, bf16[512,128]{1,0:T(8,128)(2,1)S(1)}, u32[]{:S(2)}, u32[]{:S(2)}) %collective-permute-start.31) | collective-permute-done | bytes 131104 | tf_op jit(solution)/shard_map/ppermute | solution.py:115
  (120 shorter events, 62.0 us)
Async XLA Ops:
  13.7 15.6 %collective-permute-start.2 = (bf16[1040,128]{1,0:T(8,128)(2,1)S(1)}, bf16[1040,128]{1,0:T(8,128)(2,1)S(1)}, u32[]{:S(2)}, u32[]{:S(2)}) collective-permute-start(bf16[1040,128]{1,0:T(8,128)(2,1)S(1)} %get-tuple-element.107), channel_id=1, source_target_pairs={{0,16},{1,49},{2,18},{3,51},{4,20},{5,53},{6,22},{7,55},{8,24},{9,... | collective-permute-start | bytes 798728 | tf_op jit(solution)/shard_map/ppermute | solution.py:115
  18.1 11.3 %collective-permute-start.1 = (bf16[1040,128]{1,0:T(8,128)(2,1)S(1)}, bf16[1040,128]{1,0:T(8,128)(2,1)S(1)}, u32[]{:S(2)}, u32[]{:S(2)}) collective-permute-start(bf16[1040,128]{1,0:T(8,128)(2,1)S(1)} %get-tuple-element.107), channel_id=1, source_target_pairs={{0,8},{1,57},{2,10},{3,59},{4,12},{5,61},{6,14},{7,63},{8,16},{9,1... | collective-permute-start | bytes 798728 | tf_op jit(solution)/shard_map/ppermute | solution.py:115
  24.2 16.2 %collective-permute-start.7 = (s32[128]{0:T(128)S(1)}, s32[128]{0:T(128)S(1)}, u32[]{:S(2)}, u32[]{:S(2)}) collective-permute-start(s32[128]{0:T(128)S(1)} %get-tuple-element.110), channel_id=1, source_target_pairs={{0,2},{1,65},{2,4},{3,67},{4,6},{5,69},{6,0},{7,71},{8,10},{9,73},... | collective-permute-start | bytes 1544 | tf_op jit(solution)/shard_map/ppermute | solution.py:115
  25.6 14.8 %collective-permute-start.8 = (s32[128]{0:T(128)S(1)}, s32[128]{0:T(128)S(1)}, u32[]{:S(2)}, u32[]{:S(2)}) collective-permute-start(s32[128]{0:T(128)S(1)} %get-tuple-element.111), channel_id=1, source_target_pairs={{0,4},{1,129},{2,6},{3,131},{4,0},{5,133},{6,2},{7,135},{8,12},{9,... | collective-permute-start | bytes 1544 | tf_op jit(solution)/shard_map/ppermute | solution.py:115
  28.2 12.2 %collective-permute-start.9 = (s32[128]{0:T(128)S(1)}, s32[128]{0:T(128)S(1)}, u32[]{:S(2)}, u32[]{:S(2)}) collective-permute-start(s32[128]{0:T(128)S(1)} %get-tuple-element.112), channel_id=1, source_target_pairs={{0,6},{1,193},{2,0},{3,195},{4,2},{5,197},{6,4},{7,199},{8,14},{9,... | collective-permute-start | bytes 1544 | tf_op jit(solution)/shard_map/ppermute | solution.py:115
  40.5 27.2 %collective-permute-start.12 = (bf16[4224,128]{1,0:T(8,128)(2,1)S(1)}, bf16[4224,128]{1,0:T(8,128)(2,1)S(1)}, u32[]{:S(2)}, u32[]{:S(2)}) collective-permute-start(bf16[4224,128]{1,0:T(8,128)(2,1)S(1)} %constant_dynamic-update-slice_fusion.a_ref), channel_id=1, source_target_pairs={{0,64},{1,3},{2,66},{3,5},{4,68},{5,7},{6,70},{7,1},{8,72},{9,11},... | collective-permute-start | bytes 3244040 | tf_op jit(solution)/shard_map/ppermute | solution.py:115
  41.5 26.2 %collective-permute-start.11 = (bf16[4224,128]{1,0:T(8,128)(2,1)S(1)}, bf16[4224,128]{1,0:T(8,128)(2,1)S(1)}, u32[]{:S(2)}, u32[]{:S(2)}) collective-permute-start(bf16[4224,128]{1,0:T(8,128)(2,1)S(1)} %constant_dynamic-update-slice_fusion.a_ref), channel_id=1, source_target_pairs={{0,128},{1,5},{2,130},{3,7},{4,132},{5,1},{6,134},{7,3},{8,136},{9... | collective-permute-start | bytes 3244040 | tf_op jit(solution)/shard_map/ppermute | solution.py:115
  42.7 25.7 %collective-permute-start.10 = (bf16[4224,128]{1,0:T(8,128)(2,1)S(1)}, bf16[4224,128]{1,0:T(8,128)(2,1)}, u32[]{:S(2)}, u32[]{:S(2)}) collective-permute-start(bf16[4224,128]{1,0:T(8,128)(2,1)S(1)} %constant_dynamic-update-slice_fusion.a_ref), channel_id=1, source_target_pairs={{0,192},{1,7},{2,194},{3,1},{4,196},{5,3},{6,198},{7,5},{8,200},{9... | collective-permute-start | bytes 3244040 | tf_op jit(solution)/shard_map/ppermute | solution.py:115
  44.0 36.3 %collective-permute-start.13 = (bf16[64,128,128]{2,1,0:T(8,128)(2,1)}, bf16[64,128,128]{2,1,0:T(8,128)(2,1)}, u32[]{:S(2)}, u32[]{:S(2)}) collective-permute-start(bf16[64,128,128]{2,1,0:T(8,128)(2,1)} %param.13), channel_id=1, source_target_pairs={{0,1},{1,0},{2,3},{3,2},{4,5},{5,4},{6,7},{7,6},{8,9},{9,8},{10,11... | collective-permute-start | bytes 6291464 | tf_op jit(solution)/shard_map/ppermute | solution.py:115
  73.8 23.0 %collective-permute-start.14 = (bf16[3584,128]{1,0:T(8,128)(2,1)S(1)}, bf16[3584,128]{1,0:T(8,128)(2,1)S(1)}, u32[]{:S(2)}, u32[]{:S(2)}) collective-permute-start(bf16[3584,128]{1,0:T(8,128)(2,1)S(1)} %get-tuple-element.117), channel_id=1, source_target_pairs={{0,6},{1,193},{2,0},{3,195},{4,2},{5,197},{6,4},{7,199},{8,14},{9,... | collective-permute-start | bytes 2752520 | tf_op jit(solution)/shard_map/ppermute | solution.py:115
  76.6 23.8 %collective-permute-start.15 = (bf16[3584,128]{1,0:T(8,128)(2,1)S(1)}, bf16[3584,128]{1,0:T(8,128)(2,1)S(1)}, u32[]{:S(2)}, u32[]{:S(2)}) collective-permute-start(bf16[3584,128]{1,0:T(8,128)(2,1)S(1)} %get-tuple-element.118), channel_id=1, source_target_pairs={{0,2},{1,65},{2,4},{3,67},{4,6},{5,69},{6,0},{7,71},{8,10},{9,73},... | collective-permute-start | bytes 2752520 | tf_op jit(solution)/shard_map/ppermute | solution.py:115
  76.9 26.8 %collective-permute-start.16 = (bf16[3584,128]{1,0:T(8,128)(2,1)S(1)}, bf16[3584,128]{1,0:T(8,128)(2,1)S(1)}, u32[]{:S(2)}, u32[]{:S(2)}) collective-permute-start(bf16[3584,128]{1,0:T(8,128)(2,1)S(1)} %get-tuple-element.119), channel_id=1, source_target_pairs={{0,4},{1,129},{2,6},{3,131},{4,0},{5,133},{6,2},{7,135},{8,12},{9,... | collective-permute-start | bytes 2752520 | tf_op jit(solution)/shard_map/ppermute | solution.py:115
  112.2 28.0 %collective-permute-start.19 = (bf16[3584,128]{1,0:T(8,128)(2,1)S(1)}, bf16[3584,128]{1,0:T(8,128)(2,1)S(1)}, u32[]{:S(2)}, u32[]{:S(2)}) collective-permute-start(bf16[3584,128]{1,0:T(8,128)(2,1)S(1)} %get-tuple-element.122), channel_id=1, source_target_pairs={{0,4},{1,129},{2,6},{3,131},{4,0},{5,133},{6,2},{7,135},{8,12},{9,... | collective-permute-start | bytes 2752520 | tf_op jit(solution)/shard_map/ppermute | solution.py:115
  117.3 22.9 %collective-permute-start.18 = (bf16[3584,128]{1,0:T(8,128)(2,1)S(1)}, bf16[3584,128]{1,0:T(8,128)(2,1)S(1)}, u32[]{:S(2)}, u32[]{:S(2)}) collective-permute-start(bf16[3584,128]{1,0:T(8,128)(2,1)S(1)} %get-tuple-element.121), channel_id=1, source_target_pairs={{0,2},{1,65},{2,4},{3,67},{4,6},{5,69},{6,0},{7,71},{8,10},{9,73},... | collective-permute-start | bytes 2752520 | tf_op jit(solution)/shard_map/ppermute | solution.py:115
  117.4 22.8 %collective-permute-start.20 = (bf16[3584,128]{1,0:T(8,128)(2,1)S(1)}, bf16[3584,128]{1,0:T(8,128)(2,1)S(1)}, u32[]{:S(2)}, u32[]{:S(2)}) collective-permute-start(bf16[3584,128]{1,0:T(8,128)(2,1)S(1)} %get-tuple-element.123), channel_id=1, source_target_pairs={{0,6},{1,193},{2,0},{3,195},{4,2},{5,197},{6,4},{7,199},{8,14},{9,... | collective-permute-start | bytes 2752520 | tf_op jit(solution)/shard_map/ppermute | solution.py:115
  130.9 9.2 %collective-permute-start.23 = (f32[144,128]{1,0:T(8,128)S(1)}, f32[144,128]{1,0:T(8,128)S(1)}, u32[]{:S(2)}, u32[]{:S(2)}) collective-permute-start(f32[144,128]{1,0:T(8,128)S(1)} %add.213), channel_id=1, source_target_pairs={{0,32},{1,33},{2,34},{3,35},{4,36},{5,37},{6,38},{7,39},{8,40},{9,... | collective-permute-start | bytes 221192 | tf_op jit(solution)/shard_map/ppermute | solution.py:115
  142.9 26.5 %collective-permute-start.24 = (bf16[4096,128]{1,0:T(8,128)(2,1)S(1)}, bf16[4096,128]{1,0:T(8,128)(2,1)S(1)}, u32[]{:S(2)}, u32[]{:S(2)}) collective-permute-start(bf16[4096,128]{1,0:T(8,128)(2,1)S(1)} %get-tuple-element.126), channel_id=1, source_target_pairs={{0,64},{1,3},{2,66},{3,5},{4,68},{5,7},{6,70},{7,1},{8,72},{9,11},... | collective-permute-start | bytes 3145736 | tf_op jit(solution)/shard_map/ppermute | solution.py:115
  143.0 26.4 %collective-permute-start.25 = (bf16[4096,128]{1,0:T(8,128)(2,1)S(1)}, bf16[4096,128]{1,0:T(8,128)(2,1)S(1)}, u32[]{:S(2)}, u32[]{:S(2)}) collective-permute-start(bf16[4096,128]{1,0:T(8,128)(2,1)S(1)} %get-tuple-element.127), channel_id=1, source_target_pairs={{0,128},{1,5},{2,130},{3,7},{4,132},{5,1},{6,134},{7,3},{8,136},{9... | collective-permute-start | bytes 3145736 | tf_op jit(solution)/shard_map/ppermute | solution.py:115
  143.1 26.9 %collective-permute-start.26 = (bf16[4096,128]{1,0:T(8,128)(2,1)S(1)}, bf16[4096,128]{1,0:T(8,128)(2,1)S(1)}, u32[]{:S(2)}, u32[]{:S(2)}) collective-permute-start(bf16[4096,128]{1,0:T(8,128)(2,1)S(1)} %get-tuple-element.128), channel_id=1, source_target_pairs={{0,192},{1,7},{2,194},{3,1},{4,196},{5,3},{6,198},{7,5},{8,200},{9... | collective-permute-start | bytes 3145736 | tf_op jit(solution)/shard_map/ppermute | solution.py:115
  172.8 21.7 %collective-permute-start.27 = (f32[144,128]{1,0:T(8,128)S(1)}, f32[144,128]{1,0:T(8,128)S(1)}, u32[]{:S(2)}, u32[]{:S(2)}) collective-permute-start(f32[144,128]{1,0:T(8,128)S(1)} %get-tuple-element.129), channel_id=1, source_target_pairs={{0,64},{1,65},{2,66},{3,67},{4,68},{5,69},{6,70},{7,71},{8,72},{9,... | collective-permute-start | bytes 221192 | tf_op jit(solution)/shard_map/ppermute | solution.py:115
  174.2 39.9 %collective-permute-start.33 = (bf16[1024,128]{1,0:T(8,128)(2,1)S(1)}, bf16[1024,128]{1,0:T(8,128)(2,1)S(1)}, u32[]{:S(2)}, u32[]{:S(2)}) collective-permute-start(bf16[1024,128]{1,0:T(8,128)(2,1)S(1)} %pad_maximum_fusion.1), channel_id=1, source_target_pairs={{0,56},{1,9},{2,58},{3,11},{4,60},{5,13},{6,62},{7,15},{8,0},{9,17... | collective-permute-start | bytes 786440 | tf_op jit(solution)/shard_map/ppermute | solution.py:115
  190.2 23.9 %collective-permute-start.34 = (bf16[1024,128]{1,0:T(8,128)(2,1)S(1)}, bf16[1024,128]{1,0:T(8,128)(2,1)S(1)}, u32[]{:S(2)}, u32[]{:S(2)}) collective-permute-start(bf16[1024,128]{1,0:T(8,128)(2,1)S(1)} %pad_maximum_fusion.2), channel_id=1, source_target_pairs={{0,48},{1,17},{2,50},{3,19},{4,52},{5,21},{6,54},{7,23},{8,56},{9,... | collective-permute-start | bytes 786440 | tf_op jit(solution)/shard_map/ppermute | solution.py:115
  191.2 22.9 %collective-permute-start.35 = (bf16[1024,128]{1,0:T(8,128)(2,1)S(1)}, bf16[1024,128]{1,0:T(8,128)(2,1)S(1)}, u32[]{:S(2)}, u32[]{:S(2)}) collective-permute-start(bf16[1024,128]{1,0:T(8,128)(2,1)S(1)} %pad_maximum_fusion.3), channel_id=1, source_target_pairs={{0,40},{1,25},{2,42},{3,27},{4,44},{5,29},{6,46},{7,31},{8,48},{9,... | collective-permute-start | bytes 786440 | tf_op jit(solution)/shard_map/ppermute | solution.py:115
  200.0 14.1 %collective-permute-start.31 = (bf16[512,128]{1,0:T(8,128)(2,1)S(1)}, bf16[512,128]{1,0:T(8,128)(2,1)S(1)}, u32[]{:S(2)}, u32[]{:S(2)}) collective-permute-start(bf16[512,128]{1,0:T(8,128)(2,1)S(1)} %get-tuple-element.131), channel_id=1, source_target_pairs={{0,32},{1,33},{2,34},{3,35},{4,36},{5,37},{6,38},{7,39},{8,40},{9,... | collective-permute-start | bytes 393224 | tf_op jit(solution)/shard_map/ppermute | solution.py:115
  (20 other events, 249.0 us)

commit v2 on v1

--- a/solution.py
+++ b/solution.py
@@ -265,9 +265,9 @@
     for k, (req, out) in enumerate(((q1, o1), (q2, o2), (q3, o3))):
 
         def body(i, carry, req=req, out=out, k=k):
+            blocks = [local_block(parts, req[i * 8 + u], table, k + 1) for u in range(8)]
             for u in range(8):
-                p = i * 8 + u
-                out[half_rows(p), :] = local_block(parts, req[p], table, k + 1)
+                out[half_rows(i * 8 + u), :] = blocks[u]
             return carry
 
         lax.fori_loop(0, CAP // 8, body, 0)
@@ -336,13 +336,13 @@
     first = REM0 + (step - 1) * CAP
 
     def body(i, carry):
+        done = []
         for u in range(8):
-            p = i * 8 + u
-            t = info[first + p]
+            t = info[first + i * 8 + u]
             left = turned_ref[half_rows(info[ROW0 + t]), :]
-            out[half_rows(p), :] = jnp.dot(
-                left, tiles[t], preferred_element_type=jnp.float32
-            ).astype(jnp.bfloat16)
+            done.append(jnp.dot(left, tiles[t], preferred_element_type=jnp.float32))
+        for u in range(8):
+            out[half_rows(i * 8 + u), :] = done[u].astype(jnp.bfloat16)
         return carry
 
     lax.fori_loop(0, (info[CNT0 + step] + 7) >> 3, body, 0)
@@ -466,8 +466,13 @@
             swap_ref[(m - 5) * ROWS : (m - 4) * ROWS, :] = value
 
 
+def keep_sum_kernel(keep_ref, far_ref, sums_ref, out_ref, passed_ref):
+    out_ref[...] = keep_ref[...].astype(jnp.float32) + far_ref[...].astype(jnp.float32)
+    passed_ref[...] = sums_ref[...]
+
+
 def last_sum_kernel(
-    core_ref, sums_ref, keep_ref, far_ref, a_ref, b_ref, c_ref, hold_ref, send_ref, passed_ref
+    core_ref, sums_ref, keep_ref, a_ref, b_ref, c_ref, hold_ref, send_ref, passed_ref
 ):
     passed_ref[...] = sums_ref[...]
     core = core_ref[0]
@@ -478,7 +483,7 @@
         value = a_ref[at, :].astype(jnp.float32) + b_ref[at, :].astype(jnp.float32)
         value = value + c_ref[at, :].astype(jnp.float32)
         if first < ROWS:
-            value = value + keep_ref[at, :].astype(jnp.float32) + far_ref[at, :].astype(jnp.float32)
+            value = value + keep_ref[at, :]
         return value
 
     for n in range(2):
@@ -520,9 +525,9 @@
     core_array = jnp.reshape(core, (1,)).astype(i32)
     dma = pltpu.SemaphoreType.DMA
 
-    local_rows = block_row - node * NB
-    packed = jnp.pad(tile_slot * NB + local_rows, (0, BLK - 64))
-    own_meta = jnp.concatenate([packed[None, :], send_list.T], axis=0)
+    own_meta = jnp.concatenate(
+        [jnp.concatenate([tile_slot, block_row])[None, :], send_list.T], axis=0
+    )
     other_meta = to_other_core(own_meta)
     tiles = jnp.concatenate([edge_tiles, to_other_core(edge_tiles)], axis=0)
 
@@ -543,9 +548,8 @@
         column += [piece[MSG - ROWS :], piece[: MSG - ROWS]]
     column = jnp.concatenate(column, axis=0)
 
-    both = jnp.concatenate([own_meta[0, :64], other_meta[0, :64]])
-    rows = both % NB
-    slot = both // NB
+    slot = jnp.concatenate([own_meta[0, :64], other_meta[0, :64]])
+    rows = jnp.concatenate([own_meta[0, 64:], other_meta[0, 64:]]) - node * NB
     source, which = slot // 2, slot % 2
     step_y = (source // (NZ * NX) - y) % NY
     step_z = (source // NX - z) % NZ
@@ -680,15 +684,22 @@
     ]
     pieces = [along_z(pieces[s - 1], -s) for s in (3, 2, 1)][::-1]
     sums = butterfly(sums, lambda step, y, z, x, c: (y ^ step, z, x, c), NY)
+    keep, sums = call(
+        keep_sum_kernel,
+        [struct((ROWS, BLK), f32), struct((SUMS, BLK), f32)],
+        [VMEM] * 3,
+        [VMEM] * 2,
+        moved_bytes=500000,
+    )(keep, opposite, sums)
     sums = butterfly(sums, lambda step, y, z, x, c: (y, z, x ^ step, c), NX)
 
     hold, send, sums = call(
         last_sum_kernel,
         [struct((ROWS, BLK), f32)] * 2 + [struct((SUMS, BLK), f32)],
-        [SMEM] + [VMEM] * 6,
+        [SMEM] + [VMEM] * 5,
         [VMEM] * 3,
         moved_bytes=1500000,
-    )(core_array, sums, keep, opposite, *pieces)
+    )(core_array, sums, keep, *pieces)
     feature_grad, weight_grad, bias_grad = call(
         turn_kernel,
         [struct((NB // 2 * BLK, BLK), f32), struct((BLK, BLK), f32), struct((1, BLK), f32)],

time: 228 us -> 228 us (level)
  transfers between devices with their start and end apart: 37 -> 37, of which waited for: 20 -> 19; matrix products, arithmetic and copies ran while one was open for 3% -> 3% of each run, Pallas kernels for 8% -> 8%
where the time goes in v2:
time: 228 us; the launch traced here: 226 us
  waiting for transfers between devices  96.1 us (42%)
  starting transfers between devices  77.3 us (34%)
  Pallas kernels  29.7 us (13%)
  between operations  14.7 us (6%)
  local copies, waits for them, and re-layouts  5.81 us (3%)
    ppermute x37, waiting for transfers between devices, moved(): return lax.ppermute(value, ('nodes', 'rep'), pairs)  96.1 us
    ppermute x37, starting transfers between devices, moved(): return lax.ppermute(value, ('nodes', 'rep'), pairs)  77.3 us
    pallas_call x1, Pallas kernels, shards(): call(plan_kernel, [struct((INFO,), i32)] + [struct((128,), i32)] * 3, [SM...  5.31 us
    pallas_call x2, Pallas kernels, shards(): call(functools.partial(far_kernel, steps), struct((ROWS, BLK), kind), [VM...  4.67 us
  transfers between devices with their start and end apart: 37, of which 19 were waited for; matrix products, arithmetic and copies ran while one was open for 3% of the time, Pallas kernels for 8%

profile of v2, /device:TPU:1, one launch (start us, length us, event | category | flops | bytes accessed | tf_op | source)
XLA Modules:
  0.0 226.2 jit_solution(2636428518014734800)
XLA Ops:
  8.6 3.2 %collective-permute-start = (s32[3,128]{1,0:T(4,128)S(1)}, s32[3,128]{1,0:T(4,128)S(1)}, u32[]{:S(2)}, u32[]{:S(2)}) collective-permute-start(s32[3,128]{1,0:T(4,128)S(1)} %pad_add_fusion.own_ref), channel_id=1, source_target_pairs={{0,1},{1,0},{2,3},{3,2},{4,5},{5,4},{6,7},{7,6},{8,9},{9,8},{10,11... | collective-permute-start | bytes 4616 | tf_op jit(solution)/shard_map/ppermute | solution.py:115
  13.8 4.4 %collective-permute-start.2 = (bf16[1040,128]{1,0:T(8,128)(2,1)S(1)}, bf16[1040,128]{1,0:T(8,128)(2,1)S(1)}, u32[]{:S(2)}, u32[]{:S(2)}) collective-permute-start(bf16[1040,128]{1,0:T(8,128)(2,1)S(1)} %get-tuple-element.109), channel_id=1, source_target_pairs={{0,16},{1,49},{2,18},{3,51},{4,20},{5,53},{6,22},{7,55},{8,24},{9,... | collective-permute-start | bytes 798728 | tf_op jit(solution)/shard_map/ppermute | solution.py:115
  19.1 5.3 %shard_map.111 = (s32[640]{0:T(1024)S(1)}, s32[128]{0:T(128)S(1)}, s32[128]{0:T(128)S(1)}, s32[128]{0:T(128)S(1)}) custom-call(s32[128]{0:T(128)S(1)} %fusion.20.code_ref, s32[128]{0:T(128)S(1)} %add_subtract_fusion.rows_ref), custom_call_target="tpu_custom_call" | custom-call | bytes 100000 | tf_op jit(solution)/shard_map/pallas_call | solution.py:563
  30.8 4.4 %collective-permute-done.3 = bf16[1040,128]{1,0:T(8,128)(2,1)S(1)} collective-permute-done((bf16[1040,128]{1,0:T(8,128)(2,1)S(1)}, bf16[1040,128]{1,0:T(8,128)(2,1)S(1)}, u32[]{:S(2)}, u32[]{:S(2)}) %collective-permute-start.3) | collective-permute-done | bytes 266272 | tf_op jit(solution)/shard_map/ppermute | solution.py:115
  44.2 2.8 %collective-permute-start.13 = (bf16[64,128,128]{2,1,0:T(8,128)(2,1)}, bf16[64,128,128]{2,1,0:T(8,128)(2,1)}, u32[]{:S(2)}, u32[]{:S(2)}) collective-permute-start(bf16[64,128,128]{2,1,0:T(8,128)(2,1)} %param.13), channel_id=1, source_target_pairs={{0,1},{1,0},{2,3},{3,2},{4,5},{5,4},{6,7},{7,6},{8,9},{9,8},{10,11... | collective-permute-start | bytes 6291464 | tf_op jit(solution)/shard_map/ppermute | solution.py:115
  47.0 20.9 %collective-permute-done.12.d_ref = bf16[4224,128]{1,0:T(8,128)(2,1)S(1)} collective-permute-done((bf16[4224,128]{1,0:T(8,128)(2,1)S(1)}, bf16[4224,128]{1,0:T(8,128)(2,1)S(1)}, u32[]{:S(2)}, u32[]{:S(2)}) %collective-permute-start.12) | collective-permute-done | bytes 1081376 | tf_op jit(solution)/shard_map/ppermute | solution.py:115
  69.7 4.2 %shard_map.114 = (bf16[3584,128]{1,0:T(8,128)(2,1)S(1)}, bf16[3584,128]{1,0:T(8,128)(2,1)S(1)}, bf16[3584,128]{1,0:T(8,128)(2,1)S(1)}) custom-call(bf16[4224,128]{1,0:T(8,128)(2,1)S(1)} %constant_dynamic-update-slice_fusion.a_ref, bf16[4224,128]{1,0:T(8,128)(2,1)} %collective-permute-done.10.b_ref, bf16[4224,128]{1,0:T(8,128)(2,1)S(1)} %collective-permute-done.11.c_ref, ...), custom_call_target="tpu_custom_call" | custom-call | bytes 7000000 | tf_op jit(solution)/shard_map/pallas_call | solution.py:587
  73.9 2.8 %collective-permute-start.14 = (bf16[3584,128]{1,0:T(8,128)(2,1)S(1)}, bf16[3584,128]{1,0:T(8,128)(2,1)S(1)}, u32[]{:S(2)}, u32[]{:S(2)}) collective-permute-start(bf16[3584,128]{1,0:T(8,128)(2,1)S(1)} %get-tuple-element.119), channel_id=1, source_target_pairs={{0,6},{1,193},{2,0},{3,195},{4,2},{5,197},{6,4},{7,199},{8,14},{9,... | collective-permute-start | bytes 2752520 | tf_op jit(solution)/shard_map/ppermute | solution.py:115
  82.3 3.4 %shard_map.113.near_ref = f32[512,128]{1,0:T(8,128)S(1)} custom-call(bf16[4224,128]{1,0:T(8,128)(2,1)S(1)} %constant_dynamic-update-slice_fusion.a_ref, bf16[4224,128]{1,0:T(8,128)(2,1)} %collective-permute-done.10.b_ref, bf16[4224,128]{1,0:T(8,128)(2,1)S(1)} %collective-permute-done.11.c_ref, bf16[4224,128]{1,0:T(8,128)(2,1)S(1)} %collective-permute-done.12.d_ref, ...), custom_call_target="tpu_custom_call" | custom-call | flops 67108864 | bytes 11000000 | tf_op jit(solution)/shard_map/pallas_call | solution.py:597
  85.7 11.2 %collective-permute-done.14.refs_0_ = bf16[3584,128]{1,0:T(8,128)(2,1)S(1)} collective-permute-done((bf16[3584,128]{1,0:T(8,128)(2,1)S(1)}, bf16[3584,128]{1,0:T(8,128)(2,1)S(1)}, u32[]{:S(2)}, u32[]{:S(2)}) %collective-permute-start.14) | collective-permute-done | bytes 917536 | tf_op jit(solution)/shard_map/ppermute | solution.py:115
  96.9 3.6 %collective-permute-done.15.refs_1_ = bf16[3584,128]{1,0:T(8,128)(2,1)S(1)} collective-permute-done((bf16[3584,128]{1,0:T(8,128)(2,1)S(1)}, bf16[3584,128]{1,0:T(8,128)(2,1)S(1)}, u32[]{:S(2)}, u32[]{:S(2)}) %collective-permute-start.15) | collective-permute-done | bytes 917536 | tf_op jit(solution)/shard_map/ppermute | solution.py:115
  100.5 2.9 %shard_map.115.near_ref = f32[512,128]{1,0:T(8,128)S(1)} custom-call(f32[512,128]{1,0:T(8,128)S(1)} %shard_map.113.near_ref, bf16[3584,128]{1,0:T(8,128)(2,1)S(1)} %collective-permute-done.14.refs_0_, bf16[3584,128]{1,0:T(8,128)(2,1)S(1)} %collective-permute-done.15.refs_1_, ...), custom_call_target="tpu_custom_call" | custom-call | flops 134217728 | bytes 7000000 | tf_op jit(solution)/shard_map/pallas_call | solution.py:613
  107.8 4.3 %shard_map.117 = (bf16[1024,128]{1,0:T(8,128)(2,1)}, f32[144,128]{1,0:T(8,128)S(1)}, bf16[512,128]{1,0:T(8,128)(2,1)S(1)}, bf16[3584,128]{1,0:T(8,128)(2,1)S(1)}) custom-call(s32[1]{0:T(128)} %bitcast.15.core_ref, bf16[512,128]{1,0:T(8,128)(2,1)S(1)} %shard_map.116.own_agg, bf16[512,128]{1,0:T(8,128)(2,1)S(1)} %collective-permute-done.17.other_agg, ...), custom_call_target="tpu_custom_call" | custom-call | flops 268435456 | bytes 8000000 | tf_op jit(solution)/shard_map/pallas_call | solution.py:624
  112.1 3.0 %collective-permute-start.19 = (bf16[3584,128]{1,0:T(8,128)(2,1)S(1)}, bf16[3584,128]{1,0:T(8,128)(2,1)S(1)}, u32[]{:S(2)}, u32[]{:S(2)}) collective-permute-start(bf16[3584,128]{1,0:T(8,128)(2,1)S(1)} %get-tuple-element.124), channel_id=1, source_target_pairs={{0,4},{1,129},{2,6},{3,131},{4,0},{5,133},{6,2},{7,135},{8,12},{9,... | collective-permute-start | bytes 2752520 | tf_op jit(solution)/shard_map/ppermute | solution.py:115
  125.6 5.4 %collective-permute-done.22 = f32[144,128]{1,0:T(8,128)S(1)} collective-permute-done((f32[144,128]{1,0:T(8,128)S(1)}, f32[144,128]{1,0:T(8,128)S(1)}, u32[]{:S(2)}, u32[]{:S(2)}) %collective-permute-start.22) | collective-permute-done | bytes 73760 | tf_op jit(solution)/shard_map/ppermute | solution.py:115
  131.0 4.5 %collective-permute-start.23 = (f32[144,128]{1,0:T(8,128)S(1)}, f32[144,128]{1,0:T(8,128)S(1)}, u32[]{:S(2)}, u32[]{:S(2)}) collective-permute-start(f32[144,128]{1,0:T(8,128)S(1)} %add.201), channel_id=1, source_target_pairs={{0,32},{1,33},{2,34},{3,35},{4,36},{5,37},{6,38},{7,39},{8,40},{9,... | collective-permute-start | bytes 221192 | tf_op jit(solution)/shard_map/ppermute | solution.py:115
  135.5 4.2 %collective-permute-done.23 = f32[144,128]{1,0:T(8,128)S(1)} collective-permute-done((f32[144,128]{1,0:T(8,128)S(1)}, f32[144,128]{1,0:T(8,128)S(1)}, u32[]{:S(2)}, u32[]{:S(2)}) %collective-permute-start.23) | collective-permute-done | bytes 73760 | tf_op jit(solution)/shard_map/ppermute | solution.py:115
  139.8 3.0 %shard_map.119 = (bf16[4096,128]{1,0:T(8,128)(2,1)S(1)}, bf16[4096,128]{1,0:T(8,128)(2,1)S(1)}, bf16[4096,128]{1,0:T(8,128)(2,1)S(1)}, bf16[4096,128]{1,0:T(8,128)(2,1)S(1)}) custom-call(s32[640]{0:T(1024)S(1)} %get-tuple-element.107.info_ref.refs_3_.refs_2_, s32[512]{0:T(512)S(1)} %reshape.149.table_ref, s32[128]{0:T(128)S(1)} %collective-permute-done.7.first_ref, ...), custom_call_target="tpu_custom_call" | custom-call | flops 67108864 | bytes 11000000 | tf_op jit(solution)/shard_map/pallas_call | solution.py:653
  145.6 23.7 %collective-permute-done.24.b_ref = bf16[4096,128]{1,0:T(8,128)(2,1)S(1)} collective-permute-done((bf16[4096,128]{1,0:T(8,128)(2,1)S(1)}, bf16[4096,128]{1,0:T(8,128)(2,1)S(1)}, u32[]{:S(2)}, u32[]{:S(2)}) %collective-permute-start.24) | collective-permute-done | bytes 1048608 | tf_op jit(solution)/shard_map/ppermute | solution.py:115
  170.9 20.6 %collective-permute-start.27 = (bf16[512,128]{1,0:T(8,128)(2,1)S(1)}, bf16[512,128]{1,0:T(8,128)(2,1)S(1)}, u32[]{:S(2)}, u32[]{:S(2)}) collective-permute-start(bf16[512,128]{1,0:T(8,128)(2,1)S(1)} %get-tuple-element.132), channel_id=1, source_target_pairs={{0,32},{1,33},{2,34},{3,35},{4,36},{5,37},{6,38},{7,39},{8,40},{9,... | collective-permute-start | bytes 393224 | tf_op jit(solution)/shard_map/ppermute | solution.py:115
  194.7 3.3 %collective-permute-start.29 = (f32[144,128]{1,0:T(8,128)S(1)}, f32[144,128]{1,0:T(8,128)S(1)}, u32[]{:S(2)}, u32[]{:S(2)}) collective-permute-start(f32[144,128]{1,0:T(8,128)S(1)} %add.203), channel_id=1, source_target_pairs={{0,128},{1,129},{2,130},{3,131},{4,132},{5,133},{6,134},{7,135},{8... | collective-permute-start | bytes 221192 | tf_op jit(solution)/shard_map/ppermute | solution.py:115
  200.0 3.5 %collective-permute-done.30 = f32[144,128]{1,0:T(8,128)S(1)} collective-permute-done((f32[144,128]{1,0:T(8,128)S(1)}, f32[144,128]{1,0:T(8,128)S(1)}, u32[]{:S(2)}, u32[]{:S(2)}) %collective-permute-start.30) | collective-permute-done | bytes 73760 | tf_op jit(solution)/shard_map/ppermute | solution.py:115
  204.4 4.0 %collective-permute-done.31 = f32[144,128]{1,0:T(8,128)S(1)} collective-permute-done((f32[144,128]{1,0:T(8,128)S(1)}, f32[144,128]{1,0:T(8,128)S(1)}, u32[]{:S(2)}, u32[]{:S(2)}) %collective-permute-start.31) | collective-permute-done | bytes 73760 | tf_op jit(solution)/shard_map/ppermute | solution.py:115
  208.5 6.9 %collective-permute-done.35.c_ref = bf16[1024,128]{1,0:T(8,128)(2,1)S(1)} collective-permute-done((bf16[1024,128]{1,0:T(8,128)(2,1)S(1)}, bf16[1024,128]{1,0:T(8,128)(2,1)S(1)}, u32[]{:S(2)}, u32[]{:S(2)}) %collective-permute-start.35) | collective-permute-done | bytes 262176 | tf_op jit(solution)/shard_map/ppermute | solution.py:115
  (121 shorter events, 56.0 us)
Async XLA Ops:
  13.8 15.8 %collective-permute-start.2 = (bf16[1040,128]{1,0:T(8,128)(2,1)S(1)}, bf16[1040,128]{1,0:T(8,128)(2,1)S(1)}, u32[]{:S(2)}, u32[]{:S(2)}) collective-permute-start(bf16[1040,128]{1,0:T(8,128)(2,1)S(1)} %get-tuple-element.109), channel_id=1, source_target_pairs={{0,16},{1,49},{2,18},{3,51},{4,20},{5,53},{6,22},{7,55},{8,24},{9,... | collective-permute-start | bytes 798728 | tf_op jit(solution)/shard_map/ppermute | solution.py:115
  18.1 11.4 %collective-permute-start.1 = (bf16[1040,128]{1,0:T(8,128)(2,1)S(1)}, bf16[1040,128]{1,0:T(8,128)(2,1)S(1)}, u32[]{:S(2)}, u32[]{:S(2)}) collective-permute-start(bf16[1040,128]{1,0:T(8,128)(2,1)S(1)} %get-tuple-element.109), channel_id=1, source_target_pairs={{0,8},{1,57},{2,10},{3,59},{4,12},{5,61},{6,14},{7,63},{8,16},{9,1... | collective-permute-start | bytes 798728 | tf_op jit(solution)/shard_map/ppermute | solution.py:115
  24.4 16.2 %collective-permute-start.7 = (s32[128]{0:T(128)S(1)}, s32[128]{0:T(128)S(1)}, u32[]{:S(2)}, u32[]{:S(2)}) collective-permute-start(s32[128]{0:T(128)S(1)} %get-tuple-element.112), channel_id=1, source_target_pairs={{0,2},{1,65},{2,4},{3,67},{4,6},{5,69},{6,0},{7,71},{8,10},{9,73},... | collective-permute-start | bytes 1544 | tf_op jit(solution)/shard_map/ppermute | solution.py:115
  25.8 14.8 %collective-permute-start.8 = (s32[128]{0:T(128)S(1)}, s32[128]{0:T(128)S(1)}, u32[]{:S(2)}, u32[]{:S(2)}) collective-permute-start(s32[128]{0:T(128)S(1)} %get-tuple-element.113), channel_id=1, source_target_pairs={{0,4},{1,129},{2,6},{3,131},{4,0},{5,133},{6,2},{7,135},{8,12},{9,... | collective-permute-start | bytes 1544 | tf_op jit(solution)/shard_map/ppermute | solution.py:115
  28.4 12.2 %collective-permute-start.9 = (s32[128]{0:T(128)S(1)}, s32[128]{0:T(128)S(1)}, u32[]{:S(2)}, u32[]{:S(2)}) collective-permute-start(s32[128]{0:T(128)S(1)} %get-tuple-element.114), channel_id=1, source_target_pairs={{0,6},{1,193},{2,0},{3,195},{4,2},{5,197},{6,4},{7,199},{8,14},{9,... | collective-permute-start | bytes 1544 | tf_op jit(solution)/shard_map/ppermute | solution.py:115
  40.7 27.2 %collective-permute-start.12 = (bf16[4224,128]{1,0:T(8,128)(2,1)S(1)}, bf16[4224,128]{1,0:T(8,128)(2,1)S(1)}, u32[]{:S(2)}, u32[]{:S(2)}) collective-permute-start(bf16[4224,128]{1,0:T(8,128)(2,1)S(1)} %constant_dynamic-update-slice_fusion.a_ref), channel_id=1, source_target_pairs={{0,64},{1,3},{2,66},{3,5},{4,68},{5,7},{6,70},{7,1},{8,72},{9,11},... | collective-permute-start | bytes 3244040 | tf_op jit(solution)/shard_map/ppermute | solution.py:115
  41.7 26.2 %collective-permute-start.11 = (bf16[4224,128]{1,0:T(8,128)(2,1)S(1)}, bf16[4224,128]{1,0:T(8,128)(2,1)S(1)}, u32[]{:S(2)}, u32[]{:S(2)}) collective-permute-start(bf16[4224,128]{1,0:T(8,128)(2,1)S(1)} %constant_dynamic-update-slice_fusion.a_ref), channel_id=1, source_target_pairs={{0,128},{1,5},{2,130},{3,7},{4,132},{5,1},{6,134},{7,3},{8,136},{9... | collective-permute-start | bytes 3244040 | tf_op jit(solution)/shard_map/ppermute | solution.py:115
  42.8 25.8 %collective-permute-start.10 = (bf16[4224,128]{1,0:T(8,128)(2,1)S(1)}, bf16[4224,128]{1,0:T(8,128)(2,1)}, u32[]{:S(2)}, u32[]{:S(2)}) collective-permute-start(bf16[4224,128]{1,0:T(8,128)(2,1)S(1)} %constant_dynamic-update-slice_fusion.a_ref), channel_id=1, source_target_pairs={{0,192},{1,7},{2,194},{3,1},{4,196},{5,3},{6,198},{7,5},{8,200},{9... | collective-permute-start | bytes 3244040 | tf_op jit(solution)/shard_map/ppermute | solution.py:115
  44.2 36.2 %collective-permute-start.13 = (bf16[64,128,128]{2,1,0:T(8,128)(2,1)}, bf16[64,128,128]{2,1,0:T(8,128)(2,1)}, u32[]{:S(2)}, u32[]{:S(2)}) collective-permute-start(bf16[64,128,128]{2,1,0:T(8,128)(2,1)} %param.13), channel_id=1, source_target_pairs={{0,1},{1,0},{2,3},{3,2},{4,5},{5,4},{6,7},{7,6},{8,9},{9,8},{10,11... | collective-permute-start | bytes 6291464 | tf_op jit(solution)/shard_map/ppermute | solution.py:115
  73.9 23.0 %collective-permute-start.14 = (bf16[3584,128]{1,0:T(8,128)(2,1)S(1)}, bf16[3584,128]{1,0:T(8,128)(2,1)S(1)}, u32[]{:S(2)}, u32[]{:S(2)}) collective-permute-start(bf16[3584,128]{1,0:T(8,128)(2,1)S(1)} %get-tuple-element.119), channel_id=1, source_target_pairs={{0,6},{1,193},{2,0},{3,195},{4,2},{5,197},{6,4},{7,199},{8,14},{9,... | collective-permute-start | bytes 2752520 | tf_op jit(solution)/shard_map/ppermute | solution.py:115
  76.7 23.8 %collective-permute-start.15 = (bf16[3584,128]{1,0:T(8,128)(2,1)S(1)}, bf16[3584,128]{1,0:T(8,128)(2,1)S(1)}, u32[]{:S(2)}, u32[]{:S(2)}) collective-permute-start(bf16[3584,128]{1,0:T(8,128)(2,1)S(1)} %get-tuple-element.120), channel_id=1, source_target_pairs={{0,2},{1,65},{2,4},{3,67},{4,6},{5,69},{6,0},{7,71},{8,10},{9,73},... | collective-permute-start | bytes 2752520 | tf_op jit(solution)/shard_map/ppermute | solution.py:115
  77.0 26.5 %collective-permute-start.16 = (bf16[3584,128]{1,0:T(8,128)(2,1)S(1)}, bf16[3584,128]{1,0:T(8,128)(2,1)S(1)}, u32[]{:S(2)}, u32[]{:S(2)}) collective-permute-start(bf16[3584,128]{1,0:T(8,128)(2,1)S(1)} %get-tuple-element.121), channel_id=1, source_target_pairs={{0,4},{1,129},{2,6},{3,131},{4,0},{5,133},{6,2},{7,135},{8,12},{9,... | collective-permute-start | bytes 2752520 | tf_op jit(solution)/shard_map/ppermute | solution.py:115
  112.1 27.7 %collective-permute-start.19 = (bf16[3584,128]{1,0:T(8,128)(2,1)S(1)}, bf16[3584,128]{1,0:T(8,128)(2,1)S(1)}, u32[]{:S(2)}, u32[]{:S(2)}) collective-permute-start(bf16[3584,128]{1,0:T(8,128)(2,1)S(1)} %get-tuple-element.124), channel_id=1, source_target_pairs={{0,4},{1,129},{2,6},{3,131},{4,0},{5,133},{6,2},{7,135},{8,12},{9,... | collective-permute-start | bytes 2752520 | tf_op jit(solution)/shard_map/ppermute | solution.py:115
  117.3 22.5 %collective-permute-start.18 = (bf16[3584,128]{1,0:T(8,128)(2,1)S(1)}, bf16[3584,128]{1,0:T(8,128)(2,1)S(1)}, u32[]{:S(2)}, u32[]{:S(2)}) collective-permute-start(bf16[3584,128]{1,0:T(8,128)(2,1)S(1)} %get-tuple-element.123), channel_id=1, source_target_pairs={{0,2},{1,65},{2,4},{3,67},{4,6},{5,69},{6,0},{7,71},{8,10},{9,73},... | collective-permute-start | bytes 2752520 | tf_op jit(solution)/shard_map/ppermute | solution.py:115
  117.4 22.4 %collective-permute-start.20 = (bf16[3584,128]{1,0:T(8,128)(2,1)S(1)}, bf16[3584,128]{1,0:T(8,128)(2,1)S(1)}, u32[]{:S(2)}, u32[]{:S(2)}) collective-permute-start(bf16[3584,128]{1,0:T(8,128)(2,1)S(1)} %get-tuple-element.125), channel_id=1, source_target_pairs={{0,6},{1,193},{2,0},{3,195},{4,2},{5,197},{6,4},{7,199},{8,14},{9,... | collective-permute-start | bytes 2752520 | tf_op jit(solution)/shard_map/ppermute | solution.py:115
  142.8 26.5 %collective-permute-start.24 = (bf16[4096,128]{1,0:T(8,128)(2,1)S(1)}, bf16[4096,128]{1,0:T(8,128)(2,1)S(1)}, u32[]{:S(2)}, u32[]{:S(2)}) collective-permute-start(bf16[4096,128]{1,0:T(8,128)(2,1)S(1)} %get-tuple-element.128), channel_id=1, source_target_pairs={{0,64},{1,3},{2,66},{3,5},{4,68},{5,7},{6,70},{7,1},{8,72},{9,11},... | collective-permute-start | bytes 3145736 | tf_op jit(solution)/shard_map/ppermute | solution.py:115
  142.9 26.4 %collective-permute-start.25 = (bf16[4096,128]{1,0:T(8,128)(2,1)S(1)}, bf16[4096,128]{1,0:T(8,128)(2,1)S(1)}, u32[]{:S(2)}, u32[]{:S(2)}) collective-permute-start(bf16[4096,128]{1,0:T(8,128)(2,1)S(1)} %get-tuple-element.129), channel_id=1, source_target_pairs={{0,128},{1,5},{2,130},{3,7},{4,132},{5,1},{6,134},{7,3},{8,136},{9... | collective-permute-start | bytes 3145736 | tf_op jit(solution)/shard_map/ppermute | solution.py:115
  143.0 26.6 %collective-permute-start.26 = (bf16[4096,128]{1,0:T(8,128)(2,1)S(1)}, bf16[4096,128]{1,0:T(8,128)(2,1)S(1)}, u32[]{:S(2)}, u32[]{:S(2)}) collective-permute-start(bf16[4096,128]{1,0:T(8,128)(2,1)S(1)} %get-tuple-element.130), channel_id=1, source_target_pairs={{0,192},{1,7},{2,194},{3,1},{4,196},{5,3},{6,198},{7,5},{8,200},{9... | collective-permute-start | bytes 3145736 | tf_op jit(solution)/shard_map/ppermute | solution.py:115
  170.1 21.4 %collective-permute-start.32 = (bf16[1536,128]{1,0:T(8,128)(2,1)S(1)}, bf16[1536,128]{1,0:T(8,128)(2,1)S(1)}, u32[]{:S(2)}, u32[]{:S(2)}) collective-permute-start(bf16[1536,128]{1,0:T(8,128)(2,1)S(1)} %get-tuple-element.137), channel_id=1, source_target_pairs={{0,1},{1,0},{2,3},{3,2},{4,5},{5,4},{6,7},{7,6},{8,9},{9,8},{10,11... | collective-permute-start | bytes 1179656 | tf_op jit(solution)/shard_map/ppermute | solution.py:115
  170.5 24.2 %collective-permute-start.28 = (f32[144,128]{1,0:T(8,128)S(1)}, f32[144,128]{1,0:T(8,128)S(1)}, u32[]{:S(2)}, u32[]{:S(2)}) collective-permute-start(f32[144,128]{1,0:T(8,128)S(1)} %get-tuple-element.133), channel_id=1, source_target_pairs={{0,64},{1,65},{2,66},{3,67},{4,68},{5,69},{6,70},{7,71},{8,72},{9,... | collective-permute-start | bytes 221192 | tf_op jit(solution)/shard_map/ppermute | solution.py:115
  170.9 29.0 %collective-permute-start.27 = (bf16[512,128]{1,0:T(8,128)(2,1)S(1)}, bf16[512,128]{1,0:T(8,128)(2,1)S(1)}, u32[]{:S(2)}, u32[]{:S(2)}) collective-permute-start(bf16[512,128]{1,0:T(8,128)(2,1)S(1)} %get-tuple-element.132), channel_id=1, source_target_pairs={{0,32},{1,33},{2,34},{3,35},{4,36},{5,37},{6,38},{7,39},{8,40},{9,... | collective-permute-start | bytes 393224 | tf_op jit(solution)/shard_map/ppermute | solution.py:115
  191.6 16.8 %collective-permute-start.33 = (bf16[1024,128]{1,0:T(8,128)(2,1)S(1)}, bf16[1024,128]{1,0:T(8,128)(2,1)S(1)}, u32[]{:S(2)}, u32[]{:S(2)}) collective-permute-start(bf16[1024,128]{1,0:T(8,128)(2,1)S(1)} %pad_maximum_fusion.1), channel_id=1, source_target_pairs={{0,56},{1,9},{2,58},{3,11},{4,60},{5,13},{6,62},{7,15},{8,0},{9,17... | collective-permute-start | bytes 786440 | tf_op jit(solution)/shard_map/ppermute | solution.py:115
  193.7 14.8 %collective-permute-start.34 = (bf16[1024,128]{1,0:T(8,128)(2,1)S(1)}, bf16[1024,128]{1,0:T(8,128)(2,1)S(1)}, u32[]{:S(2)}, u32[]{:S(2)}) collective-permute-start(bf16[1024,128]{1,0:T(8,128)(2,1)S(1)} %pad_maximum_fusion.2), channel_id=1, source_target_pairs={{0,48},{1,17},{2,50},{3,19},{4,52},{5,21},{6,54},{7,23},{8,56},{9,... | collective-permute-start | bytes 786440 | tf_op jit(solution)/shard_map/ppermute | solution.py:115
  194.1 21.2 %collective-permute-start.35 = (bf16[1024,128]{1,0:T(8,128)(2,1)S(1)}, bf16[1024,128]{1,0:T(8,128)(2,1)S(1)}, u32[]{:S(2)}, u32[]{:S(2)}) collective-permute-start(bf16[1024,128]{1,0:T(8,128)(2,1)S(1)} %pad_maximum_fusion.3), channel_id=1, source_target_pairs={{0,40},{1,25},{2,42},{3,27},{4,44},{5,29},{6,46},{7,31},{8,48},{9,... | collective-permute-start | bytes 786440 | tf_op jit(solution)/shard_map/ppermute | solution.py:115
  (20 other events, 180.9 us)

commit v3 on v2

--- a/solution.py
+++ b/solution.py
@@ -399,15 +399,11 @@
 NORM = 1.0 / math.sqrt(NY * NZ * NX * NB * BLK)
 
 
-def two_parts(value):
-    upper = value.astype(jnp.bfloat16)
-    return upper, (value - upper.astype(jnp.float32)).astype(jnp.bfloat16)
-
-
 def owner_kernel(
     info_ref, table_ref, first_ref, second_ref, third_ref, turned_ref, tiles,
-    r1, r2, r3, sums_ref, o0, o1, o2, o3, total, info, table, q1, q2, q3, sem,
+    r1, r2, r3, sums_ref, o0, o1, o2, o3, passed_ref, total, info, table, q1, q2, q3, sem,
 ):
+    passed_ref[...] = sums_ref[...]
     copies = start_all(
         [(info_ref, info), (table_ref, table), (first_ref, q1), (second_ref, q2), (third_ref, q3)],
         sem,
@@ -466,13 +462,17 @@
             swap_ref[(m - 5) * ROWS : (m - 4) * ROWS, :] = value
 
 
-def keep_sum_kernel(keep_ref, far_ref, sums_ref, out_ref, passed_ref):
-    out_ref[...] = keep_ref[...].astype(jnp.float32) + far_ref[...].astype(jnp.float32)
+def relay_kernel(mine_ref, swap_ref, third_ref, far_ref, sums_ref, out_ref, passed_ref):
     passed_ref[...] = sums_ref[...]
+    at = slice(ROWS, 2 * ROWS)
+    own = mine_ref[at, :].astype(jnp.float32) + third_ref[:ROWS, :].astype(jnp.float32)
+    out_ref[:ROWS, :] = (own + far_ref[...].astype(jnp.float32)).astype(jnp.bfloat16)
+    other = swap_ref[at, :].astype(jnp.float32) + third_ref[ROWS:, :].astype(jnp.float32)
+    out_ref[ROWS:, :] = other.astype(jnp.bfloat16)
 
 
 def last_sum_kernel(
-    core_ref, sums_ref, keep_ref, a_ref, b_ref, c_ref, hold_ref, send_ref, passed_ref
+    core_ref, sums_ref, keep_ref, a_ref, b_ref, hold_ref, send_ref, passed_ref
 ):
     passed_ref[...] = sums_ref[...]
     core = core_ref[0]
@@ -481,9 +481,8 @@
     def total(first):
         at = slice(first, first + half)
         value = a_ref[at, :].astype(jnp.float32) + b_ref[at, :].astype(jnp.float32)
-        value = value + c_ref[at, :].astype(jnp.float32)
         if first < ROWS:
-            value = value + keep_ref[at, :]
+            value = value + keep_ref[at, :].astype(jnp.float32)
         return value
 
     for n in range(2):
@@ -509,12 +508,22 @@
     bias_ref[...] = sums_ref[BLK : BLK + 1, :] * NORM
 
 
-def butterfly(value, target, size):
-    step = 1
-    while step < size:
+def butterfly(value, target, steps):
+    for step in steps:
         value = value + moved(value, functools.partial(target, step))
-        step *= 2
     return value
+
+
+def across_y(step, y, z, x, c):
+    return (y ^ step, z, x, c)
+
+
+def across_z(step, y, z, x, c):
+    return (y, z ^ step, x, c)
+
+
+def across_x(step, y, z, x, c):
+    return (y, z, x ^ step, c)
 
 
 def shards(features, weight, out_bias, edge_tiles, block_row, tile_slot, send_list, out_grad):
@@ -609,7 +618,7 @@
         moved_bytes=11000000,
     )(*parts, tiles, info, table)
     agg_half = near
-    for steps, kind in (((1, 3), f32), ((2,), bf16)):
+    for steps, kind in (((1,), f32), ((3,), f32), ((2,), bf16)):
         agg_half = call(
             functools.partial(far_kernel, steps),
             struct((ROWS, BLK), kind),
@@ -649,12 +658,12 @@
     second_back = along_sparse(second_back, 2)
     back = [along_sparse(first_back, 1), second_back, along_sparse(third_back, 3)]
 
-    sums = butterfly(sums, lambda step, y, z, x, c: (y, z ^ step, x, c), NZ)
-    owned = call(
+    sums = butterfly(sums, across_z, (1, 2, 4))
+    *owned, sums = call(
         owner_kernel,
-        [struct((SEND, BLK), bf16)] + [struct((SEND, BLK), bf16)] * 3,
+        [struct((SEND, BLK), bf16)] * 4 + [struct((SUMS, BLK), f32)],
         [ANY] * 5 + [VMEM] * 6,
-        [VMEM] * 4,
+        [VMEM] * 5,
         [
             pltpu.VMEM((257 * HALF, BLK), f32),
             pltpu.SMEM((INFO,), i32),
@@ -666,6 +675,7 @@
         moved_bytes=11000000,
         vmem=21,
     )(info, table, *requests, turned, tiles, *back, sums)
+    sums = butterfly(sums, across_y, (1,))
     owned = [owned[0]] + [along_dense(owned[j], j) for j in range(1, 4)]
     keep, opposite, mine, swap, sums = call(
         split_sum_kernel,
@@ -676,30 +686,29 @@
         [VMEM] * 5,
         moved_bytes=5000000,
     )(*owned, sums)
-    opposite = along_z(opposite, 4)
+    opposite = along_z(opposite, -2)
     swap = to_other_core(swap)
-    pieces = [
-        jnp.concatenate([mine[s * ROWS : (s + 1) * ROWS], swap[s * ROWS : (s + 1) * ROWS]], axis=0)
-        for s in range(3)
-    ]
-    pieces = [along_z(pieces[s - 1], -s) for s in (3, 2, 1)][::-1]
-    sums = butterfly(sums, lambda step, y, z, x, c: (y ^ step, z, x, c), NY)
-    keep, sums = call(
-        keep_sum_kernel,
-        [struct((ROWS, BLK), f32), struct((SUMS, BLK), f32)],
-        [VMEM] * 3,
+    first, third = (
+        along_z(jnp.concatenate([ref[at : at + ROWS] for ref in (mine, swap)], axis=0), -1)
+        for at in (0, 2 * ROWS)
+    )
+    sums = butterfly(sums, across_y, (2,))
+    second, sums = call(
+        relay_kernel,
+        [struct((2 * ROWS, BLK), bf16), struct((SUMS, BLK), f32)],
+        [VMEM] * 5,
         [VMEM] * 2,
-        moved_bytes=500000,
-    )(keep, opposite, sums)
-    sums = butterfly(sums, lambda step, y, z, x, c: (y, z, x ^ step, c), NX)
-
+        moved_bytes=1500000,
+    )(mine, swap, third, opposite, sums)
+    second = along_z(second, -2)
+    sums = butterfly(sums, across_x, (1, 2))
     hold, send, sums = call(
         last_sum_kernel,
         [struct((ROWS, BLK), f32)] * 2 + [struct((SUMS, BLK), f32)],
-        [SMEM] + [VMEM] * 5,
+        [SMEM] + [VMEM] * 4,
         [VMEM] * 3,
         moved_bytes=1500000,
-    )(core_array, sums, keep, *pieces)
+    )(core_array, sums, keep, first, second)
     feature_grad, weight_grad, bias_grad = call(
         turn_kernel,
         [struct((NB // 2 * BLK, BLK), f32), struct((BLK, BLK), f32), struct((1, BLK), f32)],

time: 228 us -> 226 us (level)
    pallas_call x2 -> x3, Pallas kernels: 4.67 us -> 5.86 us  [shards(): call(functools.partial(far_kernel, steps), struct((ROWS, BLK), kind), [VM...]
  transfers between devices with their start and end apart: 37 -> 37, of which waited for: 19 -> 22; matrix products, arithmetic and copies ran while one was open for 3% -> 3% of each run, Pallas kernels for 8% -> 9%
where the time goes in v3:
time: 226 us; the launch traced here: 225 us
  waiting for transfers between devices  94.5 us (42%)
  starting transfers between devices  76.4 us (34%)
  Pallas kernels  30.7 us (14%)
  between operations  14.7 us (7%)
  local copies, waits for them, and re-layouts  5.79 us (3%)
    ppermute x37, waiting for transfers between devices, moved(): return lax.ppermute(value, ('nodes', 'rep'), pairs)  94.5 us
    ppermute x37, starting transfers between devices, moved(): return lax.ppermute(value, ('nodes', 'rep'), pairs)  76.4 us
    pallas_call x3, Pallas kernels, shards(): call(functools.partial(far_kernel, steps), struct((ROWS, BLK), kind), [VM...  5.86 us
    pallas_call x1, Pallas kernels, shards(): call(plan_kernel, [struct((INFO,), i32)] + [struct((128,), i32)] * 3, [SM...  5.31 us
  transfers between devices with their start and end apart: 37, of which 22 were waited for; matrix products, arithmetic and copies ran while one was open for 3% of the time, Pallas kernels for 9%

profile of v3, /device:TPU:1, one launch (start us, length us, event | category | flops | bytes accessed | tf_op | source)
XLA Modules:
  0.0 224.7 jit_solution(2045857068302193993)
XLA Ops:
  8.6 3.2 %collective-permute-start = (s32[3,128]{1,0:T(4,128)S(1)}, s32[3,128]{1,0:T(4,128)S(1)}, u32[]{:S(2)}, u32[]{:S(2)}) collective-permute-start(s32[3,128]{1,0:T(4,128)S(1)} %pad_add_fusion.own_ref), channel_id=1, source_target_pairs={{0,1},{1,0},{2,3},{3,2},{4,5},{5,4},{6,7},{7,6},{8,9},{9,8},{10,11... | collective-permute-start | bytes 4616 | tf_op jit(solution)/shard_map/ppermute | solution.py:115
  13.8 4.4 %collective-permute-start.2 = (bf16[1040,128]{1,0:T(8,128)(2,1)S(1)}, bf16[1040,128]{1,0:T(8,128)(2,1)S(1)}, u32[]{:S(2)}, u32[]{:S(2)}) collective-permute-start(bf16[1040,128]{1,0:T(8,128)(2,1)S(1)} %get-tuple-element.110), channel_id=1, source_target_pairs={{0,16},{1,49},{2,18},{3,51},{4,20},{5,53},{6,22},{7,55},{8,24},{9,... | collective-permute-start | bytes 798728 | tf_op jit(solution)/shard_map/ppermute | solution.py:115
  19.1 5.3 %shard_map.111 = (s32[640]{0:T(1024)S(1)}, s32[128]{0:T(128)S(1)}, s32[128]{0:T(128)S(1)}, s32[128]{0:T(128)S(1)}) custom-call(s32[128]{0:T(128)S(1)} %fusion.20.code_ref, s32[128]{0:T(128)S(1)} %add_subtract_fusion.rows_ref), custom_call_target="tpu_custom_call" | custom-call | bytes 100000 | tf_op jit(solution)/shard_map/pallas_call | solution.py:572
  30.8 4.4 %collective-permute-done.3 = bf16[1040,128]{1,0:T(8,128)(2,1)S(1)} collective-permute-done((bf16[1040,128]{1,0:T(8,128)(2,1)S(1)}, bf16[1040,128]{1,0:T(8,128)(2,1)S(1)}, u32[]{:S(2)}, u32[]{:S(2)}) %collective-permute-start.3) | collective-permute-done | bytes 266272 | tf_op jit(solution)/shard_map/ppermute | solution.py:115
  44.2 2.8 %collective-permute-start.13 = (bf16[64,128,128]{2,1,0:T(8,128)(2,1)}, bf16[64,128,128]{2,1,0:T(8,128)(2,1)}, u32[]{:S(2)}, u32[]{:S(2)}) collective-permute-start(bf16[64,128,128]{2,1,0:T(8,128)(2,1)} %param.13), channel_id=1, source_target_pairs={{0,1},{1,0},{2,3},{3,2},{4,5},{5,4},{6,7},{7,6},{8,9},{9,8},{10,11... | collective-permute-start | bytes 6291464 | tf_op jit(solution)/shard_map/ppermute | solution.py:115
  47.0 20.9 %collective-permute-done.12.d_ref = bf16[4224,128]{1,0:T(8,128)(2,1)S(1)} collective-permute-done((bf16[4224,128]{1,0:T(8,128)(2,1)S(1)}, bf16[4224,128]{1,0:T(8,128)(2,1)S(1)}, u32[]{:S(2)}, u32[]{:S(2)}) %collective-permute-start.12) | collective-permute-done | bytes 1081376 | tf_op jit(solution)/shard_map/ppermute | solution.py:115
  69.7 4.2 %shard_map.114 = (bf16[3584,128]{1,0:T(8,128)(2,1)S(1)}, bf16[3584,128]{1,0:T(8,128)(2,1)S(1)}, bf16[3584,128]{1,0:T(8,128)(2,1)S(1)}) custom-call(bf16[4224,128]{1,0:T(8,128)(2,1)S(1)} %constant_dynamic-update-slice_fusion.a_ref, bf16[4224,128]{1,0:T(8,128)(2,1)} %collective-permute-done.10.b_ref, bf16[4224,128]{1,0:T(8,128)(2,1)S(1)} %collective-permute-done.11.c_ref, ...), custom_call_target="tpu_custom_call" | custom-call | bytes 7000000 | tf_op jit(solution)/shard_map/pallas_call | solution.py:596
  73.9 2.8 %collective-permute-start.14 = (bf16[3584,128]{1,0:T(8,128)(2,1)S(1)}, bf16[3584,128]{1,0:T(8,128)(2,1)S(1)}, u32[]{:S(2)}, u32[]{:S(2)}) collective-permute-start(bf16[3584,128]{1,0:T(8,128)(2,1)S(1)} %get-tuple-element.120), channel_id=1, source_target_pairs={{0,6},{1,193},{2,0},{3,195},{4,2},{5,197},{6,4},{7,199},{8,14},{9,... | collective-permute-start | bytes 2752520 | tf_op jit(solution)/shard_map/ppermute | solution.py:115
  82.3 3.1 %shard_map.113.near_ref = f32[512,128]{1,0:T(8,128)S(1)} custom-call(bf16[4224,128]{1,0:T(8,128)(2,1)S(1)} %constant_dynamic-update-slice_fusion.a_ref, bf16[4224,128]{1,0:T(8,128)(2,1)} %collective-permute-done.10.b_ref, bf16[4224,128]{1,0:T(8,128)(2,1)S(1)} %collective-permute-done.11.c_ref, bf16[4224,128]{1,0:T(8,128)(2,1)S(1)} %collective-permute-done.12.d_ref, ...), custom_call_target="tpu_custom_call" | custom-call | flops 67108864 | bytes 11000000 | tf_op jit(solution)/shard_map/pallas_call | solution.py:606
  85.4 11.5 %collective-permute-done.14.refs_0_ = bf16[3584,128]{1,0:T(8,128)(2,1)S(1)} collective-permute-done((bf16[3584,128]{1,0:T(8,128)(2,1)S(1)}, bf16[3584,128]{1,0:T(8,128)(2,1)S(1)}, u32[]{:S(2)}, u32[]{:S(2)}) %collective-permute-start.14) | collective-permute-done | bytes 917536 | tf_op jit(solution)/shard_map/ppermute | solution.py:115
  106.7 4.3 %shard_map.118 = (bf16[1024,128]{1,0:T(8,128)(2,1)}, f32[144,128]{1,0:T(8,128)S(1)}, bf16[512,128]{1,0:T(8,128)(2,1)S(1)}, bf16[3584,128]{1,0:T(8,128)(2,1)S(1)}) custom-call(s32[1]{0:T(128)} %bitcast.15.core_ref, bf16[512,128]{1,0:T(8,128)(2,1)S(1)} %shard_map.117.own_agg, bf16[512,128]{1,0:T(8,128)(2,1)S(1)} %collective-permute-done.17.other_agg, ...), custom_call_target="tpu_custom_call" | custom-call | flops 268435456 | bytes 8000000 | tf_op jit(solution)/shard_map/pallas_call | solution.py:633
  112.9 2.7 %shard_map.119 = (bf16[3584,128]{1,0:T(8,128)(2,1)S(1)}, bf16[3584,128]{1,0:T(8,128)(2,1)S(1)}) custom-call(bf16[128,128,128]{2,1,0:T(8,128)(2,1)S(1)} %constant_dynamic-update-slice_fusion.6.tiles.refs_1_, bf16[512,128]{1,0:T(8,128)(2,1)S(1)} %get-tuple-element.123.turned_ref, s32[640]{0:T(1024)S(1)} %get-tuple-element.108.info_ref.refs_2_), custom_call_target="tpu_custom_call" | custom-call | flops 134217728 | bytes 4000000 | tf_op jit(solution)/shard_map/pallas_call | solution.py:649
  124.5 5.1 %collective-permute-done.22 = f32[144,128]{1,0:T(8,128)S(1)} collective-permute-done((f32[144,128]{1,0:T(8,128)S(1)}, f32[144,128]{1,0:T(8,128)S(1)}, u32[]{:S(2)}, u32[]{:S(2)}) %collective-permute-start.22) | collective-permute-done | bytes 73760 | tf_op jit(solution)/shard_map/ppermute | solution.py:115
  129.6 4.6 %collective-permute-start.23 = (f32[144,128]{1,0:T(8,128)S(1)}, f32[144,128]{1,0:T(8,128)S(1)}, u32[]{:S(2)}, u32[]{:S(2)}) collective-permute-start(f32[144,128]{1,0:T(8,128)S(1)} %add.201), channel_id=1, source_target_pairs={{0,32},{1,33},{2,34},{3,35},{4,36},{5,37},{6,38},{7,39},{8,40},{9,... | collective-permute-start | bytes 221192 | tf_op jit(solution)/shard_map/ppermute | solution.py:115
  136.8 2.6 %shard_map.120 = (bf16[4096,128]{1,0:T(8,128)(2,1)S(1)}, bf16[4096,128]{1,0:T(8,128)(2,1)S(1)}, bf16[4096,128]{1,0:T(8,128)(2,1)S(1)}, bf16[4096,128]{1,0:T(8,128)(2,1)S(1)}, f32[144,128]{1,0:T(8,128)S(1)}) custom-call(s32[640]{0:T(1024)S(1)} %get-tuple-element.108.info_ref.refs_2_, s32[512]{0:T(512)S(1)} %reshape.149.table_ref, ...), custom_call_target="tpu_custom_call" | custom-call | flops 67108864 | bytes 11000000 | tf_op jit(solution)/shard_map/pallas_call | solution.py:662
  142.2 3.2 %collective-permute-done.27 = f32[144,128]{1,0:T(8,128)S(1)} collective-permute-done((f32[144,128]{1,0:T(8,128)S(1)}, f32[144,128]{1,0:T(8,128)S(1)}, u32[]{:S(2)}, u32[]{:S(2)}) %collective-permute-start.27) | collective-permute-done | bytes 73760 | tf_op jit(solution)/shard_map/ppermute | solution.py:115
  145.4 20.5 %collective-permute-done.24.b_ref = bf16[4096,128]{1,0:T(8,128)(2,1)S(1)} collective-permute-done((bf16[4096,128]{1,0:T(8,128)(2,1)S(1)}, bf16[4096,128]{1,0:T(8,128)(2,1)S(1)}, u32[]{:S(2)}, u32[]{:S(2)}) %collective-permute-start.24) | collective-permute-done | bytes 1048608 | tf_op jit(solution)/shard_map/ppermute | solution.py:115
  167.1 5.2 %collective-permute-start.28 = (bf16[1536,128]{1,0:T(8,128)(2,1)S(1)}, bf16[1536,128]{1,0:T(8,128)(2,1)S(1)}, u32[]{:S(2)}, u32[]{:S(2)}) collective-permute-start(bf16[1536,128]{1,0:T(8,128)(2,1)S(1)} %get-tuple-element.134), channel_id=1, source_target_pairs={{0,1},{1,0},{2,3},{3,2},{4,5},{5,4},{6,7},{7,6},{8,9},{9,8},{10,11... | collective-permute-start | bytes 1179656 | tf_op jit(solution)/shard_map/ppermute | solution.py:115
  173.7 16.1 %collective-permute-start.29 = (bf16[1024,128]{1,0:T(8,128)(2,1)S(1)}, bf16[1024,128]{1,0:T(8,128)(2,1)S(1)}, u32[]{:S(2)}, u32[]{:S(2)}) collective-permute-start(bf16[1024,128]{1,0:T(8,128)(2,1)S(1)} %pad_maximum_fusion.1), channel_id=1, source_target_pairs={{0,56},{1,9},{2,58},{3,11},{4,60},{5,13},{6,62},{7,15},{8,0},{9,17... | collective-permute-start | bytes 786440 | tf_op jit(solution)/shard_map/ppermute | solution.py:115
  191.8 2.7 %collective-permute-done.31 = f32[144,128]{1,0:T(8,128)S(1)} collective-permute-done((f32[144,128]{1,0:T(8,128)S(1)}, f32[144,128]{1,0:T(8,128)S(1)}, u32[]{:S(2)}, u32[]{:S(2)}) %collective-permute-start.31) | collective-permute-done | bytes 73760 | tf_op jit(solution)/shard_map/ppermute | solution.py:115
  194.7 5.4 %collective-permute-done.30.far_ref = bf16[512,128]{1,0:T(8,128)(2,1)S(1)} collective-permute-done((bf16[512,128]{1,0:T(8,128)(2,1)S(1)}, bf16[512,128]{1,0:T(8,128)(2,1)S(1)}, u32[]{:S(2)}, u32[]{:S(2)}) %collective-permute-start.30) | collective-permute-done | bytes 131104 | tf_op jit(solution)/shard_map/ppermute | solution.py:115
  200.4 3.5 %collective-permute-done.32 = f32[144,128]{1,0:T(8,128)S(1)} collective-permute-done((f32[144,128]{1,0:T(8,128)S(1)}, f32[144,128]{1,0:T(8,128)S(1)}, u32[]{:S(2)}, u32[]{:S(2)}) %collective-permute-start.32) | collective-permute-done | bytes 73760 | tf_op jit(solution)/shard_map/ppermute | solution.py:115
  204.9 3.8 %collective-permute-done.33 = f32[144,128]{1,0:T(8,128)S(1)} collective-permute-done((f32[144,128]{1,0:T(8,128)S(1)}, f32[144,128]{1,0:T(8,128)S(1)}, u32[]{:S(2)}, u32[]{:S(2)}) %collective-permute-start.33) | collective-permute-done | bytes 73760 | tf_op jit(solution)/shard_map/ppermute | solution.py:115
  210.2 4.9 %collective-permute-start.36 = (f32[512,128]{1,0:T(8,128)S(1)}, f32[512,128]{1,0:T(8,128)S(1)}, u32[]{:S(2)}, u32[]{:S(2)}) collective-permute-start(f32[512,128]{1,0:T(8,128)S(1)} %get-tuple-element.143), channel_id=1, source_target_pairs={{0,1},{1,0},{2,3},{3,2},{4,5},{5,4},{6,7},{7,6},{8,9},{9,8},{10,11... | collective-permute-start | bytes 786440 | tf_op jit(solution)/shard_map/ppermute | solution.py:115
  (121 shorter events, 63.0 us)
Async XLA Ops:
  13.8 15.8 %collective-permute-start.2 = (bf16[1040,128]{1,0:T(8,128)(2,1)S(1)}, bf16[1040,128]{1,0:T(8,128)(2,1)S(1)}, u32[]{:S(2)}, u32[]{:S(2)}) collective-permute-start(bf16[1040,128]{1,0:T(8,128)(2,1)S(1)} %get-tuple-element.110), channel_id=1, source_target_pairs={{0,16},{1,49},{2,18},{3,51},{4,20},{5,53},{6,22},{7,55},{8,24},{9,... | collective-permute-start | bytes 798728 | tf_op jit(solution)/shard_map/ppermute | solution.py:115
  18.1 11.4 %collective-permute-start.1 = (bf16[1040,128]{1,0:T(8,128)(2,1)S(1)}, bf16[1040,128]{1,0:T(8,128)(2,1)S(1)}, u32[]{:S(2)}, u32[]{:S(2)}) collective-permute-start(bf16[1040,128]{1,0:T(8,128)(2,1)S(1)} %get-tuple-element.110), channel_id=1, source_target_pairs={{0,8},{1,57},{2,10},{3,59},{4,12},{5,61},{6,14},{7,63},{8,16},{9,1... | collective-permute-start | bytes 798728 | tf_op jit(solution)/shard_map/ppermute | solution.py:115
  24.4 16.2 %collective-permute-start.7 = (s32[128]{0:T(128)S(1)}, s32[128]{0:T(128)S(1)}, u32[]{:S(2)}, u32[]{:S(2)}) collective-permute-start(s32[128]{0:T(128)S(1)} %get-tuple-element.113), channel_id=1, source_target_pairs={{0,2},{1,65},{2,4},{3,67},{4,6},{5,69},{6,0},{7,71},{8,10},{9,73},... | collective-permute-start | bytes 1544 | tf_op jit(solution)/shard_map/ppermute | solution.py:115
  25.8 14.8 %collective-permute-start.8 = (s32[128]{0:T(128)S(1)}, s32[128]{0:T(128)S(1)}, u32[]{:S(2)}, u32[]{:S(2)}) collective-permute-start(s32[128]{0:T(128)S(1)} %get-tuple-element.114), channel_id=1, source_target_pairs={{0,4},{1,129},{2,6},{3,131},{4,0},{5,133},{6,2},{7,135},{8,12},{9,... | collective-permute-start | bytes 1544 | tf_op jit(solution)/shard_map/ppermute | solution.py:115
  28.4 12.2 %collective-permute-start.9 = (s32[128]{0:T(128)S(1)}, s32[128]{0:T(128)S(1)}, u32[]{:S(2)}, u32[]{:S(2)}) collective-permute-start(s32[128]{0:T(128)S(1)} %get-tuple-element.115), channel_id=1, source_target_pairs={{0,6},{1,193},{2,0},{3,195},{4,2},{5,197},{6,4},{7,199},{8,14},{9,... | collective-permute-start | bytes 1544 | tf_op jit(solution)/shard_map/ppermute | solution.py:115
  40.7 27.2 %collective-permute-start.12 = (bf16[4224,128]{1,0:T(8,128)(2,1)S(1)}, bf16[4224,128]{1,0:T(8,128)(2,1)S(1)}, u32[]{:S(2)}, u32[]{:S(2)}) collective-permute-start(bf16[4224,128]{1,0:T(8,128)(2,1)S(1)} %constant_dynamic-update-slice_fusion.a_ref), channel_id=1, source_target_pairs={{0,64},{1,3},{2,66},{3,5},{4,68},{5,7},{6,70},{7,1},{8,72},{9,11},... | collective-permute-start | bytes 3244040 | tf_op jit(solution)/shard_map/ppermute | solution.py:115
  41.7 26.2 %collective-permute-start.11 = (bf16[4224,128]{1,0:T(8,128)(2,1)S(1)}, bf16[4224,128]{1,0:T(8,128)(2,1)S(1)}, u32[]{:S(2)}, u32[]{:S(2)}) collective-permute-start(bf16[4224,128]{1,0:T(8,128)(2,1)S(1)} %constant_dynamic-update-slice_fusion.a_ref), channel_id=1, source_target_pairs={{0,128},{1,5},{2,130},{3,7},{4,132},{5,1},{6,134},{7,3},{8,136},{9... | collective-permute-start | bytes 3244040 | tf_op jit(solution)/shard_map/ppermute | solution.py:115
  42.8 25.8 %collective-permute-start.10 = (bf16[4224,128]{1,0:T(8,128)(2,1)S(1)}, bf16[4224,128]{1,0:T(8,128)(2,1)}, u32[]{:S(2)}, u32[]{:S(2)}) collective-permute-start(bf16[4224,128]{1,0:T(8,128)(2,1)S(1)} %constant_dynamic-update-slice_fusion.a_ref), channel_id=1, source_target_pairs={{0,192},{1,7},{2,194},{3,1},{4,196},{5,3},{6,198},{7,5},{8,200},{9... | collective-permute-start | bytes 3244040 | tf_op jit(solution)/shard_map/ppermute | solution.py:115
  44.2 36.2 %collective-permute-start.13 = (bf16[64,128,128]{2,1,0:T(8,128)(2,1)}, bf16[64,128,128]{2,1,0:T(8,128)(2,1)}, u32[]{:S(2)}, u32[]{:S(2)}) collective-permute-start(bf16[64,128,128]{2,1,0:T(8,128)(2,1)} %param.13), channel_id=1, source_target_pairs={{0,1},{1,0},{2,3},{3,2},{4,5},{5,4},{6,7},{7,6},{8,9},{9,8},{10,11... | collective-permute-start | bytes 6291464 | tf_op jit(solution)/shard_map/ppermute | solution.py:115
  73.9 23.0 %collective-permute-start.14 = (bf16[3584,128]{1,0:T(8,128)(2,1)S(1)}, bf16[3584,128]{1,0:T(8,128)(2,1)S(1)}, u32[]{:S(2)}, u32[]{:S(2)}) collective-permute-start(bf16[3584,128]{1,0:T(8,128)(2,1)S(1)} %get-tuple-element.120), channel_id=1, source_target_pairs={{0,6},{1,193},{2,0},{3,195},{4,2},{5,197},{6,4},{7,199},{8,14},{9,... | collective-permute-start | bytes 2752520 | tf_op jit(solution)/shard_map/ppermute | solution.py:115
  76.7 23.8 %collective-permute-start.15 = (bf16[3584,128]{1,0:T(8,128)(2,1)S(1)}, bf16[3584,128]{1,0:T(8,128)(2,1)S(1)}, u32[]{:S(2)}, u32[]{:S(2)}) collective-permute-start(bf16[3584,128]{1,0:T(8,128)(2,1)S(1)} %get-tuple-element.121), channel_id=1, source_target_pairs={{0,2},{1,65},{2,4},{3,67},{4,6},{5,69},{6,0},{7,71},{8,10},{9,73},... | collective-permute-start | bytes 2752520 | tf_op jit(solution)/shard_map/ppermute | solution.py:115
  77.0 25.7 %collective-permute-start.16 = (bf16[3584,128]{1,0:T(8,128)(2,1)S(1)}, bf16[3584,128]{1,0:T(8,128)(2,1)S(1)}, u32[]{:S(2)}, u32[]{:S(2)}) collective-permute-start(bf16[3584,128]{1,0:T(8,128)(2,1)S(1)} %get-tuple-element.122), channel_id=1, source_target_pairs={{0,4},{1,129},{2,6},{3,131},{4,0},{5,133},{6,2},{7,135},{8,12},{9,... | collective-permute-start | bytes 2752520 | tf_op jit(solution)/shard_map/ppermute | solution.py:115
  111.0 25.8 %collective-permute-start.19 = (bf16[3584,128]{1,0:T(8,128)(2,1)S(1)}, bf16[3584,128]{1,0:T(8,128)(2,1)S(1)}, u32[]{:S(2)}, u32[]{:S(2)}) collective-permute-start(bf16[3584,128]{1,0:T(8,128)(2,1)S(1)} %get-tuple-element.125), channel_id=1, source_target_pairs={{0,4},{1,129},{2,6},{3,131},{4,0},{5,133},{6,2},{7,135},{8,12},{9,... | collective-permute-start | bytes 2752520 | tf_op jit(solution)/shard_map/ppermute | solution.py:115
  115.5 21.2 %collective-permute-start.18 = (bf16[3584,128]{1,0:T(8,128)(2,1)S(1)}, bf16[3584,128]{1,0:T(8,128)(2,1)S(1)}, u32[]{:S(2)}, u32[]{:S(2)}) collective-permute-start(bf16[3584,128]{1,0:T(8,128)(2,1)S(1)} %get-tuple-element.124), channel_id=1, source_target_pairs={{0,2},{1,65},{2,4},{3,67},{4,6},{5,69},{6,0},{7,71},{8,10},{9,73},... | collective-permute-start | bytes 2752520 | tf_op jit(solution)/shard_map/ppermute | solution.py:115
  116.5 20.3 %collective-permute-start.20 = (bf16[3584,128]{1,0:T(8,128)(2,1)S(1)}, bf16[3584,128]{1,0:T(8,128)(2,1)S(1)}, u32[]{:S(2)}, u32[]{:S(2)}) collective-permute-start(bf16[3584,128]{1,0:T(8,128)(2,1)S(1)} %get-tuple-element.126), channel_id=1, source_target_pairs={{0,6},{1,193},{2,0},{3,195},{4,2},{5,197},{6,4},{7,199},{8,14},{9,... | collective-permute-start | bytes 2752520 | tf_op jit(solution)/shard_map/ppermute | solution.py:115
  122.8 6.8 %collective-permute-start.22 = (f32[144,128]{1,0:T(8,128)S(1)}, f32[144,128]{1,0:T(8,128)S(1)}, u32[]{:S(2)}, u32[]{:S(2)}) collective-permute-start(f32[144,128]{1,0:T(8,128)S(1)} %add.200), channel_id=1, source_target_pairs={{0,16},{1,17},{2,18},{3,19},{4,20},{5,21},{6,22},{7,23},{8,24},{9,... | collective-permute-start | bytes 221192 | tf_op jit(solution)/shard_map/ppermute | solution.py:115
  129.6 7.2 %collective-permute-start.23 = (f32[144,128]{1,0:T(8,128)S(1)}, f32[144,128]{1,0:T(8,128)S(1)}, u32[]{:S(2)}, u32[]{:S(2)}) collective-permute-start(f32[144,128]{1,0:T(8,128)S(1)} %add.201), channel_id=1, source_target_pairs={{0,32},{1,33},{2,34},{3,35},{4,36},{5,37},{6,38},{7,39},{8,40},{9,... | collective-permute-start | bytes 221192 | tf_op jit(solution)/shard_map/ppermute | solution.py:115
  139.5 26.5 %collective-permute-start.24 = (bf16[4096,128]{1,0:T(8,128)(2,1)S(1)}, bf16[4096,128]{1,0:T(8,128)(2,1)S(1)}, u32[]{:S(2)}, u32[]{:S(2)}) collective-permute-start(bf16[4096,128]{1,0:T(8,128)(2,1)S(1)} %get-tuple-element.129), channel_id=1, source_target_pairs={{0,64},{1,3},{2,66},{3,5},{4,68},{5,7},{6,70},{7,1},{8,72},{9,11},... | collective-permute-start | bytes 3145736 | tf_op jit(solution)/shard_map/ppermute | solution.py:115
  139.5 26.4 %collective-permute-start.25 = (bf16[4096,128]{1,0:T(8,128)(2,1)S(1)}, bf16[4096,128]{1,0:T(8,128)(2,1)S(1)}, u32[]{:S(2)}, u32[]{:S(2)}) collective-permute-start(bf16[4096,128]{1,0:T(8,128)(2,1)S(1)} %get-tuple-element.130), channel_id=1, source_target_pairs={{0,128},{1,5},{2,130},{3,7},{4,132},{5,1},{6,134},{7,3},{8,136},{9... | collective-permute-start | bytes 3145736 | tf_op jit(solution)/shard_map/ppermute | solution.py:115
  140.1 26.4 %collective-permute-start.26 = (bf16[4096,128]{1,0:T(8,128)(2,1)S(1)}, bf16[4096,128]{1,0:T(8,128)(2,1)S(1)}, u32[]{:S(2)}, u32[]{:S(2)}) collective-permute-start(bf16[4096,128]{1,0:T(8,128)(2,1)S(1)} %get-tuple-element.131), channel_id=1, source_target_pairs={{0,192},{1,7},{2,194},{3,1},{4,196},{5,3},{6,198},{7,5},{8,200},{9... | collective-permute-start | bytes 3145736 | tf_op jit(solution)/shard_map/ppermute | solution.py:115
  173.7 26.4 %collective-permute-start.29 = (bf16[1024,128]{1,0:T(8,128)(2,1)S(1)}, bf16[1024,128]{1,0:T(8,128)(2,1)S(1)}, u32[]{:S(2)}, u32[]{:S(2)}) collective-permute-start(bf16[1024,128]{1,0:T(8,128)(2,1)S(1)} %pad_maximum_fusion.1), channel_id=1, source_target_pairs={{0,56},{1,9},{2,58},{3,11},{4,60},{5,13},{6,62},{7,15},{8,0},{9,17... | collective-permute-start | bytes 786440 | tf_op jit(solution)/shard_map/ppermute | solution.py:115
  191.0 9.1 %collective-permute-start.30 = (bf16[512,128]{1,0:T(8,128)(2,1)S(1)}, bf16[512,128]{1,0:T(8,128)(2,1)S(1)}, u32[]{:S(2)}, u32[]{:S(2)}) collective-permute-start(bf16[512,128]{1,0:T(8,128)(2,1)S(1)} %get-tuple-element.135), channel_id=1, source_target_pairs={{0,48},{1,17},{2,50},{3,19},{4,52},{5,21},{6,54},{7,23},{8,56},{9,... | collective-permute-start | bytes 393224 | tf_op jit(solution)/shard_map/ppermute | solution.py:115
  194.6 14.1 %collective-permute-start.34 = (bf16[1024,128]{1,0:T(8,128)(2,1)S(1)}, bf16[1024,128]{1,0:T(8,128)(2,1)S(1)}, u32[]{:S(2)}, u32[]{:S(2)}) collective-permute-start(bf16[1024,128]{1,0:T(8,128)(2,1)S(1)} %pad_maximum_fusion.2), channel_id=1, source_target_pairs={{0,56},{1,9},{2,58},{3,11},{4,60},{5,13},{6,62},{7,15},{8,0},{9,17... | collective-permute-start | bytes 786440 | tf_op jit(solution)/shard_map/ppermute | solution.py:115
  200.2 9.8 %collective-permute-start.35 = (bf16[1024,128]{1,0:T(8,128)(2,1)S(1)}, bf16[1024,128]{1,0:T(8,128)(2,1)S(1)}, u32[]{:S(2)}, u32[]{:S(2)}) collective-permute-start(bf16[1024,128]{1,0:T(8,128)(2,1)S(1)} %get-tuple-element.139), channel_id=1, source_target_pairs={{0,48},{1,17},{2,50},{3,19},{4,52},{5,21},{6,54},{7,23},{8,56},{9,... | collective-permute-start | bytes 786440 | tf_op jit(solution)/shard_map/ppermute | solution.py:115
  (20 other events, 244.9 us)

commit v4 on v3

--- a/solution.py
+++ b/solution.py
@@ -675,7 +675,7 @@
         moved_bytes=11000000,
         vmem=21,
     )(info, table, *requests, turned, tiles, *back, sums)
-    sums = butterfly(sums, across_y, (1,))
+    sums = butterfly(sums, across_y, (1, 2))
     owned = [owned[0]] + [along_dense(owned[j], j) for j in range(1, 4)]
     keep, opposite, mine, swap, sums = call(
         split_sum_kernel,
@@ -692,7 +692,7 @@
         along_z(jnp.concatenate([ref[at : at + ROWS] for ref in (mine, swap)], axis=0), -1)
         for at in (0, 2 * ROWS)
     )
-    sums = butterfly(sums, across_y, (2,))
+    sums = butterfly(sums, across_x, (1,))
     second, sums = call(
         relay_kernel,
         [struct((2 * ROWS, BLK), bf16), struct((SUMS, BLK), f32)],
@@ -701,7 +701,7 @@
         moved_bytes=1500000,
     )(mine, swap, third, opposite, sums)
     second = along_z(second, -2)
-    sums = butterfly(sums, across_x, (1, 2))
+    sums = butterfly(sums, across_x, (2,))
     hold, send, sums = call(
         last_sum_kernel,
         [struct((ROWS, BLK), f32)] * 2 + [struct((SUMS, BLK), f32)],

time: 226 us -> 228 us (level)
  starting transfers between devices: 76.4 us -> 82.1 us
  waiting for transfers between devices: 94.5 us -> 91 us
    ppermute x37, starting transfers between devices: 76.4 us -> 82.1 us  [moved(): return lax.ppermute(value, ('nodes', 'rep'), pairs)]
    ppermute x37, waiting for transfers between devices: 94.5 us -> 91 us  [moved(): return lax.ppermute(value, ('nodes', 'rep'), pairs)]
where the time goes in v4:
time: 228 us; the launch traced here: 227 us
  waiting for transfers between devices  91 us (40%)
  starting transfers between devices  82.1 us (36%)
  Pallas kernels  30.7 us (13%)
  between operations  14.7 us (6%)
  local copies, waits for them, and re-layouts  5.79 us (3%)
    ppermute x37, waiting for transfers between devices, moved(): return lax.ppermute(value, ('nodes', 'rep'), pairs)  91 us
    ppermute x37, starting transfers between devices, moved(): return lax.ppermute(value, ('nodes', 'rep'), pairs)  82.1 us
    pallas_call x3, Pallas kernels, shards(): call(functools.partial(far_kernel, steps), struct((ROWS, BLK), kind), [VM...  5.86 us
    pallas_call x1, Pallas kernels, shards(): call(plan_kernel, [struct((INFO,), i32)] + [struct((128,), i32)] * 3, [SM...  5.31 us
  transfers between devices with their start and end apart: 37, of which 22 were waited for; matrix products, arithmetic and copies ran while one was open for 3% of the time, Pallas kernels for 9%

profile of v4, /device:TPU:1, one launch (start us, length us, event | category | flops | bytes accessed | tf_op | source)
XLA Modules:
  0.0 226.9 jit_solution(318075948279993818)
XLA Ops:
  8.6 3.2 %collective-permute-start = (s32[3,128]{1,0:T(4,128)S(1)}, s32[3,128]{1,0:T(4,128)S(1)}, u32[]{:S(2)}, u32[]{:S(2)}) collective-permute-start(s32[3,128]{1,0:T(4,128)S(1)} %pad_add_fusion.own_ref), channel_id=1, source_target_pairs={{0,1},{1,0},{2,3},{3,2},{4,5},{5,4},{6,7},{7,6},{8,9},{9,8},{10,11... | collective-permute-start | bytes 4616 | tf_op jit(solution)/shard_map/ppermute | solution.py:115
  13.8 4.4 %collective-permute-start.2 = (bf16[1040,128]{1,0:T(8,128)(2,1)S(1)}, bf16[1040,128]{1,0:T(8,128)(2,1)S(1)}, u32[]{:S(2)}, u32[]{:S(2)}) collective-permute-start(bf16[1040,128]{1,0:T(8,128)(2,1)S(1)} %get-tuple-element.110), channel_id=1, source_target_pairs={{0,16},{1,49},{2,18},{3,51},{4,20},{5,53},{6,22},{7,55},{8,24},{9,... | collective-permute-start | bytes 798728 | tf_op jit(solution)/shard_map/ppermute | solution.py:115
  19.1 5.3 %shard_map.111 = (s32[640]{0:T(1024)S(1)}, s32[128]{0:T(128)S(1)}, s32[128]{0:T(128)S(1)}, s32[128]{0:T(128)S(1)}) custom-call(s32[128]{0:T(128)S(1)} %fusion.20.code_ref, s32[128]{0:T(128)S(1)} %add_subtract_fusion.rows_ref), custom_call_target="tpu_custom_call" | custom-call | bytes 100000 | tf_op jit(solution)/shard_map/pallas_call | solution.py:572
  30.8 4.4 %collective-permute-done.3 = bf16[1040,128]{1,0:T(8,128)(2,1)S(1)} collective-permute-done((bf16[1040,128]{1,0:T(8,128)(2,1)S(1)}, bf16[1040,128]{1,0:T(8,128)(2,1)S(1)}, u32[]{:S(2)}, u32[]{:S(2)}) %collective-permute-start.3) | collective-permute-done | bytes 266272 | tf_op jit(solution)/shard_map/ppermute | solution.py:115
  44.2 2.8 %collective-permute-start.13 = (bf16[64,128,128]{2,1,0:T(8,128)(2,1)}, bf16[64,128,128]{2,1,0:T(8,128)(2,1)}, u32[]{:S(2)}, u32[]{:S(2)}) collective-permute-start(bf16[64,128,128]{2,1,0:T(8,128)(2,1)} %param.13), channel_id=1, source_target_pairs={{0,1},{1,0},{2,3},{3,2},{4,5},{5,4},{6,7},{7,6},{8,9},{9,8},{10,11... | collective-permute-start | bytes 6291464 | tf_op jit(solution)/shard_map/ppermute | solution.py:115
  47.0 20.9 %collective-permute-done.12.d_ref = bf16[4224,128]{1,0:T(8,128)(2,1)S(1)} collective-permute-done((bf16[4224,128]{1,0:T(8,128)(2,1)S(1)}, bf16[4224,128]{1,0:T(8,128)(2,1)S(1)}, u32[]{:S(2)}, u32[]{:S(2)}) %collective-permute-start.12) | collective-permute-done | bytes 1081376 | tf_op jit(solution)/shard_map/ppermute | solution.py:115
  69.7 4.2 %shard_map.114 = (bf16[3584,128]{1,0:T(8,128)(2,1)S(1)}, bf16[3584,128]{1,0:T(8,128)(2,1)S(1)}, bf16[3584,128]{1,0:T(8,128)(2,1)S(1)}) custom-call(bf16[4224,128]{1,0:T(8,128)(2,1)S(1)} %constant_dynamic-update-slice_fusion.a_ref, bf16[4224,128]{1,0:T(8,128)(2,1)} %collective-permute-done.10.b_ref, bf16[4224,128]{1,0:T(8,128)(2,1)S(1)} %collective-permute-done.11.c_ref, ...), custom_call_target="tpu_custom_call" | custom-call | bytes 7000000 | tf_op jit(solution)/shard_map/pallas_call | solution.py:596
  73.9 2.8 %collective-permute-start.14 = (bf16[3584,128]{1,0:T(8,128)(2,1)S(1)}, bf16[3584,128]{1,0:T(8,128)(2,1)S(1)}, u32[]{:S(2)}, u32[]{:S(2)}) collective-permute-start(bf16[3584,128]{1,0:T(8,128)(2,1)S(1)} %get-tuple-element.120), channel_id=1, source_target_pairs={{0,6},{1,193},{2,0},{3,195},{4,2},{5,197},{6,4},{7,199},{8,14},{9,... | collective-permute-start | bytes 2752520 | tf_op jit(solution)/shard_map/ppermute | solution.py:115
  82.3 3.1 %shard_map.113.near_ref = f32[512,128]{1,0:T(8,128)S(1)} custom-call(bf16[4224,128]{1,0:T(8,128)(2,1)S(1)} %constant_dynamic-update-slice_fusion.a_ref, bf16[4224,128]{1,0:T(8,128)(2,1)} %collective-permute-done.10.b_ref, bf16[4224,128]{1,0:T(8,128)(2,1)S(1)} %collective-permute-done.11.c_ref, bf16[4224,128]{1,0:T(8,128)(2,1)S(1)} %collective-permute-done.12.d_ref, ...), custom_call_target="tpu_custom_call" | custom-call | flops 67108864 | bytes 11000000 | tf_op jit(solution)/shard_map/pallas_call | solution.py:606
  85.4 11.5 %collective-permute-done.14.refs_0_ = bf16[3584,128]{1,0:T(8,128)(2,1)S(1)} collective-permute-done((bf16[3584,128]{1,0:T(8,128)(2,1)S(1)}, bf16[3584,128]{1,0:T(8,128)(2,1)S(1)}, u32[]{:S(2)}, u32[]{:S(2)}) %collective-permute-start.14) | collective-permute-done | bytes 917536 | tf_op jit(solution)/shard_map/ppermute | solution.py:115
  106.4 4.3 %shard_map.118 = (bf16[1024,128]{1,0:T(8,128)(2,1)}, f32[144,128]{1,0:T(8,128)S(1)}, bf16[512,128]{1,0:T(8,128)(2,1)S(1)}, bf16[3584,128]{1,0:T(8,128)(2,1)S(1)}) custom-call(s32[1]{0:T(128)} %bitcast.15.core_ref, bf16[512,128]{1,0:T(8,128)(2,1)S(1)} %shard_map.117.own_agg, bf16[512,128]{1,0:T(8,128)(2,1)S(1)} %collective-permute-done.17.other_agg, ...), custom_call_target="tpu_custom_call" | custom-call | flops 268435456 | bytes 8000000 | tf_op jit(solution)/shard_map/pallas_call | solution.py:633
  110.7 2.8 %collective-permute-start.19 = (bf16[3584,128]{1,0:T(8,128)(2,1)S(1)}, bf16[3584,128]{1,0:T(8,128)(2,1)S(1)}, u32[]{:S(2)}, u32[]{:S(2)}) collective-permute-start(bf16[3584,128]{1,0:T(8,128)(2,1)S(1)} %get-tuple-element.125), channel_id=1, source_target_pairs={{0,4},{1,129},{2,6},{3,131},{4,0},{5,133},{6,2},{7,135},{8,12},{9,... | collective-permute-start | bytes 2752520 | tf_op jit(solution)/shard_map/ppermute | solution.py:115
  113.4 2.7 %shard_map.119 = (bf16[3584,128]{1,0:T(8,128)(2,1)S(1)}, bf16[3584,128]{1,0:T(8,128)(2,1)S(1)}) custom-call(bf16[128,128,128]{2,1,0:T(8,128)(2,1)S(1)} %constant_dynamic-update-slice_fusion.6.tiles.refs_1_, bf16[512,128]{1,0:T(8,128)(2,1)S(1)} %get-tuple-element.123.turned_ref, s32[640]{0:T(1024)S(1)} %get-tuple-element.108.info_ref.refs_2_), custom_call_target="tpu_custom_call" | custom-call | flops 134217728 | bytes 4000000 | tf_op jit(solution)/shard_map/pallas_call | solution.py:649
  116.2 2.7 %collective-permute-start.20 = (bf16[3584,128]{1,0:T(8,128)(2,1)S(1)}, bf16[3584,128]{1,0:T(8,128)(2,1)S(1)}, u32[]{:S(2)}, u32[]{:S(2)}) collective-permute-start(bf16[3584,128]{1,0:T(8,128)(2,1)S(1)} %get-tuple-element.126), channel_id=1, source_target_pairs={{0,6},{1,193},{2,0},{3,195},{4,2},{5,197},{6,4},{7,199},{8,14},{9,... | collective-permute-start | bytes 2752520 | tf_op jit(solution)/shard_map/ppermute | solution.py:115
  124.1 3.8 %collective-permute-done.22 = f32[144,128]{1,0:T(8,128)S(1)} collective-permute-done((f32[144,128]{1,0:T(8,128)S(1)}, f32[144,128]{1,0:T(8,128)S(1)}, u32[]{:S(2)}, u32[]{:S(2)}) %collective-permute-start.22) | collective-permute-done | bytes 73760 | tf_op jit(solution)/shard_map/ppermute | solution.py:115
  127.9 6.4 %collective-permute-start.23 = (f32[144,128]{1,0:T(8,128)S(1)}, f32[144,128]{1,0:T(8,128)S(1)}, u32[]{:S(2)}, u32[]{:S(2)}) collective-permute-start(f32[144,128]{1,0:T(8,128)S(1)} %add.201), channel_id=1, source_target_pairs={{0,32},{1,33},{2,34},{3,35},{4,36},{5,37},{6,38},{7,39},{8,40},{9,... | collective-permute-start | bytes 221192 | tf_op jit(solution)/shard_map/ppermute | solution.py:115
  136.2 2.6 %shard_map.120 = (bf16[4096,128]{1,0:T(8,128)(2,1)S(1)}, bf16[4096,128]{1,0:T(8,128)(2,1)S(1)}, bf16[4096,128]{1,0:T(8,128)(2,1)S(1)}, bf16[4096,128]{1,0:T(8,128)(2,1)S(1)}, f32[144,128]{1,0:T(8,128)S(1)}) custom-call(s32[640]{0:T(1024)S(1)} %get-tuple-element.108.info_ref.refs_2_, s32[512]{0:T(512)S(1)} %reshape.149.table_ref, ...), custom_call_target="tpu_custom_call" | custom-call | flops 67108864 | bytes 11000000 | tf_op jit(solution)/shard_map/pallas_call | solution.py:662
  142.8 3.2 %collective-permute-done.27 = f32[144,128]{1,0:T(8,128)S(1)} collective-permute-done((f32[144,128]{1,0:T(8,128)S(1)}, f32[144,128]{1,0:T(8,128)S(1)}, u32[]{:S(2)}, u32[]{:S(2)}) %collective-permute-start.27) | collective-permute-done | bytes 73760 | tf_op jit(solution)/shard_map/ppermute | solution.py:115
  147.1 4.5 %collective-permute-done.28 = f32[144,128]{1,0:T(8,128)S(1)} collective-permute-done((f32[144,128]{1,0:T(8,128)S(1)}, f32[144,128]{1,0:T(8,128)S(1)}, u32[]{:S(2)}, u32[]{:S(2)}) %collective-permute-start.28) | collective-permute-done | bytes 73760 | tf_op jit(solution)/shard_map/ppermute | solution.py:115
  151.6 13.7 %collective-permute-done.24.b_ref = bf16[4096,128]{1,0:T(8,128)(2,1)S(1)} collective-permute-done((bf16[4096,128]{1,0:T(8,128)(2,1)S(1)}, bf16[4096,128]{1,0:T(8,128)(2,1)S(1)}, u32[]{:S(2)}, u32[]{:S(2)}) %collective-permute-start.24) | collective-permute-done | bytes 1048608 | tf_op jit(solution)/shard_map/ppermute | solution.py:115
  166.5 28.6 %collective-permute-start.29 = (bf16[1536,128]{1,0:T(8,128)(2,1)S(1)}, bf16[1536,128]{1,0:T(8,128)(2,1)S(1)}, u32[]{:S(2)}, u32[]{:S(2)}) collective-permute-start(bf16[1536,128]{1,0:T(8,128)(2,1)S(1)} %get-tuple-element.134), channel_id=1, source_target_pairs={{0,1},{1,0},{2,3},{3,2},{4,5},{5,4},{6,7},{7,6},{8,9},{9,8},{10,11... | collective-permute-start | bytes 1179656 | tf_op jit(solution)/shard_map/ppermute | solution.py:115
  201.2 5.4 %collective-permute-done.31.far_ref = bf16[512,128]{1,0:T(8,128)(2,1)S(1)} collective-permute-done((bf16[512,128]{1,0:T(8,128)(2,1)S(1)}, bf16[512,128]{1,0:T(8,128)(2,1)S(1)}, u32[]{:S(2)}, u32[]{:S(2)}) %collective-permute-start.31) | collective-permute-done | bytes 131104 | tf_op jit(solution)/shard_map/ppermute | solution.py:115
  207.4 4.2 %collective-permute-done.33 = f32[144,128]{1,0:T(8,128)S(1)} collective-permute-done((f32[144,128]{1,0:T(8,128)S(1)}, f32[144,128]{1,0:T(8,128)S(1)}, u32[]{:S(2)}, u32[]{:S(2)}) %collective-permute-start.33) | collective-permute-done | bytes 73760 | tf_op jit(solution)/shard_map/ppermute | solution.py:115
  211.7 5.0 %collective-permute-done.35.b_ref = bf16[1024,128]{1,0:T(8,128)(2,1)S(1)} collective-permute-done((bf16[1024,128]{1,0:T(8,128)(2,1)S(1)}, bf16[1024,128]{1,0:T(8,128)(2,1)S(1)}, u32[]{:S(2)}, u32[]{:S(2)}) %collective-permute-start.35) | collective-permute-done | bytes 262176 | tf_op jit(solution)/shard_map/ppermute | solution.py:115
  (121 shorter events, 59.8 us)
Async XLA Ops:
  13.8 15.8 %collective-permute-start.2 = (bf16[1040,128]{1,0:T(8,128)(2,1)S(1)}, bf16[1040,128]{1,0:T(8,128)(2,1)S(1)}, u32[]{:S(2)}, u32[]{:S(2)}) collective-permute-start(bf16[1040,128]{1,0:T(8,128)(2,1)S(1)} %get-tuple-element.110), channel_id=1, source_target_pairs={{0,16},{1,49},{2,18},{3,51},{4,20},{5,53},{6,22},{7,55},{8,24},{9,... | collective-permute-start | bytes 798728 | tf_op jit(solution)/shard_map/ppermute | solution.py:115
  18.1 11.4 %collective-permute-start.1 = (bf16[1040,128]{1,0:T(8,128)(2,1)S(1)}, bf16[1040,128]{1,0:T(8,128)(2,1)S(1)}, u32[]{:S(2)}, u32[]{:S(2)}) collective-permute-start(bf16[1040,128]{1,0:T(8,128)(2,1)S(1)} %get-tuple-element.110), channel_id=1, source_target_pairs={{0,8},{1,57},{2,10},{3,59},{4,12},{5,61},{6,14},{7,63},{8,16},{9,1... | collective-permute-start | bytes 798728 | tf_op jit(solution)/shard_map/ppermute | solution.py:115
  24.4 16.2 %collective-permute-start.7 = (s32[128]{0:T(128)S(1)}, s32[128]{0:T(128)S(1)}, u32[]{:S(2)}, u32[]{:S(2)}) collective-permute-start(s32[128]{0:T(128)S(1)} %get-tuple-element.113), channel_id=1, source_target_pairs={{0,2},{1,65},{2,4},{3,67},{4,6},{5,69},{6,0},{7,71},{8,10},{9,73},... | collective-permute-start | bytes 1544 | tf_op jit(solution)/shard_map/ppermute | solution.py:115
  25.8 14.8 %collective-permute-start.8 = (s32[128]{0:T(128)S(1)}, s32[128]{0:T(128)S(1)}, u32[]{:S(2)}, u32[]{:S(2)}) collective-permute-start(s32[128]{0:T(128)S(1)} %get-tuple-element.114), channel_id=1, source_target_pairs={{0,4},{1,129},{2,6},{3,131},{4,0},{5,133},{6,2},{7,135},{8,12},{9,... | collective-permute-start | bytes 1544 | tf_op jit(solution)/shard_map/ppermute | solution.py:115
  28.4 12.2 %collective-permute-start.9 = (s32[128]{0:T(128)S(1)}, s32[128]{0:T(128)S(1)}, u32[]{:S(2)}, u32[]{:S(2)}) collective-permute-start(s32[128]{0:T(128)S(1)} %get-tuple-element.115), channel_id=1, source_target_pairs={{0,6},{1,193},{2,0},{3,195},{4,2},{5,197},{6,4},{7,199},{8,14},{9,... | collective-permute-start | bytes 1544 | tf_op jit(solution)/shard_map/ppermute | solution.py:115
  40.7 27.2 %collective-permute-start.12 = (bf16[4224,128]{1,0:T(8,128)(2,1)S(1)}, bf16[4224,128]{1,0:T(8,128)(2,1)S(1)}, u32[]{:S(2)}, u32[]{:S(2)}) collective-permute-start(bf16[4224,128]{1,0:T(8,128)(2,1)S(1)} %constant_dynamic-update-slice_fusion.a_ref), channel_id=1, source_target_pairs={{0,64},{1,3},{2,66},{3,5},{4,68},{5,7},{6,70},{7,1},{8,72},{9,11},... | collective-permute-start | bytes 3244040 | tf_op jit(solution)/shard_map/ppermute | solution.py:115
  41.7 26.2 %collective-permute-start.11 = (bf16[4224,128]{1,0:T(8,128)(2,1)S(1)}, bf16[4224,128]{1,0:T(8,128)(2,1)S(1)}, u32[]{:S(2)}, u32[]{:S(2)}) collective-permute-start(bf16[4224,128]{1,0:T(8,128)(2,1)S(1)} %constant_dynamic-update-slice_fusion.a_ref), channel_id=1, source_target_pairs={{0,128},{1,5},{2,130},{3,7},{4,132},{5,1},{6,134},{7,3},{8,136},{9... | collective-permute-start | bytes 3244040 | tf_op jit(solution)/shard_map/ppermute | solution.py:115
  42.8 25.8 %collective-permute-start.10 = (bf16[4224,128]{1,0:T(8,128)(2,1)S(1)}, bf16[4224,128]{1,0:T(8,128)(2,1)}, u32[]{:S(2)}, u32[]{:S(2)}) collective-permute-start(bf16[4224,128]{1,0:T(8,128)(2,1)S(1)} %constant_dynamic-update-slice_fusion.a_ref), channel_id=1, source_target_pairs={{0,192},{1,7},{2,194},{3,1},{4,196},{5,3},{6,198},{7,5},{8,200},{9... | collective-permute-start | bytes 3244040 | tf_op jit(solution)/shard_map/ppermute | solution.py:115
  44.2 36.2 %collective-permute-start.13 = (bf16[64,128,128]{2,1,0:T(8,128)(2,1)}, bf16[64,128,128]{2,1,0:T(8,128)(2,1)}, u32[]{:S(2)}, u32[]{:S(2)}) collective-permute-start(bf16[64,128,128]{2,1,0:T(8,128)(2,1)} %param.13), channel_id=1, source_target_pairs={{0,1},{1,0},{2,3},{3,2},{4,5},{5,4},{6,7},{7,6},{8,9},{9,8},{10,11... | collective-permute-start | bytes 6291464 | tf_op jit(solution)/shard_map/ppermute | solution.py:115
  73.9 23.0 %collective-permute-start.14 = (bf16[3584,128]{1,0:T(8,128)(2,1)S(1)}, bf16[3584,128]{1,0:T(8,128)(2,1)S(1)}, u32[]{:S(2)}, u32[]{:S(2)}) collective-permute-start(bf16[3584,128]{1,0:T(8,128)(2,1)S(1)} %get-tuple-element.120), channel_id=1, source_target_pairs={{0,6},{1,193},{2,0},{3,195},{4,2},{5,197},{6,4},{7,199},{8,14},{9,... | collective-permute-start | bytes 2752520 | tf_op jit(solution)/shard_map/ppermute | solution.py:115
  76.7 23.8 %collective-permute-start.15 = (bf16[3584,128]{1,0:T(8,128)(2,1)S(1)}, bf16[3584,128]{1,0:T(8,128)(2,1)S(1)}, u32[]{:S(2)}, u32[]{:S(2)}) collective-permute-start(bf16[3584,128]{1,0:T(8,128)(2,1)S(1)} %get-tuple-element.121), channel_id=1, source_target_pairs={{0,2},{1,65},{2,4},{3,67},{4,6},{5,69},{6,0},{7,71},{8,10},{9,73},... | collective-permute-start | bytes 2752520 | tf_op jit(solution)/shard_map/ppermute | solution.py:115
  77.0 25.7 %collective-permute-start.16 = (bf16[3584,128]{1,0:T(8,128)(2,1)S(1)}, bf16[3584,128]{1,0:T(8,128)(2,1)S(1)}, u32[]{:S(2)}, u32[]{:S(2)}) collective-permute-start(bf16[3584,128]{1,0:T(8,128)(2,1)S(1)} %get-tuple-element.122), channel_id=1, source_target_pairs={{0,4},{1,129},{2,6},{3,131},{4,0},{5,133},{6,2},{7,135},{8,12},{9,... | collective-permute-start | bytes 2752520 | tf_op jit(solution)/shard_map/ppermute | solution.py:115
  110.7 25.5 %collective-permute-start.19 = (bf16[3584,128]{1,0:T(8,128)(2,1)S(1)}, bf16[3584,128]{1,0:T(8,128)(2,1)S(1)}, u32[]{:S(2)}, u32[]{:S(2)}) collective-permute-start(bf16[3584,128]{1,0:T(8,128)(2,1)S(1)} %get-tuple-element.125), channel_id=1, source_target_pairs={{0,4},{1,129},{2,6},{3,131},{4,0},{5,133},{6,2},{7,135},{8,12},{9,... | collective-permute-start | bytes 2752520 | tf_op jit(solution)/shard_map/ppermute | solution.py:115
  116.1 20.1 %collective-permute-start.18 = (bf16[3584,128]{1,0:T(8,128)(2,1)S(1)}, bf16[3584,128]{1,0:T(8,128)(2,1)S(1)}, u32[]{:S(2)}, u32[]{:S(2)}) collective-permute-start(bf16[3584,128]{1,0:T(8,128)(2,1)S(1)} %get-tuple-element.124), channel_id=1, source_target_pairs={{0,2},{1,65},{2,4},{3,67},{4,6},{5,69},{6,0},{7,71},{8,10},{9,73},... | collective-permute-start | bytes 2752520 | tf_op jit(solution)/shard_map/ppermute | solution.py:115
  116.2 20.0 %collective-permute-start.20 = (bf16[3584,128]{1,0:T(8,128)(2,1)S(1)}, bf16[3584,128]{1,0:T(8,128)(2,1)S(1)}, u32[]{:S(2)}, u32[]{:S(2)}) collective-permute-start(bf16[3584,128]{1,0:T(8,128)(2,1)S(1)} %get-tuple-element.126), channel_id=1, source_target_pairs={{0,6},{1,193},{2,0},{3,195},{4,2},{5,197},{6,4},{7,199},{8,14},{9,... | collective-permute-start | bytes 2752520 | tf_op jit(solution)/shard_map/ppermute | solution.py:115
  127.9 8.3 %collective-permute-start.23 = (f32[144,128]{1,0:T(8,128)S(1)}, f32[144,128]{1,0:T(8,128)S(1)}, u32[]{:S(2)}, u32[]{:S(2)}) collective-permute-start(f32[144,128]{1,0:T(8,128)S(1)} %add.201), channel_id=1, source_target_pairs={{0,32},{1,33},{2,34},{3,35},{4,36},{5,37},{6,38},{7,39},{8,40},{9,... | collective-permute-start | bytes 221192 | tf_op jit(solution)/shard_map/ppermute | solution.py:115
  138.8 26.5 %collective-permute-start.24 = (bf16[4096,128]{1,0:T(8,128)(2,1)S(1)}, bf16[4096,128]{1,0:T(8,128)(2,1)S(1)}, u32[]{:S(2)}, u32[]{:S(2)}) collective-permute-start(bf16[4096,128]{1,0:T(8,128)(2,1)S(1)} %get-tuple-element.129), channel_id=1, source_target_pairs={{0,64},{1,3},{2,66},{3,5},{4,68},{5,7},{6,70},{7,1},{8,72},{9,11},... | collective-permute-start | bytes 3145736 | tf_op jit(solution)/shard_map/ppermute | solution.py:115
  140.3 25.0 %collective-permute-start.25 = (bf16[4096,128]{1,0:T(8,128)(2,1)S(1)}, bf16[4096,128]{1,0:T(8,128)(2,1)S(1)}, u32[]{:S(2)}, u32[]{:S(2)}) collective-permute-start(bf16[4096,128]{1,0:T(8,128)(2,1)S(1)} %get-tuple-element.130), channel_id=1, source_target_pairs={{0,128},{1,5},{2,130},{3,7},{4,132},{5,1},{6,134},{7,3},{8,136},{9... | collective-permute-start | bytes 3145736 | tf_op jit(solution)/shard_map/ppermute | solution.py:115
  141.0 24.9 %collective-permute-start.26 = (bf16[4096,128]{1,0:T(8,128)(2,1)S(1)}, bf16[4096,128]{1,0:T(8,128)(2,1)S(1)}, u32[]{:S(2)}, u32[]{:S(2)}) collective-permute-start(bf16[4096,128]{1,0:T(8,128)(2,1)S(1)} %get-tuple-element.131), channel_id=1, source_target_pairs={{0,192},{1,7},{2,194},{3,1},{4,196},{5,3},{6,198},{7,5},{8,200},{9... | collective-permute-start | bytes 3145736 | tf_op jit(solution)/shard_map/ppermute | solution.py:115
  166.5 30.0 %collective-permute-start.29 = (bf16[1536,128]{1,0:T(8,128)(2,1)S(1)}, bf16[1536,128]{1,0:T(8,128)(2,1)S(1)}, u32[]{:S(2)}, u32[]{:S(2)}) collective-permute-start(bf16[1536,128]{1,0:T(8,128)(2,1)S(1)} %get-tuple-element.134), channel_id=1, source_target_pairs={{0,1},{1,0},{2,3},{3,2},{4,5},{5,4},{6,7},{7,6},{8,9},{9,8},{10,11... | collective-permute-start | bytes 1179656 | tf_op jit(solution)/shard_map/ppermute | solution.py:115
  196.6 10.1 %collective-permute-start.30 = (bf16[1024,128]{1,0:T(8,128)(2,1)S(1)}, bf16[1024,128]{1,0:T(8,128)(2,1)S(1)}, u32[]{:S(2)}, u32[]{:S(2)}) collective-permute-start(bf16[1024,128]{1,0:T(8,128)(2,1)S(1)} %pad_maximum_fusion.1), channel_id=1, source_target_pairs={{0,56},{1,9},{2,58},{3,11},{4,60},{5,13},{6,62},{7,15},{8,0},{9,17... | collective-permute-start | bytes 786440 | tf_op jit(solution)/shard_map/ppermute | solution.py:115
  196.8 9.9 %collective-permute-start.31 = (bf16[512,128]{1,0:T(8,128)(2,1)S(1)}, bf16[512,128]{1,0:T(8,128)(2,1)S(1)}, u32[]{:S(2)}, u32[]{:S(2)}) collective-permute-start(bf16[512,128]{1,0:T(8,128)(2,1)S(1)} %get-tuple-element.135), channel_id=1, source_target_pairs={{0,48},{1,17},{2,50},{3,19},{4,52},{5,21},{6,54},{7,23},{8,56},{9,... | collective-permute-start | bytes 393224 | tf_op jit(solution)/shard_map/ppermute | solution.py:115
  200.3 11.4 %collective-permute-start.34 = (bf16[1024,128]{1,0:T(8,128)(2,1)S(1)}, bf16[1024,128]{1,0:T(8,128)(2,1)S(1)}, u32[]{:S(2)}, u32[]{:S(2)}) collective-permute-start(bf16[1024,128]{1,0:T(8,128)(2,1)S(1)} %pad_maximum_fusion.2), channel_id=1, source_target_pairs={{0,56},{1,9},{2,58},{3,11},{4,60},{5,13},{6,62},{7,15},{8,0},{9,17... | collective-permute-start | bytes 786440 | tf_op jit(solution)/shard_map/ppermute | solution.py:115
  206.7 9.9 %collective-permute-start.35 = (bf16[1024,128]{1,0:T(8,128)(2,1)S(1)}, bf16[1024,128]{1,0:T(8,128)(2,1)S(1)}, u32[]{:S(2)}, u32[]{:S(2)}) collective-permute-start(bf16[1024,128]{1,0:T(8,128)(2,1)S(1)} %get-tuple-element.139), channel_id=1, source_target_pairs={{0,48},{1,17},{2,50},{3,19},{4,52},{5,21},{6,54},{7,23},{8,56},{9,... | collective-permute-start | bytes 786440 | tf_op jit(solution)/shard_map/ppermute | solution.py:115
  (20 other events, 155.3 us)
